TPU v7x, 128 devices: a whole 4x4x4 slice. The times are simulated.
128 devices in a mesh: ep: 16 (over x, z), etp: 8 (over y, core).
Axes of the slice: x: 4, y: 4, z: 4, core: 2. Of those that a mesh axis runs over, the one named last changes fastest.
Arguments:
- tokens: bfloat16 [1024, 7168], P('ep', 'etp'), may hold values from -6 to 6
- cotangent: bfloat16 [1024, 7168], P('ep', 'etp'), may hold values from -6 to 6
- expert_ids: int32 [1024, 8], P('ep'), may hold values from 0 to 15, all different within a row; in each aligned block of 64 rows (0 to 63, 64 to 127, ...) at most 40 rows name the same one
- routing_gate_weight: bfloat16 [1024, 8], P('ep'), may hold values from 0.049804688 to 1
- gate_projection_weight: bfloat16 [16, 7168, 2048], P('ep', None, 'etp'), may hold values from -0.0625 to 0.0625
- up_weight: bfloat16 [16, 7168, 2048], P('ep', None, 'etp'), may hold values from -0.0625 to 0.0625
- down_weight: bfloat16 [16, 2048, 7168], P('ep', 'etp'), may hold values from -0.125 to 0.125
Outputs:
- input_grad: bfloat16 [1024, 7168], P('ep', 'etp')
- gate_grad: float32 [1024, 8], P('ep')
- w_gate_grad: bfloat16 [16, 7168, 2048], P('ep', None, 'etp')
- w_up_grad: bfloat16 [16, 7168, 2048], P('ep', None, 'etp')
- w_down_grad: bfloat16 [16, 2048, 7168], P('ep', 'etp')
Inputs may be any that keep to these rules, and one draw needn't show every extreme that they name: `expert_ids`: each row names 8 different experts. Among the rows of one index of ep no expert is named more than 40 times, a bound that some block reaches.
All inputs are finite; a program needn't handle non-finite values.
Results may differ from a plain program's by a relative error of at most 0.019.
Values may be sent and summed in bfloat16 or wider, within the bound.
No kernel may reach another device: no remote copies, remote signals or barrier semaphores. Data moves between devices by JAX's collectives and lax.ppermute only.
A program may use at most 192 MiB of HBM per device.

v0:
```python
import jax
import jax.numpy as jnp
from jax import lax
from jax.sharding import PartitionSpec as P


def local(
    tokens,
    cotangent,
    expert_ids,
    routing_gate_weight,
    gate_projection_weight,
    up_weight,
    down_weight,
):
    ep_count = lax.axis_size("ep")
    tok_rows = tokens.shape[0]
    choose = expert_ids.shape[1]
    capacity = min(tok_rows, tok_rows * choose * 5 // (4 * ep_count))
    width = down_weight.shape[2]
    flat_ids = expert_ids.reshape(-1)
    onehot = (flat_ids[:, None] == jnp.arange(ep_count, dtype=jnp.int32)[None, :]).astype(jnp.int32)
    before = jnp.cumsum(onehot, axis=0) - onehot
    rank = jnp.sum(before * onehot, axis=1)
    target_slot = flat_ids * capacity + rank
    source = jnp.repeat(jnp.arange(tok_rows, dtype=jnp.int32), choose)
    slot_positions = ep_count * capacity
    slice_cols = tokens.shape[1]
    send_x = (
        jnp.zeros((slot_positions, slice_cols), jnp.bfloat16)
        .at[target_slot]
        .set(tokens[source])
        .reshape(ep_count, capacity, slice_cols)
    )
    send_dy = (
        jnp.zeros((slot_positions, slice_cols), jnp.bfloat16)
        .at[target_slot]
        .set(cotangent[source])
        .reshape(ep_count, capacity, slice_cols)
    )
    send_g = (
        jnp.zeros((slot_positions,), jnp.bfloat16)
        .at[target_slot]
        .set(routing_gate_weight.reshape(-1))
        .reshape(ep_count, capacity)
    )
    recv_x, recv_dy, recv_g = (
        lax.all_to_all(send_x, "ep", split_axis=0, concat_axis=0, tiled=True),
        lax.all_to_all(send_dy, "ep", split_axis=0, concat_axis=0, tiled=True),
        lax.all_to_all(send_g, "ep", split_axis=0, concat_axis=0, tiled=True),
    )
    full_x, full_dy = (
        lax.all_gather(recv_x, "etp", axis=2, tiled=True),
        lax.all_gather(recv_dy, "etp", axis=2, tiled=True),
    )
    xe = full_x.reshape(slot_positions, width)
    dye = full_dy.reshape(slot_positions, width)
    wg = gate_projection_weight[0]
    wu = up_weight[0]
    wd = down_weight[0]
    a = jnp.dot(xe, wg, preferred_element_type=jnp.float32)
    b = jnp.dot(xe, wu, preferred_element_type=jnp.float32)
    sig = jax.nn.sigmoid(a)
    s = a * sig
    h = s * b
    gf = recv_g.reshape(slot_positions).astype(jnp.float32)[:, None]
    hs = (gf * h).astype(jnp.bfloat16)
    down_weight_gradient = jnp.dot(hs.T, dye, preferred_element_type=jnp.float32).astype(
        jnp.bfloat16
    )
    raw = jnp.dot(dye, wd.T, preferred_element_type=jnp.float32)
    gate_local = jnp.sum(h * raw, axis=1)
    dh = gf * raw
    da = (dh * b * sig * (1.0 + a * (1.0 - sig))).astype(jnp.bfloat16)
    db = (dh * s).astype(jnp.bfloat16)
    gate_weight_gradient = jnp.dot(xe.T, da, preferred_element_type=jnp.float32).astype(
        jnp.bfloat16
    )
    up_weight_gradient = jnp.dot(xe.T, db, preferred_element_type=jnp.float32).astype(jnp.bfloat16)
    partial_value = jnp.dot(da, wg.T, preferred_element_type=jnp.float32) + jnp.dot(
        db, wu.T, preferred_element_type=jnp.float32
    )
    rounded = partial_value.astype(jnp.bfloat16)
    slotted_gate = lax.psum(gate_local, "etp").reshape(ep_count, capacity)
    terms = lax.optimization_barrier(rounded).astype(jnp.float32).reshape(ep_count, capacity, width)
    share = lax.psum_scatter(
        terms.astype(jnp.bfloat16), "etp", scatter_dimension=2, tiled=True
    ).astype(jnp.float32)
    back, gate_back = (
        lax.all_to_all(share, "ep", split_axis=0, concat_axis=0, tiled=True),
        lax.all_to_all(slotted_gate, "ep", split_axis=0, concat_axis=0, tiled=True),
    )
    picked = back.reshape(slot_positions, slice_cols)[target_slot].reshape(
        tok_rows, choose, slice_cols
    )
    input_grad = jnp.sum(picked, axis=1).astype(jnp.bfloat16)
    gate_grad = gate_back.reshape(slot_positions)[target_slot].reshape(tok_rows, choose)
    return (
        input_grad,
        gate_grad,
        gate_weight_gradient[None],
        up_weight_gradient[None],
        down_weight_gradient[None],
    )


def solution(mesh):
    in_specs = (
        P("ep", "etp"),
        P("ep", "etp"),
        P("ep", None),
        P("ep", None),
        P("ep", None, "etp"),
        P("ep", None, "etp"),
        P("ep", "etp", None),
    )
    out_specs = (
        P("ep", "etp"),
        P("ep", None),
        P("ep", None, "etp"),
        P("ep", None, "etp"),
        P("ep", "etp", None),
    )
    return jax.shard_map(local, mesh=mesh, in_specs=in_specs, out_specs=out_specs, check_vma=False)
```

profile of v0, /device:TPU:0, one launch (start us, length us, event | category | flops | bytes accessed | tf_op | source)
XLA Modules:
  0.0 372.8 jit_solution(18059893435496112565)
XLA Ops:
  7.2 0.7 broadcast_multiply_fusion
  7.9 0.8 copy.19
  9.1 1.2 reduce-window.6
  10.7 6.1 %scatter_custom_fusion.2 = bf16[640,896]{1,0:T(8,128)(2,1)S(1)} fusion(s32[512]{0:T(512)S(1)} %bitcast.72, bf16[64,896]{1,0:T(8,128)(2,1)S(1)} %copy-done, s32[1024]{0:T(1024)S(1)} %pad_clamp_fusion.1, bf16[]{:T(256)} %constant.7.clone.1), kind=kCustom, calls=%fused_computation.24 | custom fusion | bytes 1146882 | tf_op jit(solution)/shard_map/scatter | solution.py:32
  16.8 26.1 %all_to_all.34 = bf16[16,40,896]{2,1,0:T(8,128)(2,1)} all-to-all(bf16[16,40,896]{2,1,0:T(8,128)(2,1)S(1)} %bitcast.71), channel_id=1, replica_groups=mesh['ep'=16,'etp'=8] {'ep'}, dimensions={0} | all-to-all | bytes 2293760 | tf_op jit(solution)/shard_map/all_to_all | solution.py:48
  43.1 7.4 %scatter_custom_fusion.1 = bf16[640,896]{1,0:T(8,128)(2,1)S(1)} fusion(s32[512]{0:T(512)S(1)} %bitcast.73, bf16[64,896]{1,0:T(8,128)(2,1)} %param.8, s32[1024]{0:T(1024)S(1)} %pad_clamp_fusion.1, bf16[]{:T(256)} %constant.7.clone.1), kind=kCustom, calls=%fused_computation.26 | custom fusion | bytes 1147392 | tf_op jit(solution)/shard_map/scatter | solution.py:38
  50.5 20.4 %all_to_all.35 = bf16[16,40,896]{2,1,0:T(8,128)(2,1)} all-to-all(bf16[16,40,896]{2,1,0:T(8,128)(2,1)S(1)} %bitcast.70), channel_id=1, replica_groups=mesh['ep'=16,'etp'=8] {'ep'}, dimensions={0} | all-to-all | bytes 2293760 | tf_op jit(solution)/shard_map/all_to_all | solution.py:49
  71.2 3.8 %scatter_custom_fusion = bf16[640]{0:T(1024)(128)(2,1)S(1)} fusion(s32[512]{0:T(512)S(1)} %bitcast.74, bf16[512]{0:T(512)(128)(2,1)S(1)} %reshape.184, bf16[]{:T(256)} %constant.7.clone.1), kind=kCustom, calls=%fused_computation.53 | custom fusion | bytes 1282 | tf_op jit(solution)/shard_map/scatter | solution.py:44
  75.1 10.9 %all_to_all.36 = bf16[16,1,40]{2,1,0:T(2,128)(2,1)S(1)} all-to-all(bf16[16,1,40]{2,1,0:T(2,128)(2,1)S(1)} %all_to_all.28), channel_id=1, replica_groups=mesh['ep'=16,'etp'=8] {'ep'}, dimensions={0} | all-to-all | bytes 2560 | tf_op jit(solution)/shard_map/all_to_all | solution.py:50
  86.1 8.0 %all-gather.5.cloned.1.call-done = bf16[16,40,7168]{2,1,0:T(8,128)(2,1)} async-done(((bf16[16,40,896]{2,1,0:T(8,128)(2,1)}), bf16[16,40,7168]{2,1,0:T(8,128)(2,1)}) %all-gather.5.cloned.1.call-update) | async-done | bytes 9175056 | tf_op jit(solution)/shard_map/all_gather | solution.py:53
  94.1 7.8 %fusion.5 = f32[640,256]{0,1:T(8,128)S(1)} fusion(bf16[640,7168]{1,0:T(8,128)(2,1)} %bitcast.78, bf16[1,7168,256]{2,1,0:T(8,128)(2,1)} %param.11), kind=kOutput, calls=%fused_computation.16 | convolution fusion | flops 2348810240 | bytes 13500416 | tf_op jit(solution)/shard_map/dot_general | solution.py:61
  102.5 3.3 fusion.8
  105.8 43.2 %all-gather.3.cloned.1.call-done = bf16[16,40,7168]{2,1,0:T(8,128)(2,1)} async-done(((bf16[16,40,896]{2,1,0:T(8,128)(2,1)}), bf16[16,40,7168]{2,1,0:T(8,128)(2,1)}) %all-gather.3.cloned.1.call-update) | async-done | bytes 9175056 | tf_op jit(solution)/shard_map/all_gather | solution.py:54
  149.1 8.0 %multiply_reduce_fusion = (f32[640]{0:T(1024)S(1)}, bf16[640,256]{0,1:T(8,128)(2,1)S(1)}, bf16[640,256]{0,1:T(8,128)(2,1)S(1)}) fusion(f32[640,256]{0,1:T(8,128)S(1)} %fusion.8, f32[640,256]{0,1:T(8,128)S(1)} %fusion.5, f32[640]{0:T(1024)S(1)} %reshape.147, bf16[640,7168]{1,0:T(8,128)(2,1)} %bitcast.84, bf16[1,256,7168]{2,1,0:T(8,128)(2,1)} %param.13), kind=kOutput, calls=%fused_computation.29 | convolution fusion | flops 2351595008 | bytes 14816256 | tf_op jit(solution)/shard_map/dot_general | solution.py:71
  157.1 9.3 %fusion.3 = f32[640,7168]{1,0:T(8,128)} fusion(bf16[640,256]{0,1:T(8,128)(2,1)S(1)} %get-tuple-element.16, bf16[1,7168,256]{2,1,0:T(8,128)(2,1)S(1)} %copy-done.3), kind=kOutput, calls=%fused_computation.14 | convolution fusion | flops 2348810240 | bytes 22347776 | tf_op jit(solution)/shard_map/dot_general | solution.py:80
  166.4 13.4 %add_convert_fusion = bf16[640,7168]{1,0:T(8,128)(2,1)} fusion(f32[640,7168]{1,0:T(8,128)} %fusion.3, bf16[640,256]{0,1:T(8,128)(2,1)S(1)} %get-tuple-element.17, bf16[1,7168,256]{2,1,0:T(8,128)(2,1)} %param.12), kind=kOutput, calls=%fused_computation.7 | convolution fusion | flops 2357985280 | bytes 31522816 | tf_op jit(solution)/shard_map/dot_general | solution.py:80
  179.8 31.5 %copy.25 = bf16[16,40,7168]{1,0,2:T(8,128)(2,1)} copy(bf16[16,40,7168]{2,1,0:T(8,128)(2,1)} %bitcast.68) | data formatting | bytes 18350080
  211.3 40.7 %reshape.204 = bf16[7168,640]{1,0:T(8,128)(2,1)} reshape(bf16[7168,16,40]{2,1,0:T(8,128)(2,1)} %bitcast.67) | data formatting | bytes 18350080
  252.1 13.9 %psum.7 = f32[16,1,40]{2,1,0:T(1,128)} all-reduce(f32[16,1,40]{2,1,0:T(1,128)S(1)} %all_to_all.26), channel_id=1, replica_groups=mesh['ep'=16,'etp'=8] {'etp'}, use_global_device_ids=true, to_apply=%region_9.10 | all-reduce | flops 640 | bytes 5120 | tf_op jit(solution)/shard_map/psum | solution.py:84
  266.1 7.1 %all-to-all-start.4 = ((f32[16,1,40]{2,1,0:T(1,128)}), f32[16,1,40]{2,1,0:T(1,128)S(1)}, u32[]{:S(2)}, u32[]{:S(2)}) async-start(f32[16,1,40]{2,1,0:T(1,128)} %psum.7), calls=%async_computation.4 | async-start | bytes 16384 | tf_op jit(solution)/shard_map/all_to_all | solution.py:91
  273.2 35.5 %reduce-scatter.4.cloned.1.call-done = bf16[896,640]{1,0:T(8,128)(2,1)} async-done(((bf16[7168,640]{1,0:T(8,128)(2,1)}), bf16[896,640]{1,0:T(8,128)(2,1)}) %reduce-scatter.4.cloned.1.call-update) | async-done | bytes 1146896
  308.7 7.4 %reshape.205 = bf16[896,16,40]{2,1,0:T(8,128)(2,1)} reshape(bf16[896,640]{1,0:T(8,128)(2,1)} %reduce-scatter.4.cloned.1.call-done) | data formatting | bytes 2293760
  316.1 4.5 %copy.26 = bf16[16,40,896]{2,1,0:T(8,128)(2,1)S(1)} copy(bf16[16,40,896]{1,0,2:T(8,128)(2,1)} %bitcast.69) | data formatting | bytes 2293760
  320.6 1.6 convert_element_type.57
  322.1 7.1 %all-to-all-start.3 = ((f32[16,40,896]{2,1,0:T(8,128)}), f32[16,40,896]{2,1,0:T(8,128)S(1)}, u32[]{:S(2)}, u32[]{:S(2)}) async-start(f32[16,40,896]{2,1,0:T(8,128)} %convert_element_type.57), calls=%async_computation.3 | async-start | bytes 4587520 | tf_op jit(solution)/shard_map/all_to_all | solution.py:90
  329.3 9.0 %fusion.2 = bf16[1,256,7168]{2,1,0:T(8,128)(2,1)} fusion(bf16[640,7168]{1,0:T(8,128)(2,1)} %bitcast.85, f32[640]{0:T(1024)S(1)} %reshape.147, f32[640,256]{0,1:T(8,128)} %copy-done.7, f32[640,256]{0,1:T(8,128)} %copy-done.6), kind=kOutput, calls=%fused_computation.13 | convolution fusion | flops 2351792128 | bytes 14158336 | tf_op jit(solution)/shard_map/dot_general | solution.py:68
  338.3 8.7 %fusion = bf16[1,7168,256]{2,1,0:T(8,128)(2,1)} fusion(bf16[640,7168]{1,0:T(8,128)(2,1)} %bitcast.79, bf16[640,256]{0,1:T(8,128)(2,1)S(1)} %get-tuple-element.16), kind=kOutput, calls=%fused_computation.11 | convolution fusion | flops 2350645248 | bytes 13172736 | tf_op jit(solution)/shard_map/dot_general | solution.py:76
  347.0 4.6 %fusion.1 = bf16[1,7168,256]{2,1,0:T(8,128)(2,1)} fusion(bf16[640,7168]{1,0:T(8,128)(2,1)S(1)} %bitcast.83, bf16[640,256]{0,1:T(8,128)(2,1)S(1)} %get-tuple-element.17), kind=kOutput, calls=%fused_computation.12 | convolution fusion | flops 2350645248 | bytes 13172736 | tf_op jit(solution)/shard_map/dot_general | solution.py:79
  352.9 2.3 gather_fusion.1
  356.0 4.8 %all-to-all-done.3 = f32[16,40,896]{2,1,0:T(8,128)S(1)} async-done(((f32[16,40,896]{2,1,0:T(8,128)}), f32[16,40,896]{2,1,0:T(8,128)S(1)}, u32[]{:S(2)}, u32[]{:S(2)}) %all-to-all-start.3) | async-done | bytes 2293792 | tf_op jit(solution)/shard_map/all_to_all | solution.py:90
  360.8 2.7 gather_fusion
  363.5 2.6 bitcast_reduce_fusion
  (56 shorter events, 4.3 us)
Async XLA Ops:
  7.2 3.5 copy-start
  7.2 86.9 %all-gather.5.cloned.1.call-start = ((), (), s32[]{:S(2)}) async-start(), calls=%async_computation.7 | async-start | bytes 10321920 | tf_op jit(solution)/shard_map/all_gather | solution.py:53
  16.8 54.2 %copy-start.4 = (bf16[64,8]{0,1:T(8,128)(2,1)S(1)}, bf16[64,8]{0,1:T(8,128)(2,1)}, u32[]{:S(2)}) copy-start(bf16[64,8]{0,1:T(8,128)(2,1)} %param.10) | copy-start | bytes 3076
  42.9 106.1 %all-gather.3.cloned.1.call-start = ((), (), s32[]{:S(2)}) async-start(), calls=%async_computation.6 | async-start | bytes 10321920 | tf_op jit(solution)/shard_map/all_gather | solution.py:54
  70.9 237.7 %reduce-scatter.4.cloned.1.call-start = ((), (), s32[]{:S(2)}) async-start(), calls=%async_computation.8 | async-start | bytes 10321920
  94.1 7.8 %copy-start.2 = (bf16[1,7168,256]{2,1,0:T(8,128)(2,1)S(1)}, bf16[1,7168,256]{2,1,0:T(8,128)(2,1)}, u32[]{:S(2)}) copy-start(bf16[1,7168,256]{2,1,0:T(8,128)(2,1)} %param.12) | copy-start | bytes 11010052
  94.1 8.4 %copy-start.5 = (bf16[16,40,7168]{2,1,0:T(8,128)(2,1)S(1)}, bf16[16,40,7168]{2,1,0:T(8,128)(2,1)}, u32[]{:S(2)}) copy-start(bf16[16,40,7168]{2,1,0:T(8,128)(2,1)} %all-gather.5.cloned.1.call-done) | copy-start | bytes 27525124
  102.5 46.6 %copy-start.6 = (f32[640,256]{0,1:T(8,128)}, f32[640,256]{0,1:T(8,128)S(1)}, u32[]{:S(2)}) copy-start(f32[640,256]{0,1:T(8,128)S(1)} %fusion.5) | copy-start | bytes 1966084
  105.8 51.3 %copy-start.7 = (f32[640,256]{0,1:T(8,128)}, f32[640,256]{0,1:T(8,128)S(1)}, u32[]{:S(2)}) copy-start(f32[640,256]{0,1:T(8,128)S(1)} %fusion.8) | copy-start | bytes 1966084
  149.0 8.1 %copy-start.3 = (bf16[1,7168,256]{2,1,0:T(8,128)(2,1)S(1)}, bf16[1,7168,256]{2,1,0:T(8,128)(2,1)}, u32[]{:S(2)}) copy-start(bf16[1,7168,256]{2,1,0:T(8,128)(2,1)} %param.11) | copy-start | bytes 11010052
  266.1 56.1 %all-to-all-start.4 = ((f32[16,1,40]{2,1,0:T(1,128)}), f32[16,1,40]{2,1,0:T(1,128)S(1)}, u32[]{:S(2)}, u32[]{:S(2)}) async-start(f32[16,1,40]{2,1,0:T(1,128)} %psum.7), calls=%async_computation.4 | async-start | bytes 16384 | tf_op jit(solution)/shard_map/all_to_all | solution.py:91
  322.1 38.6 %all-to-all-start.3 = ((f32[16,40,896]{2,1,0:T(8,128)}), f32[16,40,896]{2,1,0:T(8,128)S(1)}, u32[]{:S(2)}, u32[]{:S(2)}) async-start(f32[16,40,896]{2,1,0:T(8,128)} %convert_element_type.57), calls=%async_computation.3 | async-start | bytes 4587520 | tf_op jit(solution)/shard_map/all_to_all | solution.py:90
  329.3 17.7 %slice-start = ((s8[9175040]{0:T(1024)(128)(4,1)}), s8[786432]{0:T(1024)(128)(4,1)S(1)}, s32[]{:S(2)}) async-start(s8[9175040]{0:T(1024)(128)(4,1)} %bitcast.81), calls=%async_computation.9 | async-start | bytes 1572864
  329.3 17.7 %slice-start.1 = ((s8[9175040]{0:T(1024)(128)(4,1)}), s8[4194304]{0:T(1024)(128)(4,1)S(1)}, s32[]{:S(2)}) async-start(s8[9175040]{0:T(1024)(128)(4,1)} %bitcast.81), calls=%async_computation.10 | async-start | bytes 8388608
  338.3 8.7 %slice-start.2 = ((s8[9175040]{0:T(1024)(128)(4,1)}), s8[4194304]{0:T(1024)(128)(4,1)S(1)}, s32[]{:S(2)}) async-start(s8[9175040]{0:T(1024)(128)(4,1)} %bitcast.81), calls=%async_computation.11 | async-start | bytes 8388608
  360.8 5.3 %copy-start.1 = (bf16[64,896]{1,0:T(8,128)(2,1)S(1)}, bf16[64,896]{1,0:T(8,128)(2,1)}, u32[]{:S(2)}) copy-start(bf16[64,896]{1,0:T(8,128)(2,1)} %param.7) | copy-start | bytes 344068
Sparse Core Ops, SparseCore 0:
  43.0 51.0 all-gather.4
  95.8 53.1 all-gather.2
  252.1 56.4 reduce-scatter.3
where the time goes:
time: 380 us; the launch traced here: 373 us
  local copies, waits for them, and re-layouts  110 us (29%)
  waiting for transfers between devices  91.5 us (24%)
  blocking collectives  71.3 us (19%)
  matrix products  64.3 us (17%)
  starting transfers between devices  14.5 us (4%)
  between operations  14.2 us (4%)
  other arithmetic  6.86 us (2%)
    unnamed x29, local copies, waits for them, and re-layouts  86.2 us
    all_gather x1, waiting for transfers between devices, local(): lax.all_gather(recv_dy, 'etp', axis=2, tiled=True)  43.2 us
    unnamed x4, waiting for transfers between devices  35.5 us
    all_to_all x1, blocking collectives, local(): lax.all_to_all(send_x, 'ep', split_axis=0, concat_axis=0, tiled=True)  26.1 us
    all_to_all x1, blocking collectives, local(): lax.all_to_all(send_dy, 'ep', split_axis=0, concat_axis=0, tiled=True)  20.4 us
    psum x1, blocking collectives, local(): slotted_gate = lax.psum(gate_local, 'etp').reshape(ep_count, capacity)  13.9 us
    dot_general x1, matrix products, local(): jnp.dot(db, wu.T, preferred_element_type=jnp.float32)  13.4 us
    all_to_all x1, blocking collectives, local(): lax.all_to_all(send_g, 'ep', split_axis=0, concat_axis=0, tiled=True)  10.9 us
  transfers between devices with their start and end apart: 5, of which 4 were waited for; matrix products, arithmetic and copies ran while one was open for 17% of the time, Pallas kernels for 0%

commit v1 on v0

--- a/solution.py
+++ b/solution.py
@@ -1,7 +1,33 @@
 import jax
 import jax.numpy as jnp
 from jax import lax
+from jax.experimental import pallas as pl
+from jax.experimental.pallas import tpu as pltpu
 from jax.sharding import PartitionSpec as P
+
+
+def nt_dot(left, right):
+    return lax.dot_general(left, right, (((1,), (1,)), ((), ())), preferred_element_type=jnp.float32)
+
+
+def input_part_kernel(da_ref, db_ref, wg_ref, wu_ref, out_ref):
+    part = nt_dot(da_ref[...], wg_ref[...]) + nt_dot(db_ref[...], wu_ref[...])
+    out_ref[0] = part.astype(jnp.bfloat16)
+
+
+def input_parts(da, db, wg, wu, slices):
+    rows, hidden = da.shape
+    cols = wg.shape[0] // slices
+    whole = pl.BlockSpec((rows, hidden), lambda j: (0, 0))
+    block = pl.BlockSpec((cols, hidden), lambda j: (j, 0))
+    return pl.pallas_call(
+        input_part_kernel,
+        grid=(slices,),
+        in_specs=[whole, whole, block, block],
+        out_specs=pl.BlockSpec((1, rows, cols), lambda j: (j, 0, 0)),
+        out_shape=jax.ShapeDtypeStruct((slices, rows, cols), jnp.bfloat16),
+        compiler_params=pltpu.CompilerParams(vmem_limit_bytes=40 * 2**20),
+    )(da, db, wg, wu)
 
 
 def local(
@@ -77,15 +103,11 @@
         jnp.bfloat16
     )
     up_weight_gradient = jnp.dot(xe.T, db, preferred_element_type=jnp.float32).astype(jnp.bfloat16)
-    partial_value = jnp.dot(da, wg.T, preferred_element_type=jnp.float32) + jnp.dot(
-        db, wu.T, preferred_element_type=jnp.float32
+    parts = input_parts(da, db, wg, wu, width // slice_cols)
+    slotted_gate = lax.psum(gate_local, "etp").reshape(ep_count, capacity)
+    share = lax.psum_scatter(parts, "etp", scatter_dimension=0, tiled=False).reshape(
+        ep_count, capacity, slice_cols
     )
-    rounded = partial_value.astype(jnp.bfloat16)
-    slotted_gate = lax.psum(gate_local, "etp").reshape(ep_count, capacity)
-    terms = lax.optimization_barrier(rounded).astype(jnp.float32).reshape(ep_count, capacity, width)
-    share = lax.psum_scatter(
-        terms.astype(jnp.bfloat16), "etp", scatter_dimension=2, tiled=True
-    ).astype(jnp.float32)
     back, gate_back = (
         lax.all_to_all(share, "ep", split_axis=0, concat_axis=0, tiled=True),
         lax.all_to_all(slotted_gate, "ep", split_axis=0, concat_axis=0, tiled=True),
@@ -93,7 +115,7 @@
     picked = back.reshape(slot_positions, slice_cols)[target_slot].reshape(
         tok_rows, choose, slice_cols
     )
-    input_grad = jnp.sum(picked, axis=1).astype(jnp.bfloat16)
+    input_grad = jnp.sum(picked.astype(jnp.float32), axis=1).astype(jnp.bfloat16)
     gate_grad = gate_back.reshape(slot_positions)[target_slot].reshape(tok_rows, choose)
     return (
         input_grad,

time: 380 us -> 258 us (0.68); the launches traced: 373 us -> 257 us
  local copies, waits for them, and re-layouts: 110 us -> 25.8 us
  matrix products: 64.3 us -> 43.3 us
  waiting for transfers between devices: 91.5 us -> 75.4 us
  Pallas kernels: 0 us -> 8.5 us
    unnamed x29 -> x15, local copies, waits for them, and re-layouts: 86.2 us -> 2.6 us
    unnamed x4 -> x3, waiting for transfers between devices: 35.5 us -> 0.05 us
    dot_general x2 -> x0, matrix products: 22.7 us -> none  [the longest x1 13.4 us: local(): jnp.dot(db, wu.T, preferred_element_type=jnp.float32)]
    reduce_scatter x0 -> x1, waiting for transfers between devices: none -> 18.2 us  [local(): lax.psum_scatter(parts, 'etp', scatter_dimension=0, tiled=False)]
    pallas_call x0 -> x1, Pallas kernels: none -> 8.5 us  [input_parts(): pl.pallas_call(input_part_kernel, grid=(slices,), in_specs=[whole, whole,...]
    dot_general x1, matrix products: 4.63 us -> 8.53 us  [local(): jnp.dot(xe.T, db, preferred_element_type=jnp.float32).astype(jnp.bfloat16)]
  transfers between devices with their start and end apart: 5 -> 5, of which waited for: 4 -> 4; matrix products, arithmetic and copies ran while one was open for 17% -> 20% of each run, Pallas kernels for 0% -> 0%
where the time goes in v1:
time: 258 us; the launch traced here: 257 us
  waiting for transfers between devices  75.4 us (29%)
  blocking collectives  71.3 us (28%)
  matrix products  43.3 us (17%)
  local copies, waits for them, and re-layouts  25.8 us (10%)
  starting transfers between devices  14.4 us (6%)
  between operations  14 us (5%)
  Pallas kernels  8.5 us (3%)
  other arithmetic  3.95 us (2%)
    all_gather x1, waiting for transfers between devices, local(): lax.all_gather(recv_dy, 'etp', axis=2, tiled=True)  44 us
    all_to_all x1, blocking collectives, local(): lax.all_to_all(send_x, 'ep', split_axis=0, concat_axis=0, tiled=True)  26.1 us
    all_to_all x1, blocking collectives, local(): lax.all_to_all(send_dy, 'ep', split_axis=0, concat_axis=0, tiled=True)  20.4 us
    reduce_scatter x1, waiting for transfers between devices, local(): lax.psum_scatter(parts, 'etp', scatter_dimension=0, tiled=False)  18.2 us
    psum x1, blocking collectives, local(): slotted_gate = lax.psum(gate_local, 'etp').reshape(ep_count, capacity)  13.9 us
    all_to_all x1, blocking collectives, local(): lax.all_to_all(send_g, 'ep', split_axis=0, concat_axis=0, tiled=True)  10.9 us
    dot_general x1, matrix products, local(): jnp.dot(xe.T, da, preferred_element_type=jnp.float32).astype(jnp.bfloat16)  8.73 us
    dot_general x1, matrix products, local(): jnp.dot(hs.T, dye, preferred_element_type=jnp.float32).astype(jnp.bfloat16)  8.57 us
  transfers between devices with their start and end apart: 5, of which 4 were waited for; matrix products, arithmetic and copies ran while one was open for 20% of the time, Pallas kernels for 0%

profile of v1, /device:TPU:0, one launch (start us, length us, event | category | flops | bytes accessed | tf_op | source)
XLA Modules:
  0.0 256.7 jit_solution(17000318685792096019)
XLA Ops:
  7.2 0.7 broadcast_multiply_fusion
  7.9 0.8 copy.33
  9.1 1.2 reduce-window.6
  10.2 0.2 slice_reduce_fusion
  10.7 6.1 %scatter_custom_fusion.2 = bf16[640,896]{1,0:T(8,128)(2,1)S(1)} fusion(s32[512]{0:T(512)S(1)} %bitcast.66, bf16[64,896]{1,0:T(8,128)(2,1)S(1)} %copy-done, s32[1024]{0:T(1024)S(1)} %pad_clamp_fusion.1, bf16[]{:T(256)} %constant.7.clone.1), kind=kCustom, calls=%fused_computation.16 | custom fusion | bytes 1146882 | tf_op jit(solution)/shard_map/scatter | solution.py:58
  16.8 26.1 %all_to_all.34 = bf16[16,40,896]{2,1,0:T(8,128)(2,1)} all-to-all(bf16[16,40,896]{2,1,0:T(8,128)(2,1)S(1)} %bitcast.64), channel_id=1, replica_groups=mesh['ep'=16,'etp'=8] {'ep'}, dimensions={0} | all-to-all | bytes 2293760 | tf_op jit(solution)/shard_map/all_to_all | solution.py:74
  42.9 0.2 all-gather.3.cloned.1.call-start
  43.1 7.3 %scatter_custom_fusion.1 = bf16[640,896]{1,0:T(8,128)(2,1)S(1)} fusion(s32[512]{0:T(512)S(1)} %bitcast.67, bf16[64,896]{1,0:T(8,128)(2,1)} %param.8, s32[1024]{0:T(1024)S(1)} %pad_clamp_fusion.1, bf16[]{:T(256)} %constant.7.clone.1), kind=kCustom, calls=%fused_computation.18 | custom fusion | bytes 1147392 | tf_op jit(solution)/shard_map/scatter | solution.py:64
  50.5 20.4 %all_to_all.35 = bf16[16,40,896]{2,1,0:T(8,128)(2,1)} all-to-all(bf16[16,40,896]{2,1,0:T(8,128)(2,1)S(1)} %bitcast.63), channel_id=1, replica_groups=mesh['ep'=16,'etp'=8] {'ep'}, dimensions={0} | all-to-all | bytes 2293760 | tf_op jit(solution)/shard_map/all_to_all | solution.py:75
  71.2 3.8 %scatter_custom_fusion = bf16[640]{0:T(1024)(128)(2,1)S(1)} fusion(s32[512]{0:T(512)S(1)} %bitcast.68, bf16[512]{0:T(512)(128)(2,1)S(1)} %reshape.182, bf16[]{:T(256)} %constant.7.clone.1), kind=kCustom, calls=%fused_computation.45 | custom fusion | bytes 1282 | tf_op jit(solution)/shard_map/scatter | solution.py:70
  75.0 10.9 %all_to_all.36 = bf16[16,1,40]{2,1,0:T(2,128)(2,1)S(1)} all-to-all(bf16[16,1,40]{2,1,0:T(2,128)(2,1)S(1)} %all_to_all.28), channel_id=1, replica_groups=mesh['ep'=16,'etp'=8] {'ep'}, dimensions={0} | all-to-all | bytes 2560 | tf_op jit(solution)/shard_map/all_to_all | solution.py:76
  86.1 8.0 %all-gather.5.cloned.1.call-done = bf16[16,40,7168]{2,1,0:T(8,128)(2,1)} async-done(((bf16[16,40,896]{2,1,0:T(8,128)(2,1)}), bf16[16,40,7168]{2,1,0:T(8,128)(2,1)}) %all-gather.5.cloned.1.call-update) | async-done | bytes 9175056 | tf_op jit(solution)/shard_map/all_gather | solution.py:79
  94.1 7.3 %fusion.20 = f32[640,256]{1,0:T(8,128)S(1)} fusion(bf16[640,7168]{1,0:T(8,128)(2,1)} %bitcast.72, bf16[1,7168,256]{2,1,0:T(8,128)(2,1)} %param.11), kind=kOutput, calls=%fused_computation.47 | convolution fusion | flops 2348810240 | bytes 13500416 | tf_op jit(solution)/shard_map/dot_general | solution.py:87
  101.4 1.0 copy-done.5
  102.5 2.5 fusion.22
  105.0 44.0 %all-gather.3.cloned.1.call-done = bf16[16,40,7168]{2,1,0:T(8,128)(2,1)} async-done(((bf16[16,40,896]{2,1,0:T(8,128)(2,1)}), bf16[16,40,7168]{2,1,0:T(8,128)(2,1)}) %all-gather.3.cloned.1.call-update) | async-done | bytes 9175056 | tf_op jit(solution)/shard_map/all_gather | solution.py:80
  149.1 7.7 %multiply_reduce_fusion = (f32[640]{0:T(1024)S(1)}, bf16[640,256]{1,0:T(8,128)(2,1)S(1)}, bf16[640,256]{1,0:T(8,128)(2,1)S(1)}) fusion(f32[640,256]{1,0:T(8,128)S(1)} %fusion.22, f32[640,256]{1,0:T(8,128)S(1)} %fusion.20, f32[640]{0:T(1024)S(1)} %reshape.145, bf16[640,7168]{1,0:T(8,128)(2,1)} %bitcast.61, bf16[1,256,7168]{2,1,0:T(8,128)(2,1)} %param.13), kind=kOutput, calls=%fused_computation.21 | convolution fusion | flops 2351595008 | bytes 14816256 | tf_op jit(solution)/shard_map/dot_general | solution.py:97
  156.7 8.5 %shard_map.110 = bf16[8,640,896]{2,1,0:T(8,128)(2,1)} custom-call(bf16[640,256]{1,0:T(8,128)(2,1)S(1)} %get-tuple-element.16.da_ref, bf16[640,256]{1,0:T(8,128)(2,1)S(1)} %get-tuple-element.17.db_ref, bf16[7168,256]{1,0:T(8,128)(2,1)S(1)} %bitcast.59, bf16[7168,256]{1,0:T(8,128)(2,1)S(1)} %bitcast.58), custom_call_target="tpu_custom_call" | custom-call | tf_op jit(solution)/shard_map/pallas_call | solution.py:23
  165.4 13.9 %psum.7 = f32[16,1,40]{2,1,0:T(1,128)} all-reduce(f32[16,1,40]{2,1,0:T(1,128)S(1)} %all_to_all.26), channel_id=1, replica_groups=mesh['ep'=16,'etp'=8] {'etp'}, use_global_device_ids=true, to_apply=%region_9.10 | all-reduce | flops 640 | bytes 5120 | tf_op jit(solution)/shard_map/psum | solution.py:107
  179.3 7.1 %all-to-all-start.4 = ((f32[16,1,40]{2,1,0:T(1,128)}), f32[16,1,40]{2,1,0:T(1,128)S(1)}, u32[]{:S(2)}, u32[]{:S(2)}) async-start(f32[16,1,40]{2,1,0:T(1,128)} %psum.7), calls=%async_computation.5 | async-start | bytes 16384 | tf_op jit(solution)/shard_map/all_to_all | solution.py:113
  186.5 8.7 %fusion = bf16[1,7168,256]{2,1,0:T(8,128)(2,1)} fusion(bf16[640,7168]{1,0:T(8,128)(2,1)} %bitcast.73, bf16[640,256]{1,0:T(8,128)(2,1)S(1)} %get-tuple-element.16.da_ref), kind=kOutput, calls=%fused_computation.10 | convolution fusion | flops 2350645248 | bytes 13172736 | tf_op jit(solution)/shard_map/dot_general | solution.py:102
  195.2 8.6 %fusion.2 = bf16[1,256,7168]{2,1,0:T(8,128)(2,1)} fusion(bf16[640,7168]{1,0:T(8,128)(2,1)} %bitcast.62, f32[640]{0:T(1024)S(1)} %reshape.145, f32[640,256]{1,0:T(8,128)S(1)} %fusion.22, f32[640,256]{1,0:T(8,128)S(1)} %fusion.20), kind=kOutput, calls=%fused_computation.12 | convolution fusion | flops 2351792128 | bytes 14158336 | tf_op jit(solution)/shard_map/dot_general | solution.py:94
  203.8 18.2 %reduce-scatter.2.cloned.1.call-done = bf16[1,640,896]{2,1,0:T(8,128)(2,1)} async-done(((bf16[8,640,896]{2,1,0:T(8,128)(2,1)}), bf16[1,640,896]{2,1,0:T(8,128)(2,1)}) %reduce-scatter.2.cloned.1.call-update) | async-done | bytes 1146896 | tf_op jit(solution)/shard_map/reduce_scatter | solution.py:108
  221.9 6.9 %all-to-all-start.3 = ((bf16[16,40,896]{2,1,0:T(8,128)(2,1)}), bf16[16,40,896]{2,1,0:T(8,128)(2,1)S(1)}, u32[]{:S(2)}, u32[]{:S(2)}) async-start(bf16[16,40,896]{2,1,0:T(8,128)(2,1)} %bitcast.65), calls=%async_computation.4 | async-start | bytes 2293760 | tf_op jit(solution)/shard_map/all_to_all | solution.py:112
  228.9 8.5 %fusion.1 = bf16[1,7168,256]{2,1,0:T(8,128)(2,1)} fusion(bf16[640,7168]{1,0:T(8,128)(2,1)} %bitcast.74, bf16[640,256]{1,0:T(8,128)(2,1)S(1)} %get-tuple-element.17.db_ref), kind=kOutput, calls=%fused_computation.11 | convolution fusion | flops 2350645248 | bytes 13172736 | tf_op jit(solution)/shard_map/dot_general | solution.py:105
  237.4 0.5 broadcast.111
  237.9 0.7 reduce.10
  238.7 2.3 gather_fusion.1
  241.1 0.7 copy.45
  241.7 5.1 %all-to-all-done.3 = bf16[16,40,896]{2,1,0:T(8,128)(2,1)S(1)} async-done(((bf16[16,40,896]{2,1,0:T(8,128)(2,1)}), bf16[16,40,896]{2,1,0:T(8,128)(2,1)S(1)}, u32[]{:S(2)}, u32[]{:S(2)}) %all-to-all-start.3) | async-done | bytes 1146912 | tf_op jit(solution)/shard_map/all_to_all | solution.py:112
  246.8 2.0 gather_fusion
  248.9 1.3 bitcast_reduce_fusion
  (39 shorter events, 1.4 us)
Async XLA Ops:
  7.2 3.5 %copy-start = (bf16[64,896]{1,0:T(8,128)(2,1)S(1)}, bf16[64,896]{1,0:T(8,128)(2,1)}, u32[]{:S(2)}) copy-start(bf16[64,896]{1,0:T(8,128)(2,1)} %param.7) | copy-start | bytes 344068
  7.2 86.9 %all-gather.5.cloned.1.call-start = ((), (), s32[]{:S(2)}) async-start(), calls=%async_computation.7 | async-start | bytes 10321920 | tf_op jit(solution)/shard_map/all_gather | solution.py:79
  16.8 54.1 %copy-start.4 = (bf16[64,8]{0,1:T(8,128)(2,1)S(1)}, bf16[64,8]{0,1:T(8,128)(2,1)}, u32[]{:S(2)}) copy-start(bf16[64,8]{0,1:T(8,128)(2,1)} %param.10) | copy-start | bytes 3076
  42.9 106.1 %all-gather.3.cloned.1.call-start = ((), (), s32[]{:S(2)}) async-start(), calls=%async_computation.6 | async-start | bytes 10321920 | tf_op jit(solution)/shard_map/all_gather | solution.py:80
  70.9 151.0 %reduce-scatter.2.cloned.1.call-start = ((), (), s32[]{:S(2)}) async-start(), calls=%async_computation.8 | async-start | bytes 10321920 | tf_op jit(solution)/shard_map/reduce_scatter | solution.py:108
  94.1 7.3 %copy-start.1 = (bf16[1,7168,256]{2,1,0:T(8,128)(2,1)S(1)}, bf16[1,7168,256]{2,1,0:T(8,128)(2,1)}, u32[]{:S(2)}) copy-start(bf16[1,7168,256]{2,1,0:T(8,128)(2,1)} %param.12) | copy-start | bytes 11010052
  94.1 8.4 %copy-start.5 = (bf16[16,40,7168]{2,1,0:T(8,128)(2,1)S(1)}, bf16[16,40,7168]{2,1,0:T(8,128)(2,1)}, u32[]{:S(2)}) copy-start(bf16[16,40,7168]{2,1,0:T(8,128)(2,1)} %all-gather.5.cloned.1.call-done) | copy-start | bytes 27525124
  149.0 7.7 %copy-start.2 = (bf16[1,7168,256]{2,1,0:T(8,128)(2,1)S(1)}, bf16[1,7168,256]{2,1,0:T(8,128)(2,1)}, u32[]{:S(2)}) copy-start(bf16[1,7168,256]{2,1,0:T(8,128)(2,1)} %param.12) | copy-start | bytes 11010052
  149.0 7.7 %copy-start.3 = (bf16[1,7168,256]{2,1,0:T(8,128)(2,1)S(1)}, bf16[1,7168,256]{2,1,0:T(8,128)(2,1)}, u32[]{:S(2)}) copy-start(bf16[1,7168,256]{2,1,0:T(8,128)(2,1)} %param.11) | copy-start | bytes 11010052
  179.3 24.4 %all-to-all-start.4 = ((f32[16,1,40]{2,1,0:T(1,128)}), f32[16,1,40]{2,1,0:T(1,128)S(1)}, u32[]{:S(2)}, u32[]{:S(2)}) async-start(f32[16,1,40]{2,1,0:T(1,128)} %psum.7), calls=%async_computation.5 | async-start | bytes 16384 | tf_op jit(solution)/shard_map/all_to_all | solution.py:113
  221.9 24.9 %all-to-all-start.3 = ((bf16[16,40,896]{2,1,0:T(8,128)(2,1)}), bf16[16,40,896]{2,1,0:T(8,128)(2,1)S(1)}, u32[]{:S(2)}, u32[]{:S(2)}) async-start(bf16[16,40,896]{2,1,0:T(8,128)(2,1)} %bitcast.65), calls=%async_computation.4 | async-start | bytes 2293760 | tf_op jit(solution)/shard_map/all_to_all | solution.py:112
Sparse Core Ops, SparseCore 0:
  43.0 51.0 all-gather.4
  95.8 53.2 all-gather.2
  165.4 56.4 reduce-scatter.1

commit v2 on v0

v2 whole, which is shorter than its diff:
```python
import functools

import jax
import jax.numpy as jnp
from jax import lax
from jax.experimental import pallas as pl
from jax.experimental.pallas import tpu as pltpu
from jax.sharding import Mesh, PartitionSpec as P

BF, F32 = jnp.bfloat16, jnp.float32
ROWS, COLS, HID, PAD, ROOM, TAIL = 640, 896, 256, 128, 40, 16
SWAP = [(0, 1), (1, 0)]
ANY = pl.BlockSpec(memory_space=pl.ANY)
VMEM = pl.BlockSpec(memory_space=pltpu.VMEM)
SMEM = pl.BlockSpec(memory_space=pltpu.SMEM)
HBM = pl.BlockSpec(memory_space=pltpu.HBM)


def partner(i, core, step):
    return i ^ 1 if core == step else 3 - i


MEET = tuple(
    [(2 * i + c, 2 * partner(i, c, step) + c) for i in range(4) for c in range(2)] for step in range(2)
)


def meet(v, step):
    return lax.ppermute(v, ("y", "core"), MEET[step])


def swap(v):
    return lax.ppermute(v, "core", SWAP)


def nn(left, right):
    return jnp.dot(left, right, preferred_element_type=F32)


def nt(left, right):
    return lax.dot_general(left, right, (((1,), (1,)), ((), ())), preferred_element_type=F32)


def tn(left, right):
    return lax.dot_general(left, right, (((0,), (0,)), ((), ())), preferred_element_type=F32)


def sds(shape, dtype=BF):
    return jax.ShapeDtypeStruct(shape, dtype)


def call(kernel, ins, outs, scratch=(), us=1, mib=24):
    return pl.pallas_call(
        kernel,
        in_specs=ins,
        out_specs=[spec for spec, _ in outs],
        out_shape=[shape for _, shape in outs],
        scratch_shapes=scratch,
        compiler_params=pltpu.CompilerParams(vmem_limit_bytes=mib * 2**20),
        cost_estimate=pl.CostEstimate(flops=0, bytes_accessed=int(us * 3.6e6), transcendentals=0),
    )


def dispatch_kernel(ids, gates, x, dy, send_x, send_dy, onehot):
    expert = lax.broadcasted_iota(jnp.int32, (16, 64), 0)
    named = jnp.zeros((16, 64), F32)
    weight = jnp.zeros((16, 64), F32)
    for k in range(8):
        here = ids[k : k + 1, :] == expert
        named = named + jnp.where(here, 1.0, 0.0)
        weight = weight + jnp.where(here, gates[k : k + 1, :], 0.0)
    one, two = (lax.broadcasted_iota(jnp.int32, (64, 64), axis) for axis in range(2))
    rank = nn(named.astype(BF), jnp.where(one < two, 1.0, 0.0).astype(BF)).astype(jnp.int32)
    slot = lax.broadcasted_iota(jnp.int32, (ROOM, 64), 0)
    picks, sums = [], []
    for e in range(16):
        pick = jnp.where((rank[e : e + 1, :] == slot) & (named[e : e + 1, :] > 0.0), 1.0, 0.0)
        picks.append(pick)
        sums.append(jnp.sum(pick * weight[e : e + 1, :], axis=1, keepdims=True))
    pick = jnp.concatenate(picks, axis=0).astype(BF)
    onehot[...] = pick
    send_x[...] = nn(pick, x[...]).astype(BF)
    send_dy[:, :COLS] = nn(pick, dy[...]).astype(BF)
    send_dy[:, COLS:] = jnp.broadcast_to(jnp.concatenate(sums, axis=0), (ROWS, PAD)).astype(BF)


def dispatch(ids, gates, x, dy):
    outs = [(VMEM, sds((ROWS, COLS))), (VMEM, sds((ROWS, COLS + PAD))), (VMEM, sds((ROWS, 64)))]
    return call(dispatch_kernel, [VMEM] * 4, outs, us=4)(ids, gates, x, dy)


def combine_kernel(back, onehot, ids, *refs):
    grad, gate = refs[-2:]
    pick = onehot[...]
    grad[...] = tn(pick, back[:, :COLS]).astype(BF)
    sums = tn(pick, back[:, COLS:])
    lane = lax.broadcasted_iota(jnp.int32, (64, PAD), 1)
    total = jnp.zeros((64, PAD), F32)
    for k in range(8):
        mine = ids[:, k : k + 1]
        value = jnp.sum(jnp.where((lane == mine) | (lane == mine + 64), sums, 0.0), axis=1, keepdims=True)
        total = total + jnp.where(lane == k, value, 0.0)
    gate[...] = total[:, :8]


def combine(back, onehot, ids):
    outs = [(VMEM, sds((64, COLS))), (VMEM, sds((64, 8), F32))]
    return call(combine_kernel, [VMEM] * 3, outs, us=3)(back, onehot, ids)


def block(ref, i):
    return ref.at[pl.ds(pl.multiple_of(i * COLS, COLS), COLS), :]


def column_block(ref, i):
    return ref.at[:, pl.ds(pl.multiple_of(i * COLS, COLS), COLS)]


def hidden_steps(first, place, xs, wg, wu, x, g, u, a, b, sems):
    def copies(n, src):
        i = place[first + n]
        return [
            pltpu.make_async_copy(src, x.at[n], sems.at[0, n]),
            pltpu.make_async_copy(block(wg, i), g.at[n], sems.at[1, n]),
            pltpu.make_async_copy(block(wu, i), u.at[n], sems.at[2, n]),
        ]

    for n in range(len(xs)):
        for copy in copies(n, xs[n]):
            copy.start()

    @pl.loop(0, len(xs))
    def _(n):
        for copy in copies(n, xs[0]):
            copy.wait()
        a[...] += nn(x[n], g[n])
        b[...] += nn(x[n], u[n])


def first_hidden_kernel(n, place, *refs):
    xs, (wg, wu, a, b, x, g, u, sems) = refs[:n], refs[n:]
    a[...] = jnp.zeros_like(a)
    b[...] = jnp.zeros_like(b)
    hidden_steps(0, place, xs, wg, wu, x, g, u, a, b, sems)


def hidden_kernel(n, place, *refs):
    xs, (wg, wu, a0, b0, s_ref, slope_ref, h_ref, x, g, u, a, b, sems) = refs[:n], refs[n:]
    a[...] = a0[...]
    b[...] = b0[...]
    hidden_steps(8 - n, place, xs, wg, wu, x, g, u, a, b, sems)
    for lo in range(0, ROWS, 128):
        rows = pl.ds(lo, 128)
        av, bv = a[rows, :], b[rows, :]
        sig = jax.nn.sigmoid(av)
        s = av * sig
        s_ref[rows, :] = s
        h_ref[rows, :] = s * bv
        slope_ref[rows, :] = bv * sig * (1.0 + av * (1.0 - sig))


def hidden_scratch(n):
    return [pltpu.VMEM((n, ROWS, COLS), BF)] + [pltpu.VMEM((n, COLS, HID), BF)] * 2


def first_hidden(place, xs, wg, wu):
    n = len(xs)
    scratch = hidden_scratch(n) + [pltpu.SemaphoreType.DMA((3, n))]
    outs = [(VMEM, sds((ROWS, HID), F32))] * 2
    kernel = functools.partial(first_hidden_kernel, n)
    return call(kernel, [SMEM] + [HBM] * (n + 2), outs, scratch, us=9, mib=32)(place, *xs, wg, wu)


def hidden(place, xs, wg, wu, a, b):
    n = len(xs)
    scratch = hidden_scratch(n) + [pltpu.VMEM((ROWS, HID), F32)] * 2 + [pltpu.SemaphoreType.DMA((3, n))]
    outs = [(VMEM, sds((ROWS, HID), F32))] * 3
    ins = [SMEM] + [HBM] * (n + 2) + [VMEM] * 2
    return call(functools.partial(hidden_kernel, n), ins, outs, scratch, us=5)(place, *xs, wg, wu, a, b)


def after(v, *later):
    return pl.pallas_call(
        lambda *refs: None,
        in_specs=[HBM] + [ANY] * len(later),
        out_specs=HBM,
        out_shape=sds(v.shape, v.dtype),
        input_output_aliases={0: 0},
    )(v, *later)


def raw_steps(ks, place, dys, wd, dy, w, acc, sems):
    def copies(n, src):
        return [
            pltpu.make_async_copy(src, dy.at[n], sems.at[0, n]),
            pltpu.make_async_copy(column_block(wd, place[ks[0] + n]), w.at[n], sems.at[1, n]),
        ]

    for n in range(len(ks)):
        for copy in copies(n, dys[n]):
            copy.start()

    @pl.loop(0, len(ks))
    def _(n):
        for copy in copies(n, dys[0]):
            copy.wait()
        acc[...] += nt(dy[n], w[n])


def first_raw_kernel(ks, place, *refs):
    n = len(ks)
    dys, (wd, _, raw, dy, w, sems) = refs[:n], refs[n:]
    raw[...] = jnp.zeros_like(raw)
    raw_steps(ks, place, dys, wd, dy, w, raw, sems)


def raw_scratch(n):
    return [pltpu.VMEM((n, ROWS, COLS), BF), pltpu.VMEM((n, HID, COLS), BF), pltpu.SemaphoreType.DMA((2, n))]


def first_raw(ks, place, dys, wd, later):
    kernel = functools.partial(first_raw_kernel, ks)
    outs = [(VMEM, sds((ROWS, HID), F32))]
    return call(kernel, [SMEM] + [HBM] * (len(ks) + 1) + [ANY], outs, raw_scratch(len(ks)), us=5)(place, *dys, wd, later)[0]


def gradient_kernel(ks, place, *refs):
    n = len(ks)
    dys = refs[:n]
    wd, first, s_ref, slope_ref, h_ref, gate, dab, hs, sums, acc, dy, w, sems = refs[n:]
    acc[...] = first[...]
    raw_steps(ks, place, dys, wd, dy, w, acc, sems)
    sums[...] = jnp.zeros_like(sums)
    for i in range(ROWS // 128):
        rows = pl.ds(128 * i, 128)
        g, raw, h = gate[rows, 0:1].astype(F32), acc[rows, :], h_ref[rows, :]
        total = jnp.sum(h * raw, axis=1, keepdims=True)
        sums[0:1, pl.ds(128 * i, 128)] = jnp.broadcast_to(total, (128, 128)).T[0:1, :]
        dh = g * raw
        dab[rows, :HID] = (dh * slope_ref[rows, :]).astype(BF)
        dab[rows, HID:] = (dh * s_ref[rows, :]).astype(BF)
        hs[rows, :] = (g * h).astype(BF)


def gradients(ks, place, dys, wd, first, s, slope, h, gate):
    outs = [(VMEM, sds((ROWS, 2 * HID))), (VMEM, sds((ROWS, HID))), (VMEM, sds((TAIL, COLS), F32))]
    kernel = functools.partial(gradient_kernel, ks)
    scratch = [pltpu.VMEM((ROWS, HID), F32)] + raw_scratch(len(ks))
    ins = [SMEM] + [HBM] * (len(ks) + 1) + [VMEM] * 5
    return call(kernel, ins, outs, scratch, us=6)(place, *dys, wd, first, s, slope, h, gate)


def input_kernel(k, place, dab, sums, wg, wu, *refs):
    sib, own, g, u, sems = refs[-5:]

    def copies(j, i):
        return [
            pltpu.make_async_copy(block(wg, i), g.at[j], sems.at[0, j]),
            pltpu.make_async_copy(block(wu, i), u.at[j], sems.at[1, j]),
        ]

    for j, out in enumerate((sib, own)):
        for copy in copies(j, place[2 * k + 1 - j]):
            copy.start()
    for j, out in enumerate((sib, own)):
        for copy in copies(j, place[2 * k + 1 - j]):
            copy.wait()
        out[:ROWS, :] = (nt(dab[:, :HID], g[j]) + nt(dab[:, HID:], u[j])).astype(BF)
        out[ROWS:, :] = sums[...].astype(BF)


def input_part(k, place, dab, sums, wg, wu, *later):
    scratch = [pltpu.VMEM((2, COLS, HID), BF)] * 2 + [pltpu.SemaphoreType.DMA((2, 2))]
    outs = [(VMEM, sds((ROWS + TAIL, COLS)))] * 2
    ins = [SMEM, VMEM, VMEM, HBM, HBM] + [ANY] * len(later)
    return call(functools.partial(input_kernel, k), ins, outs, scratch, us=3.5)(place, dab, sums, wg, wu, *later)


def column_gradient_kernel(place, *refs):
    xs, (dab, g_out, u_out, x, g, u, sems) = refs[:8], refs[8:]

    def load(k, src):
        return pltpu.make_async_copy(src, x.at[k], sems.at[0, k])

    def stores(k):
        i = place[k]
        return [
            pltpu.make_async_copy(g.at[k], block(g_out, i), sems.at[1, k]),
            pltpu.make_async_copy(u.at[k], block(u_out, i), sems.at[2, k]),
        ]

    for k in range(8):
        load(k, xs[k]).start()

    @pl.loop(0, 8)
    def _(k):
        load(k, xs[0]).wait()
        value = tn(x[k], dab[...])
        g[k] = value[:, :HID].astype(BF)
        u[k] = value[:, HID:].astype(BF)
        for copy in stores(k):
            copy.start()

    @pl.loop(0, 8)
    def _(k):
        for copy in stores(k):
            copy.wait()


def column_gradients(place, xs, dab):
    scratch = [pltpu.VMEM((8, ROWS, COLS), BF)] + [pltpu.VMEM((8, COLS, HID), BF)] * 2
    scratch += [pltpu.SemaphoreType.DMA((3, 8))]
    outs = [(HBM, sds((8 * COLS, HID)))] * 2
    return call(column_gradient_kernel, [SMEM] + [HBM] * 8 + [VMEM], outs, scratch, us=10, mib=32)(place, *xs, dab)


def row_gradient_kernel(place, *refs):
    dys, (hs, out, dy, d, sems) = refs[:8], refs[8:]

    def load(k, src):
        return pltpu.make_async_copy(src, dy.at[k], sems.at[0, k])

    def store(k):
        return pltpu.make_async_copy(d.at[k], column_block(out, place[k]), sems.at[1, k])

    for k in range(8):
        load(k, dys[k]).start()
    hst = hs[...].T

    @pl.loop(0, 8)
    def _(k):
        load(k, dys[0]).wait()
        d[k] = nn(hst, dy[k]).astype(BF)
        store(k).start()

    @pl.loop(0, 8)
    def _(k):
        store(k).wait()


def row_gradient(place, dys, hs):
    scratch = [pltpu.VMEM((8, ROWS, COLS), BF), pltpu.VMEM((8, HID, COLS), BF), pltpu.SemaphoreType.DMA((2, 8))]
    outs = [(HBM, sds((HID, 8 * COLS)))]
    return call(row_gradient_kernel, [SMEM] + [HBM] * 8 + [VMEM], outs, scratch, us=6, mib=24)(place, *dys, hs)[0]


def total_kernel(expert, *refs):
    terms, out = refs[:4], refs[-1]
    lane = lax.broadcasted_iota(jnp.int32, (128, PAD), 1)
    gates = sum(term[ROWS:, :].astype(F32) for term in terms)
    for i in range(ROWS // 128):
        rows = pl.ds(128 * i, 128)
        out[rows, :COLS] = sum(term[rows, :].astype(F32) for term in terms).astype(BF)
        gate = jnp.broadcast_to(gates[0:1, 128 * i : 128 * i + 128], (128, 128)).T
        high = gate.astype(BF).astype(F32)
        spread = jnp.where(lane == expert[0], high, 0.0) + jnp.where(lane == expert[0] + 64, gate - high, 0.0)
        out[rows, COLS:] = spread.astype(BF)


def total(expert, terms, *later):
    outs = [(VMEM, sds((ROWS, COLS + PAD)))]
    ins = [SMEM] + [VMEM] * 4 + [ANY] * len(later)
    return call(total_kernel, ins, outs, us=2)(expert, *terms, *later)[0]


def exchange(v):
    return lax.all_to_all(v.reshape(16, ROOM, -1), ("x", "z"), 0, 0, tiled=True).reshape(ROWS, -1)


def ring(v):
    return [v, meet(v, 0), meet(v, 1)]


def with_swaps(pieces):
    return [v for piece in pieces for v in (piece, swap(piece))]


def add(*terms):
    return sum(term.astype(F32) for term in terms).astype(BF)


def local(tokens, cotangent, ids, gates, wg, wu, wd):
    core, iy = lax.axis_index("core"), lax.axis_index("y")
    expert = (lax.axis_index("x") * 4 + lax.axis_index("z")).astype(jnp.int32).reshape(1)
    ys = [iy, jnp.where(core == 0, iy ^ 1, 3 - iy), jnp.where(core == 0, 3 - iy, iy ^ 1), (iy + 2) % 4]
    place = [2 * ys[k] + core if own else 2 * ys[(0, 2, 1, 3)[k]] + 1 - core for k in range(4) for own in (1, 0)]
    place = jnp.stack(place).astype(jnp.int32)
    wg, wu, wd = wg[0], wu[0], wd[0]

    send_x, send_dy, onehot = dispatch(ids.T, gates.T.astype(F32), tokens, cotangent)
    xs = ring(exchange(send_x))
    last = meet(xs[1], 1)
    xs = with_swaps(xs)
    came = exchange(send_dy)
    gate = came[:, COLS:]
    a, b = first_hidden(place, xs, wg, wu)
    dys = ring(came[:, :COLS])
    dys[1] = after(dys[1], a)
    dy_last = meet(dys[1], 1)
    xs = xs + with_swaps([last])
    dys = with_swaps(dys + [dy_last])

    s, slope, h = hidden(place, xs[6:], wg, wu, a, b)
    raw = first_raw(range(6), place, dys[:6], wd, h)
    dab, hs, sums = gradients(range(6, 8), place, dys[6:], wd, raw, s, slope, h, gate)

    def part(k, *later):
        sib, own = input_part(k, place, dab, sums, wg, wu, *later)
        return own, swap(sib)

    opposite = add(*part(3))
    second = part(2)
    first = part(1, opposite)
    opposite = meet(opposite, 1)
    near = add(*second)
    own = part(0, near)
    near = meet(near, 1)
    rest = meet(add(*first, opposite), 0)

    down_grad = row_gradient(place, dys, hs)
    gate_grad, up_grad = column_gradients(place, xs, dab)
    share = total(expert, (*own, near, rest), down_grad, gate_grad)
    input_grad, slot_grad = combine(exchange(share), onehot, ids)
    return input_grad, slot_grad, gate_grad[None], up_grad[None], down_grad[None]


def solution(mesh):
    torus = Mesh(mesh.devices.reshape(4, 4, 4, 2), ("x", "z", "y", "core"))
    ep, etp = ("x", "z"), ("y", "core")
    in_specs = (
        P(ep, etp),
        P(ep, etp),
        P(ep, None),
        P(ep, None),
        P(ep, None, etp),
        P(ep, None, etp),
        P(ep, etp, None),
    )
    out_specs = (P(ep, etp), P(ep, None), P(ep, None, etp), P(ep, None, etp), P(ep, etp, None))
    return jax.shard_map(local, mesh=torus, in_specs=in_specs, out_specs=out_specs, check_vma=False)
```

time: 380 us -> 231 us (0.61); the launches traced: 373 us -> 228 us
  local copies, waits for them, and re-layouts: 110 us -> 22.2 us
  matrix products: 64.3 us -> 0 us
  Pallas kernels: 0 us -> 60.2 us
  blocking collectives: 71.3 us -> 26 us
  between operations: 14.2 us -> 1.06 us
  starting transfers between devices: 14.5 us -> 26.6 us
    ppermute x0 -> x21, waiting for transfers between devices: none -> 66.4 us  [the longest x9 66.4 us: meet(): return lax.ppermute(v, ('y', 'core'), MEET[step])]
    unnamed x29 -> x70, local copies, waits for them, and re-layouts: 86.2 us -> 20.9 us
    dot_general x8 -> x0, matrix products: 64.3 us -> none  [the longest x1 13.4 us: local(): jnp.dot(db, wu.T, preferred_element_type=jnp.float32)]
    pallas_call x0 -> x14, Pallas kernels: none -> 60.2 us  [the longest x4 13.9 us: input_part(): call(functools.partial(input_kernel, k), ins, outs, scratch, us=3.5)]
    all_gather x2 -> x0, waiting for transfers between devices: 51.2 us -> none  [the longest x1 43.2 us: local(): lax.all_gather(recv_dy, 'etp', axis=2, tiled=True)]
    unnamed x4 -> x0, waiting for transfers between devices: 35.5 us -> none
    all_to_all x3 -> x1, blocking collectives: 57.4 us -> 26 us  [exchange(): lax.all_to_all(v.reshape(16, ROOM, -1), ('x', 'z'), 0, 0, tiled=True)]
    all_to_all x2, waiting for transfers between devices: 4.8 us -> 22.1 us  [exchange(): lax.all_to_all(v.reshape(16, ROOM, -1), ('x', 'z'), 0, 0, tiled=True)]
  transfers between devices with their start and end apart: 5 -> 23, of which waited for: 4 -> 8; matrix products, arithmetic and copies ran while one was open for 17% -> 2% of each run, Pallas kernels for 0% -> 21%
where the time goes in v2:
time: 231 us; the launch traced here: 228 us
  waiting for transfers between devices  88.5 us (38%)
  Pallas kernels  60.2 us (26%)
  starting transfers between devices  26.6 us (12%)
  blocking collectives  26 us (11%)
  local copies, waits for them, and re-layouts  22.2 us (10%)
  other arithmetic  3.8 us (2%)
    ppermute x9, waiting for transfers between devices, meet(): return lax.ppermute(v, ('y', 'core'), MEET[step])  66.4 us
    all_to_all x1, blocking collectives, exchange(): lax.all_to_all(v.reshape(16, ROOM, -1), ('x', 'z'), 0, 0, tiled=True)  26 us
    all_to_all x2, waiting for transfers between devices, exchange(): lax.all_to_all(v.reshape(16, ROOM, -1), ('x', 'z'), 0, 0, tiled=True)  22.1 us
    unnamed x70, local copies, waits for them, and re-layouts  20.9 us
    pallas_call x4, Pallas kernels, input_part(): call(functools.partial(input_kernel, k), ins, outs, scratch, us=3.5)  13.9 us
    ppermute x9, starting transfers between devices, meet(): return lax.ppermute(v, ('y', 'core'), MEET[step])  12.7 us
    all_to_all x2, starting transfers between devices, exchange(): lax.all_to_all(v.reshape(16, ROOM, -1), ('x', 'z'), 0, 0, tiled=True)  11.1 us
    pallas_call x1, Pallas kernels, column_gradients(): call(column_gradient_kernel, [SMEM] + [HBM] * 8 + [VMEM], outs, scratch,...  10.6 us
  transfers between devices with their start and end apart: 23, of which 8 were waited for; matrix products, arithmetic and copies ran while one was open for 2% of the time, Pallas kernels for 21%

profile of v2, /device:TPU:0, one launch (start us, length us, event | category | flops | bytes accessed | tf_op | source)
XLA Modules:
  0.0 228.4 jit_solution(11516776212841515882)
XLA Ops:
  3.8 1.9 shard_map.110
  5.7 26.0 %all_to_all.15 = bf16[16,40,896]{2,1,0:T(8,128)(2,1)} all-to-all(bf16[16,40,896]{2,1,0:T(8,128)(2,1)S(1)} %bitcast.41), channel_id=1, replica_groups=mesh['x'=4,'z'=4,'y'=4,'core'=2] {'x','z'}, dimensions={0} | all-to-all | bytes 2293760 | tf_op jit(solution)/shard_map/all_to_all | solution.py:367
  31.8 3.7 %all-to-all-start = ((bf16[16,40,1024]{2,1,0:T(8,128)(2,1)}), bf16[16,40,1024]{2,1,0:T(8,128)(2,1)S(1)}, u32[]{:S(2)}, u32[]{:S(2)}) async-start(bf16[16,40,1024]{2,1,0:T(8,128)(2,1)} %bitcast.11), calls=%async_computation | async-start | bytes 2621440 | tf_op jit(solution)/shard_map/all_to_all | solution.py:367
  35.5 1.7 collective-permute-start.2
  37.1 2.2 collective-permute-start.4
  39.3 24.5 %collective-permute-done.2.refs_2_ = bf16[640,896]{1,0:T(8,128)(2,1)} collective-permute-done((bf16[640,896]{1,0:T(8,128)(2,1)}, bf16[640,896]{1,0:T(8,128)(2,1)}, u32[]{:S(2)}, u32[]{:S(2)}) %collective-permute-start.2) | collective-permute-done | bytes 1146912 | tf_op jit(solution)/shard_map/ppermute | solution.py:29
  67.3 2.4 %collective-permute-start.12 = (bf16[640,896]{1,0:T(8,128)(2,1)}, bf16[640,896]{1,0:T(8,128)(2,1)}, u32[]{:S(2)}, u32[]{:S(2)}) collective-permute-start(bf16[640,896]{1,0:T(8,128)(2,1)} %collective-permute-done.2.refs_2_), channel_id=1, source_target_pairs={{0,6},{1,3},{2,4},{3,1},{4,2},{5,7},{6,0},{7,5},{8,14},{9,11},{10,... | collective-permute-start | bytes 3440648 | tf_op jit(solution)/shard_map/ppermute | solution.py:29
  69.7 2.0 copy-done
  71.7 2.0 copy-done.3
  73.7 9.2 %shard_map.111 = (f32[640,256]{1,0:T(8,128)S(1)}, f32[640,256]{1,0:T(8,128)S(1)}) custom-call(s32[8]{0:T(128)S(1)} %stack.35.place, bf16[640,896]{1,0:T(8,128)(2,1)} %bitcast.14.refs_0_, bf16[640,896]{1,0:T(8,128)(2,1)} %collective-permute-done.1.refs_1_, bf16[640,896]{1,0:T(8,128)(2,1)} %collective-permute-done.2.refs_2_, ...), custom_call_target="tpu_custom_call" | custom-call | bytes 32400000 | tf_op jit(solution)/shard_map/pallas_call | solution.py:171
  84.6 8.4 %collective-permute-done.refs_0_ = bf16[640,896]{1,0:T(8,128)(2,1)S(1)} collective-permute-done((bf16[640,896]{1,0:T(8,128)(2,1)S(1)}, bf16[640,896]{1,0:T(8,128)(2,1)S(1)}, u32[]{:S(2)}, u32[]{:S(2)}) %collective-permute-start) | collective-permute-done | bytes 1146912 | tf_op jit(solution)/shard_map/ppermute | solution.py:29
  95.5 10.9 %collective-permute-done.12.refs_0_.refs_6_ = bf16[640,896]{1,0:T(8,128)(2,1)} collective-permute-done((bf16[640,896]{1,0:T(8,128)(2,1)}, bf16[640,896]{1,0:T(8,128)(2,1)}, u32[]{:S(2)}, u32[]{:S(2)}) %collective-permute-start.12) | collective-permute-done | bytes 1146912 | tf_op jit(solution)/shard_map/ppermute | solution.py:29
  107.4 11.2 %collective-permute-done.6.refs_0_.refs_6_ = bf16[640,896]{1,0:T(8,128)(2,1)S(1)} collective-permute-done((bf16[640,896]{1,0:T(8,128)(2,1)}, bf16[640,896]{1,0:T(8,128)(2,1)S(1)}, u32[]{:S(2)}, u32[]{:S(2)}) %collective-permute-start.6) | collective-permute-done | bytes 1146912 | tf_op jit(solution)/shard_map/ppermute | solution.py:29
  119.7 2.4 %copy-done.1 = bf16[1,7168,256]{2,1,0:T(8,128)(2,1)S(1)} copy-done((bf16[1,7168,256]{2,1,0:T(8,128)(2,1)S(1)}, bf16[1,7168,256]{2,1,0:T(8,128)(2,1)}, u32[]{:S(2)}) %copy-start.1) | copy-done | bytes 3670040
  122.1 2.0 copy-done.4
  125.3 4.1 %shard_map.113 = (f32[640,256]{1,0:T(8,128)S(1)}, f32[640,256]{1,0:T(8,128)S(1)}, f32[640,256]{1,0:T(8,128)S(1)}) custom-call(s32[8]{0:T(128)S(1)} %stack.35.place, bf16[640,896]{1,0:T(8,128)(2,1)} %collective-permute-done.12.refs_0_.refs_6_, bf16[640,896]{1,0:T(8,128)(2,1)S(1)} %collective-permute-done.13.refs_1_.refs_7_, bf16[7168,256]{1,0:T(8,128)(2,1)S(1)} %bitcast.25, ...), custom_call_target="tpu_custom_call" | custom-call | bytes 18000000 | tf_op jit(solution)/shard_map/pallas_call | solution.py:179
  129.5 5.3 %shard_map.114.refs_3_ = f32[640,256]{1,0:T(8,128)S(1)} custom-call(s32[8]{0:T(128)S(1)} %stack.35.place, bf16[640,896]{1,0:T(8,128)(2,1)S(1)} %slice.8.refs_0_, bf16[640,896]{1,0:T(8,128)(2,1)S(1)} %collective-permute-done.8.refs_1_, bf16[640,896]{1,0:T(8,128)(2,1)S(1)} %copy-done.9, bf16[640,896]{1,0:T(8,128)(2,1)S(1)} %collective-permute-done.9.refs_3_, ...), custom_call_target="tpu_custom_call" | custom-call | bytes 18000000 | tf_op jit(solution)/shard_map/pallas_call | solution.py:224
  134.8 2.6 %shard_map.115 = (bf16[640,512]{1,0:T(8,128)(2,1)S(1)}, bf16[640,256]{1,0:T(8,128)(2,1)S(1)}, f32[16,896]{1,0:T(8,128)S(1)}) custom-call(s32[8]{0:T(128)S(1)} %stack.35.place, bf16[640,896]{1,0:T(8,128)(2,1)S(1)} %collective-permute-done.6.refs_0_.refs_6_, bf16[640,896]{1,0:T(8,128)(2,1)S(1)} %collective-permute-done.7.refs_1_.refs_7_, ...), custom_call_target="tpu_custom_call" | custom-call | bytes 21600000 | tf_op jit(solution)/shard_map/pallas_call | solution.py:250
  138.3 3.4 %shard_map.118 = (bf16[656,896]{1,0:T(8,128)(2,1)S(1)}, bf16[656,896]{1,0:T(8,128)(2,1)S(1)}) custom-call(s32[8]{0:T(128)S(1)} %stack.35.place, bf16[640,512]{1,0:T(8,128)(2,1)S(1)} %get-tuple-element.35.dab.refs_8_, f32[16,896]{1,0:T(8,128)S(1)} %get-tuple-element.36.sums, bf16[7168,256]{1,0:T(8,128)(2,1)S(1)} %bitcast.26, bf16[7168,256]{1,0:T(8,128)(2,1)S(1)} %bitcast.32), custom_call_target="tpu_custom_call" | custom-call | bytes 12600000 | tf_op jit(solution)/shard_map/pallas_call | solution.py:276
  142.4 3.4 %shard_map.116 = (bf16[656,896]{1,0:T(8,128)(2,1)S(1)}, bf16[656,896]{1,0:T(8,128)(2,1)S(1)}) custom-call(s32[8]{0:T(128)S(1)} %stack.35.place, bf16[640,512]{1,0:T(8,128)(2,1)S(1)} %get-tuple-element.35.dab.refs_8_, f32[16,896]{1,0:T(8,128)S(1)} %get-tuple-element.36.sums, bf16[7168,256]{1,0:T(8,128)(2,1)S(1)} %bitcast.27, bf16[7168,256]{1,0:T(8,128)(2,1)S(1)} %bitcast.33), custom_call_target="tpu_custom_call" | custom-call | bytes 12600000 | tf_op jit(solution)/shard_map/pallas_call | solution.py:276
  146.4 3.4 %shard_map.119 = (bf16[656,896]{1,0:T(8,128)(2,1)S(1)}, bf16[656,896]{1,0:T(8,128)(2,1)S(1)}) custom-call(s32[8]{0:T(128)S(1)} %stack.35.place, bf16[640,512]{1,0:T(8,128)(2,1)S(1)} %get-tuple-element.35.dab.refs_8_, f32[16,896]{1,0:T(8,128)S(1)} %get-tuple-element.36.sums, bf16[7168,256]{1,0:T(8,128)(2,1)S(1)} %bitcast.28, bf16[7168,256]{1,0:T(8,128)(2,1)S(1)} %bitcast.34, ...), custom_call_target="tpu_custom_call" | custom-call | bytes 12600000 | tf_op jit(solution)/shard_map/pallas_call | solution.py:276
  150.2 1.9 collective-permute-start.19
  153.5 3.6 %shard_map.117 = (bf16[656,896]{1,0:T(8,128)(2,1)}, bf16[656,896]{1,0:T(8,128)(2,1)S(1)}) custom-call(s32[8]{0:T(128)S(1)} %stack.35.place, bf16[640,512]{1,0:T(8,128)(2,1)S(1)} %get-tuple-element.35.dab.refs_8_, f32[16,896]{1,0:T(8,128)S(1)} %get-tuple-element.36.sums, bf16[7168,256]{1,0:T(8,128)(2,1)S(1)} %bitcast.29, bf16[7168,256]{1,0:T(8,128)(2,1)S(1)} %bitcast.35, ...), custom_call_target="tpu_custom_call" | custom-call | bytes 12600000 | tf_op jit(solution)/shard_map/pallas_call | solution.py:276
  158.5 9.1 %collective-permute-done.19 = bf16[656,896]{1,0:T(8,128)(2,1)S(1)} collective-permute-done((bf16[656,896]{1,0:T(8,128)(2,1)S(1)}, bf16[656,896]{1,0:T(8,128)(2,1)S(1)}, u32[]{:S(2)}, u32[]{:S(2)}) %collective-permute-start.19) | collective-permute-done | bytes 1175584 | tf_op jit(solution)/shard_map/ppermute | solution.py:29
  167.6 1.5 add_convert_fusion
  170.4 10.6 %shard_map.121 = (bf16[7168,256]{1,0:T(8,128)(2,1)}, bf16[7168,256]{1,0:T(8,128)(2,1)}) custom-call(s32[8]{0:T(128)S(1)} %stack.35.place, bf16[640,896]{1,0:T(8,128)(2,1)} %bitcast.14.refs_0_, bf16[640,896]{1,0:T(8,128)(2,1)} %collective-permute-done.1.refs_1_, bf16[640,896]{1,0:T(8,128)(2,1)} %collective-permute-done.2.refs_2_, ...), custom_call_target="tpu_custom_call" | custom-call | bytes 36000000 | tf_op jit(solution)/shard_map/pallas_call | solution.py:314
  181.0 7.5 %shard_map.120.refs_4_ = bf16[256,7168]{1,0:T(8,128)(2,1)} custom-call(s32[8]{0:T(128)S(1)} %stack.35.place, bf16[640,896]{1,0:T(8,128)(2,1)S(1)} %slice.8.refs_0_, bf16[640,896]{1,0:T(8,128)(2,1)S(1)} %copy-done.13, bf16[640,896]{1,0:T(8,128)(2,1)S(1)} %copy-done.9, bf16[640,896]{1,0:T(8,128)(2,1)S(1)} %copy-done.17, ...), custom_call_target="tpu_custom_call" | custom-call | bytes 21600000 | tf_op jit(solution)/shard_map/pallas_call | solution.py:344
  189.2 1.7 collective-permute-done.20.refs_3_
  190.9 2.0 copy-done.7
  193.0 4.1 %shard_map.122 = bf16[640,1024]{1,0:T(8,128)(2,1)} custom-call(s32[1]{0:T(128)} %bitcast.expert, bf16[656,896]{1,0:T(8,128)(2,1)S(1)} %copy-done.26, bf16[656,896]{1,0:T(8,128)(2,1)} %collective-permute-done.15.refs_1_, bf16[656,896]{1,0:T(8,128)(2,1)} %collective-permute-done.16.refs_2_, bf16[656,896]{1,0:T(8,128)(2,1)} %collective-permute-done.20.refs_3_, ...), custom_call_target="tpu_custom_call" | custom-call | bytes 7200000 | tf_op jit(solution)/shard_map/pallas_call | solution.py:363
  197.1 7.4 %all-to-all-start.2 = ((bf16[16,40,1024]{2,1,0:T(8,128)(2,1)}), bf16[16,40,1024]{2,1,0:T(8,128)(2,1)S(1)}, u32[]{:S(2)}, u32[]{:S(2)}) async-start(bf16[16,40,1024]{2,1,0:T(8,128)(2,1)} %bitcast.18), calls=%async_computation.2 | async-start | bytes 2621440 | tf_op jit(solution)/shard_map/all_to_all | solution.py:367
  204.6 22.1 %all-to-all-done.2 = bf16[16,40,1024]{2,1,0:T(8,128)(2,1)S(1)} async-done(((bf16[16,40,1024]{2,1,0:T(8,128)(2,1)}), bf16[16,40,1024]{2,1,0:T(8,128)(2,1)S(1)}, u32[]{:S(2)}, u32[]{:S(2)}) %all-to-all-start.2) | async-done | bytes 1310752 | tf_op jit(solution)/shard_map/all_to_all | solution.py:367
  (106 shorter events, 23.1 us)
Async XLA Ops:
  31.8 32.6 %all-to-all-start = ((bf16[16,40,1024]{2,1,0:T(8,128)(2,1)}), bf16[16,40,1024]{2,1,0:T(8,128)(2,1)S(1)}, u32[]{:S(2)}, u32[]{:S(2)}) async-start(bf16[16,40,1024]{2,1,0:T(8,128)(2,1)} %bitcast.11), calls=%async_computation | async-start | bytes 2621440 | tf_op jit(solution)/shard_map/all_to_all | solution.py:367
  35.5 28.3 %collective-permute-start.2 = (bf16[640,896]{1,0:T(8,128)(2,1)}, bf16[640,896]{1,0:T(8,128)(2,1)}, u32[]{:S(2)}, u32[]{:S(2)}) collective-permute-start(bf16[640,896]{1,0:T(8,128)(2,1)} %bitcast.14.refs_0_), channel_id=1, source_target_pairs={{0,2},{1,7},{2,0},{3,5},{4,6},{5,3},{6,4},{7,1},{8,10},{9,15},{10,... | collective-permute-start | bytes 3440648 | tf_op jit(solution)/shard_map/ppermute | solution.py:29
  37.1 26.7 %collective-permute-start.4 = (bf16[640,896]{1,0:T(8,128)(2,1)}, bf16[640,896]{1,0:T(8,128)(2,1)}, u32[]{:S(2)}, u32[]{:S(2)}) collective-permute-start(bf16[640,896]{1,0:T(8,128)(2,1)} %bitcast.14.refs_0_), channel_id=1, source_target_pairs={{0,6},{1,3},{2,4},{3,1},{4,2},{5,7},{6,0},{7,5},{8,14},{9,11},{10,... | collective-permute-start | bytes 3440648 | tf_op jit(solution)/shard_map/ppermute | solution.py:29
  39.3 28.0 %collective-permute-start.1 = (bf16[640,896]{1,0:T(8,128)(2,1)}, bf16[640,896]{1,0:T(8,128)(2,1)}, u32[]{:S(2)}, u32[]{:S(2)}) collective-permute-start(bf16[640,896]{1,0:T(8,128)(2,1)} %bitcast.14.refs_0_), channel_id=1, source_target_pairs={{0,1},{1,0},{2,3},{3,2},{4,5},{5,4},{6,7},{7,6},{8,9},{9,8},{10,11... | collective-permute-start | bytes 3440648 | tf_op jit(solution)/shard_map/ppermute | solution.py:33
  63.8 5.8 %collective-permute-start.3 = (bf16[640,896]{1,0:T(8,128)(2,1)}, bf16[640,896]{1,0:T(8,128)(2,1)}, u32[]{:S(2)}, u32[]{:S(2)}) collective-permute-start(bf16[640,896]{1,0:T(8,128)(2,1)} %collective-permute-done.2.refs_2_), channel_id=1, source_target_pairs={{0,1},{1,0},{2,3},{3,2},{4,5},{5,4},{6,7},{7,6},{8,9},{9,8},{10,11... | collective-permute-start | bytes 3440648 | tf_op jit(solution)/shard_map/ppermute | solution.py:33
  63.8 5.8 %collective-permute-start.5 = (bf16[640,896]{1,0:T(8,128)(2,1)}, bf16[640,896]{1,0:T(8,128)(2,1)}, u32[]{:S(2)}, u32[]{:S(2)}) collective-permute-start(bf16[640,896]{1,0:T(8,128)(2,1)} %collective-permute-done.4.refs_4_), channel_id=1, source_target_pairs={{0,1},{1,0},{2,3},{3,2},{4,5},{5,4},{6,7},{7,6},{8,9},{9,8},{10,11... | collective-permute-start | bytes 3440648 | tf_op jit(solution)/shard_map/ppermute | solution.py:33
  65.5 27.5 %collective-permute-start = (bf16[640,896]{1,0:T(8,128)(2,1)S(1)}, bf16[640,896]{1,0:T(8,128)(2,1)S(1)}, u32[]{:S(2)}, u32[]{:S(2)}) collective-permute-start(bf16[640,896]{1,0:T(8,128)(2,1)S(1)} %slice.8.refs_0_), channel_id=1, source_target_pairs={{0,2},{1,7},{2,0},{3,5},{4,6},{5,3},{6,4},{7,1},{8,10},{9,15},{10,... | collective-permute-start | bytes 3440648 | tf_op jit(solution)/shard_map/ppermute | solution.py:29
  66.4 40.5 %collective-permute-start.10 = (bf16[640,896]{1,0:T(8,128)(2,1)S(1)}, bf16[640,896]{1,0:T(8,128)(2,1)}, u32[]{:S(2)}, u32[]{:S(2)}) collective-permute-start(bf16[640,896]{1,0:T(8,128)(2,1)S(1)} %slice.8.refs_0_), channel_id=1, source_target_pairs={{0,6},{1,3},{2,4},{3,1},{4,2},{5,7},{6,0},{7,5},{8,14},{9,11},{10,... | collective-permute-start | bytes 3440648 | tf_op jit(solution)/shard_map/ppermute | solution.py:29
  67.3 39.1 %collective-permute-start.12 = (bf16[640,896]{1,0:T(8,128)(2,1)}, bf16[640,896]{1,0:T(8,128)(2,1)}, u32[]{:S(2)}, u32[]{:S(2)}) collective-permute-start(bf16[640,896]{1,0:T(8,128)(2,1)} %collective-permute-done.2.refs_2_), channel_id=1, source_target_pairs={{0,6},{1,3},{2,4},{3,1},{4,2},{5,7},{6,0},{7,5},{8,14},{9,11},{10,... | collective-permute-start | bytes 3440648 | tf_op jit(solution)/shard_map/ppermute | solution.py:29
  94.0 25.7 %copy-start.24 = (f32[640,256]{1,0:T(8,128)S(1)}, f32[640,256]{1,0:T(8,128)}, u32[]{:S(2)}) copy-start(f32[640,256]{1,0:T(8,128)} %copy-done.23) | copy-start | bytes 1966084
  94.0 24.6 %collective-permute-start.6 = (bf16[640,896]{1,0:T(8,128)(2,1)}, bf16[640,896]{1,0:T(8,128)(2,1)S(1)}, u32[]{:S(2)}, u32[]{:S(2)}) collective-permute-start(bf16[640,896]{1,0:T(8,128)(2,1)} %shard_map.112.refs_2_), channel_id=1, source_target_pairs={{0,6},{1,3},{2,4},{3,1},{4,2},{5,7},{6,0},{7,5},{8,14},{9,11},{10,... | collective-permute-start | bytes 3440648 | tf_op jit(solution)/shard_map/ppermute | solution.py:29
  106.3 13.3 %collective-permute-start.13 = (bf16[640,896]{1,0:T(8,128)(2,1)}, bf16[640,896]{1,0:T(8,128)(2,1)S(1)}, u32[]{:S(2)}, u32[]{:S(2)}) collective-permute-start(bf16[640,896]{1,0:T(8,128)(2,1)} %collective-permute-done.12.refs_0_.refs_6_), channel_id=1, source_target_pairs={{0,1},{1,0},{2,3},{3,2},{4,5},{5,4},{6,7},{7,6},{8,9},{9,8},{10,11... | collective-permute-start | bytes 3440648 | tf_op jit(solution)/shard_map/ppermute | solution.py:33
  106.3 23.0 %collective-permute-start.8 = (bf16[640,896]{1,0:T(8,128)(2,1)S(1)}, bf16[640,896]{1,0:T(8,128)(2,1)S(1)}, u32[]{:S(2)}, u32[]{:S(2)}) collective-permute-start(bf16[640,896]{1,0:T(8,128)(2,1)S(1)} %slice.8.refs_0_), channel_id=1, source_target_pairs={{0,1},{1,0},{2,3},{3,2},{4,5},{5,4},{6,7},{7,6},{8,9},{9,8},{10,11... | collective-permute-start | bytes 3440648 | tf_op jit(solution)/shard_map/ppermute | solution.py:33
  106.9 22.5 %collective-permute-start.11 = (bf16[640,896]{1,0:T(8,128)(2,1)}, bf16[640,896]{1,0:T(8,128)(2,1)S(1)}, u32[]{:S(2)}, u32[]{:S(2)}) collective-permute-start(bf16[640,896]{1,0:T(8,128)(2,1)} %collective-permute-done.10.refs_4_), channel_id=1, source_target_pairs={{0,1},{1,0},{2,3},{3,2},{4,5},{5,4},{6,7},{7,6},{8,9},{9,8},{10,11... | collective-permute-start | bytes 3440648 | tf_op jit(solution)/shard_map/ppermute | solution.py:33
  106.9 22.6 %collective-permute-start.9 = (bf16[640,896]{1,0:T(8,128)(2,1)}, bf16[640,896]{1,0:T(8,128)(2,1)S(1)}, u32[]{:S(2)}, u32[]{:S(2)}) collective-permute-start(bf16[640,896]{1,0:T(8,128)(2,1)} %shard_map.112.refs_2_), channel_id=1, source_target_pairs={{0,1},{1,0},{2,3},{3,2},{4,5},{5,4},{6,7},{7,6},{8,9},{9,8},{10,11... | collective-permute-start | bytes 3440648 | tf_op jit(solution)/shard_map/ppermute | solution.py:33
  118.5 16.2 %copy-start.10 = (bf16[640,896]{1,0:T(8,128)(2,1)}, bf16[640,896]{1,0:T(8,128)(2,1)S(1)}, u32[]{:S(2)}) copy-start(bf16[640,896]{1,0:T(8,128)(2,1)S(1)} %collective-permute-done.6.refs_0_.refs_6_) | copy-start | bytes 3440644
  118.5 16.2 %collective-permute-start.7 = (bf16[640,896]{1,0:T(8,128)(2,1)S(1)}, bf16[640,896]{1,0:T(8,128)(2,1)S(1)}, u32[]{:S(2)}, u32[]{:S(2)}) collective-permute-start(bf16[640,896]{1,0:T(8,128)(2,1)S(1)} %collective-permute-done.6.refs_0_.refs_6_), channel_id=1, source_target_pairs={{0,1},{1,0},{2,3},{3,2},{4,5},{5,4},{6,7},{7,6},{8,9},{9,8},{10,11... | collective-permute-start | bytes 3440648 | tf_op jit(solution)/shard_map/ppermute | solution.py:33
  141.8 4.3 %collective-permute-start.17 = (bf16[656,896]{1,0:T(8,128)(2,1)S(1)}, bf16[656,896]{1,0:T(8,128)(2,1)S(1)}, u32[]{:S(2)}, u32[]{:S(2)}) collective-permute-start(bf16[656,896]{1,0:T(8,128)(2,1)S(1)} %get-tuple-element.42), channel_id=1, source_target_pairs={{0,1},{1,0},{2,3},{3,2},{4,5},{5,4},{6,7},{7,6},{8,9},{9,8},{10,11... | collective-permute-start | bytes 3526664 | tf_op jit(solution)/shard_map/ppermute | solution.py:33
  145.8 6.3 %collective-permute-start.14 = (bf16[656,896]{1,0:T(8,128)(2,1)S(1)}, bf16[656,896]{1,0:T(8,128)(2,1)S(1)}, u32[]{:S(2)}, u32[]{:S(2)}) collective-permute-start(bf16[656,896]{1,0:T(8,128)(2,1)S(1)} %get-tuple-element.38), channel_id=1, source_target_pairs={{0,1},{1,0},{2,3},{3,2},{4,5},{5,4},{6,7},{7,6},{8,9},{9,8},{10,11... | collective-permute-start | bytes 3526664 | tf_op jit(solution)/shard_map/ppermute | solution.py:33
  149.8 8.7 %collective-permute-start.18 = (bf16[656,896]{1,0:T(8,128)(2,1)S(1)}, bf16[656,896]{1,0:T(8,128)(2,1)S(1)}, u32[]{:S(2)}, u32[]{:S(2)}) collective-permute-start(bf16[656,896]{1,0:T(8,128)(2,1)S(1)} %get-tuple-element.44), channel_id=1, source_target_pairs={{0,1},{1,0},{2,3},{3,2},{4,5},{5,4},{6,7},{7,6},{8,9},{9,8},{10,11... | collective-permute-start | bytes 3526664 | tf_op jit(solution)/shard_map/ppermute | solution.py:33
  150.2 17.4 %collective-permute-start.19 = (bf16[656,896]{1,0:T(8,128)(2,1)S(1)}, bf16[656,896]{1,0:T(8,128)(2,1)S(1)}, u32[]{:S(2)}, u32[]{:S(2)}) collective-permute-start(bf16[656,896]{1,0:T(8,128)(2,1)S(1)} %add_convert_fusion.1.refs_0_), channel_id=1, source_target_pairs={{0,6},{1,3},{2,4},{3,1},{4,2},{5,7},{6,0},{7,5},{8,14},{9,11},{10,... | collective-permute-start | bytes 3526664 | tf_op jit(solution)/shard_map/ppermute | solution.py:29
  157.1 12.0 %copy-start.25 = (bf16[656,896]{1,0:T(8,128)(2,1)}, bf16[656,896]{1,0:T(8,128)(2,1)S(1)}, u32[]{:S(2)}) copy-start(bf16[656,896]{1,0:T(8,128)(2,1)S(1)} %get-tuple-element.39.refs_0_) | copy-start | bytes 3526660
  157.1 32.1 %collective-permute-start.16 = (bf16[656,896]{1,0:T(8,128)(2,1)}, bf16[656,896]{1,0:T(8,128)(2,1)}, u32[]{:S(2)}, u32[]{:S(2)}) collective-permute-start(bf16[656,896]{1,0:T(8,128)(2,1)} %add_convert_fusion.2.refs_0_), channel_id=1, source_target_pairs={{0,6},{1,3},{2,4},{3,1},{4,2},{5,7},{6,0},{7,5},{8,14},{9,11},{10,... | collective-permute-start | bytes 3526664 | tf_op jit(solution)/shard_map/ppermute | solution.py:29
  158.5 30.0 %collective-permute-start.15 = (bf16[656,896]{1,0:T(8,128)(2,1)}, bf16[656,896]{1,0:T(8,128)(2,1)}, u32[]{:S(2)}, u32[]{:S(2)}) collective-permute-start(bf16[656,896]{1,0:T(8,128)(2,1)} %get-tuple-element.40), channel_id=1, source_target_pairs={{0,1},{1,0},{2,3},{3,2},{4,5},{5,4},{6,7},{7,6},{8,9},{9,8},{10,11... | collective-permute-start | bytes 3526664 | tf_op jit(solution)/shard_map/ppermute | solution.py:33
  169.1 21.8 %collective-permute-start.20 = (bf16[656,896]{1,0:T(8,128)(2,1)}, bf16[656,896]{1,0:T(8,128)(2,1)}, u32[]{:S(2)}, u32[]{:S(2)}) collective-permute-start(bf16[656,896]{1,0:T(8,128)(2,1)} %add_convert_fusion), channel_id=1, source_target_pairs={{0,2},{1,7},{2,0},{3,5},{4,6},{5,3},{6,4},{7,1},{8,10},{9,15},{10,... | collective-permute-start | bytes 3526664 | tf_op jit(solution)/shard_map/ppermute | solution.py:29
  170.4 10.6 %copy-start.11 = (bf16[640,896]{1,0:T(8,128)(2,1)S(1)}, bf16[640,896]{1,0:T(8,128)(2,1)}, u32[]{:S(2)}) copy-start(bf16[640,896]{1,0:T(8,128)(2,1)} %copy-done.10) | copy-start | bytes 3440644
  170.4 10.6 %copy-start.13 = (bf16[640,896]{1,0:T(8,128)(2,1)S(1)}, bf16[640,896]{1,0:T(8,128)(2,1)}, u32[]{:S(2)}) copy-start(bf16[640,896]{1,0:T(8,128)(2,1)} %copy-done.12) | copy-start | bytes 3440644
  170.4 10.6 %copy-start.15 = (bf16[640,896]{1,0:T(8,128)(2,1)S(1)}, bf16[640,896]{1,0:T(8,128)(2,1)}, u32[]{:S(2)}) copy-start(bf16[640,896]{1,0:T(8,128)(2,1)} %copy-done.14) | copy-start | bytes 3440644
  170.4 10.6 %copy-start.17 = (bf16[640,896]{1,0:T(8,128)(2,1)S(1)}, bf16[640,896]{1,0:T(8,128)(2,1)}, u32[]{:S(2)}) copy-start(bf16[640,896]{1,0:T(8,128)(2,1)} %copy-done.16) | copy-start | bytes 3440644
  170.4 10.6 %copy-start.19 = (bf16[640,896]{1,0:T(8,128)(2,1)S(1)}, bf16[640,896]{1,0:T(8,128)(2,1)}, u32[]{:S(2)}) copy-start(bf16[640,896]{1,0:T(8,128)(2,1)} %copy-done.18) | copy-start | bytes 3440644
  181.0 9.9 %copy-start.22 = (bf16[7168,256]{1,0:T(8,128)(2,1)S(1)}, bf16[7168,256]{1,0:T(8,128)(2,1)}, u32[]{:S(2)}) copy-start(bf16[7168,256]{1,0:T(8,128)(2,1)} %get-tuple-element.46.refs_5_) | copy-start | bytes 11010052
  197.1 29.6 %all-to-all-start.2 = ((bf16[16,40,1024]{2,1,0:T(8,128)(2,1)}), bf16[16,40,1024]{2,1,0:T(8,128)(2,1)S(1)}, u32[]{:S(2)}, u32[]{:S(2)}) async-start(bf16[16,40,1024]{2,1,0:T(8,128)(2,1)} %bitcast.18), calls=%async_computation.2 | async-start | bytes 2621440 | tf_op jit(solution)/shard_map/all_to_all | solution.py:367
  (25 other events, 79.4 us)

commit v3 on v2

v3 whole, which is shorter than its diff:
```python
import functools

import jax
import jax.numpy as jnp
from jax import lax
from jax.experimental import pallas as pl
from jax.experimental.pallas import tpu as pltpu
from jax.sharding import Mesh, PartitionSpec as P

BF, F32 = jnp.bfloat16, jnp.float32
ROWS, COLS, HID, PAD, ROOM, TAIL = 640, 896, 256, 128, 40, 16
SWAP = [(0, 1), (1, 0)]
ANY = pl.BlockSpec(memory_space=pl.ANY)
MOST = 61
RATE = 3e10
VMEM = pl.BlockSpec(memory_space=pltpu.VMEM)
SMEM = pl.BlockSpec(memory_space=pltpu.SMEM)
HBM = pl.BlockSpec(memory_space=pltpu.HBM)


def partner(i, core, step):
    return i ^ 1 if core == step else 3 - i


MEET = tuple(
    [(2 * i + c, 2 * partner(i, c, step) + c) for i in range(4) for c in range(2)] for step in range(2)
)


def meet(v, step):
    return lax.ppermute(v, ("y", "core"), MEET[step])


def swap(v):
    return lax.ppermute(v, "core", SWAP)


def nn(left, right):
    return jnp.dot(left, right, preferred_element_type=F32)


def nt(left, right):
    return lax.dot_general(left, right, (((1,), (1,)), ((), ())), preferred_element_type=F32)


def tn(left, right):
    return lax.dot_general(left, right, (((0,), (0,)), ((), ())), preferred_element_type=F32)


def sds(shape, dtype=BF):
    return jax.ShapeDtypeStruct(shape, dtype)


def call(kernel, ins, outs, scratch=(), us=1, mib=24):
    return pl.pallas_call(
        kernel,
        in_specs=ins,
        out_specs=[spec for spec, _ in outs],
        out_shape=[shape for _, shape in outs],
        scratch_shapes=scratch,
        compiler_params=pltpu.CompilerParams(vmem_limit_bytes=mib * 2**20),
        cost_estimate=pl.CostEstimate(flops=int(us * RATE), bytes_accessed=10000, transcendentals=0),
    )


def dispatch_kernel(ids, gates, x_ref, dy_ref, send_x, send_dy, onehot, x, dy, sems):
    copies = [pltpu.make_async_copy(x_ref, x, sems.at[0]), pltpu.make_async_copy(dy_ref, dy, sems.at[1])]
    for copy in copies:
        copy.start()
    expert = lax.broadcasted_iota(jnp.int32, (16, 64), 0)
    named = jnp.zeros((16, 64), F32)
    weight = jnp.zeros((16, 64), F32)
    for k in range(8):
        here = ids[k : k + 1, :] == expert
        named = named + jnp.where(here, 1.0, 0.0)
        weight = weight + jnp.where(here, gates[k : k + 1, :], 0.0)
    one, two = (lax.broadcasted_iota(jnp.int32, (64, 64), axis) for axis in range(2))
    rank = nn(named.astype(BF), jnp.where(one < two, 1.0, 0.0).astype(BF)).astype(jnp.int32)
    slot = lax.broadcasted_iota(jnp.int32, (ROOM, 64), 0)
    picks, sums = [], []
    for e in range(16):
        pick = jnp.where((rank[e : e + 1, :] == slot) & (named[e : e + 1, :] > 0.0), 1.0, 0.0)
        picks.append(pick)
        sums.append(jnp.sum(pick * weight[e : e + 1, :], axis=1, keepdims=True))
    pick = jnp.concatenate(picks, axis=0).astype(BF)
    onehot[...] = pick
    for copy in copies:
        copy.wait()
    send_x[...] = nn(pick, x[...]).astype(BF)
    send_dy[:, :COLS] = nn(pick, dy[...]).astype(BF)
    send_dy[:, COLS:] = jnp.broadcast_to(jnp.concatenate(sums, axis=0), (ROWS, PAD)).astype(BF)


def dispatch(ids, gates, x, dy):
    outs = [(VMEM, sds((ROWS, COLS))), (VMEM, sds((ROWS, COLS + PAD))), (VMEM, sds((ROWS, 64)))]
    scratch = [pltpu.VMEM((64, COLS), BF)] * 2 + [pltpu.SemaphoreType.DMA((2,))]
    return call(dispatch_kernel, [VMEM] * 2 + [HBM] * 2, outs, scratch, us=4)(ids, gates, x, dy)


def combine_kernel(back, onehot, ids, *refs):
    grad, gate = refs[-2:]
    pick = onehot[...]
    grad[...] = tn(pick, back[:, :COLS]).astype(BF)
    sums = tn(pick, back[:, COLS:])
    lane = lax.broadcasted_iota(jnp.int32, (64, PAD), 1)
    total = jnp.zeros((64, PAD), F32)
    for k in range(8):
        mine = ids[:, k : k + 1]
        value = jnp.sum(jnp.where((lane == mine) | (lane == mine + 64), sums, 0.0), axis=1, keepdims=True)
        total = total + jnp.where(lane == k, value, 0.0)
    gate[...] = total[:, :8]


def combine(back, onehot, ids, later):
    outs = [(VMEM, sds((64, COLS))), (VMEM, sds((64, 8), F32))]
    return call(combine_kernel, [VMEM] * 3 + [ANY], outs, us=3)(back, onehot, ids, later)


def block(ref, i):
    return ref.at[pl.ds(pl.multiple_of(i * COLS, COLS), COLS), :]


def column_block(ref, i):
    return ref.at[:, pl.ds(pl.multiple_of(i * COLS, COLS), COLS)]


def pack_kernel(*refs):
    weights, (columns, rows, w, d, sems) = refs[:6], refs[6:]
    loads, stores = [], []
    for j in range(6):
        buffer, out = (w.at[j], columns.at[:, pl.ds(HID * j, HID)]) if j < 4 else (d.at[j - 4], rows.at[pl.ds(HID * (j - 4), HID), :])
        loads.append(pltpu.make_async_copy(weights[j], buffer, sems.at[0, j]))
        stores.append(pltpu.make_async_copy(buffer, out, sems.at[1, j]))
    for copy in loads:
        copy.start()
    for load, store in zip(loads, stores):
        load.wait()
        store.start()
    for copy in stores:
        copy.wait()


def pack(*weights):
    scratch = [pltpu.VMEM((4, 8 * COLS, HID), BF), pltpu.VMEM((2, HID, 8 * COLS), BF), pltpu.SemaphoreType.DMA((2, 6))]
    outs = [(HBM, sds((8 * COLS, 4 * HID))), (HBM, sds((2 * HID, 8 * COLS)))]
    return call(pack_kernel, [HBM] * 6, outs, scratch, us=13, mib=MOST)(*weights)


def hidden_steps(ks, place, xs, ws, x, w, acc, sems):
    def copies(n, src):
        i = place[ks[0] + n]
        first = pltpu.make_async_copy(src, x.at[n], sems.at[1, n])
        return [first, pltpu.make_async_copy(block(ws, i), w.at[n], sems.at[0, n])]

    for n in range(len(ks)):
        for copy in copies(n, xs[n]):
            copy.start()

    @pl.loop(0, len(ks))
    def _(n):
        for copy in copies(n, xs[0]):
            copy.wait()
        acc[...] += nn(x[n], w[n])


def hidden_scratch(n):
    return [pltpu.VMEM((n, ROWS, COLS), BF), pltpu.VMEM((n, COLS, 4 * HID), BF), pltpu.SemaphoreType.DMA((2, n))]


def first_hidden_kernel(ks, place, *refs):
    n = len(ks)
    ws, acc, x, w, sems = refs[n:]
    acc[...] = jnp.zeros_like(acc)
    hidden_steps(ks, place, refs[:n], ws, x, w, acc, sems)


def first_hidden(ks, place, xs, ws):
    outs = [(VMEM, sds((ROWS, 4 * HID), F32))]
    kernel = functools.partial(first_hidden_kernel, ks)
    ins = [SMEM] + [HBM] * (len(ks) + 1)
    return call(kernel, ins, outs, hidden_scratch(len(ks)), us=8, mib=MOST)(place, *xs, ws)[0]


def raw_steps(ks, place, dys, ws, dy, w, acc, sems):
    def copies(n, src):
        i = place[ks[0] + n]
        first = pltpu.make_async_copy(src, dy.at[n], sems.at[1, n])
        return [first, pltpu.make_async_copy(column_block(ws, i), w.at[n], sems.at[0, n])]

    for n in range(len(ks)):
        for copy in copies(n, dys[n]):
            copy.start()

    @pl.loop(0, len(ks))
    def _(n):
        for copy in copies(n, dys[0]):
            copy.wait()
        acc[...] += nt(dy[n], w[n])


def raw_scratch(n):
    return [pltpu.VMEM((n, ROWS, COLS), BF), pltpu.VMEM((n, 2 * HID, COLS), BF), pltpu.SemaphoreType.DMA((2, n))]


def middle_kernel(place, x_last, d0, d1, d2, *refs):
    ws, ds, first, keep, send, raw, acc, x, w, sems, dy, v, dsems = refs
    acc[...] = first[...]
    hidden_steps(range(3, 4), place, [x_last], ws, x, w, acc, sems)
    keep[...] = acc[:, : 2 * HID]
    send[...] = acc[:, 2 * HID :]
    raw[...] = jnp.zeros_like(raw)
    raw_steps(range(3), place, [d0, d1, d2], ds, dy, v, raw, dsems)


def middle(place, x_last, dys, ws, ds, first):
    outs = [(VMEM, sds((ROWS, 2 * HID), F32))] * 3
    scratch = [pltpu.VMEM((ROWS, 4 * HID), F32)] + hidden_scratch(1) + raw_scratch(3)
    ins = [SMEM] + [HBM] * 6 + [VMEM]
    return call(middle_kernel, ins, outs, scratch, us=12, mib=MOST)(place, x_last, *dys, ws, ds, first)


def activation_kernel(keep, came, s_ref, slope_ref, h_ref):
    for lo in range(0, ROWS, 128):
        rows = pl.ds(lo, 128)
        ab = keep[rows, :] + came[rows, :]
        av, bv = ab[:, :HID], ab[:, HID:]
        sig = jax.nn.sigmoid(av)
        s = av * sig
        s_ref[rows, :] = s
        h_ref[rows, :] = s * bv
        slope_ref[rows, :] = bv * sig * (1.0 + av * (1.0 - sig))


def activation(keep, came):
    return call(activation_kernel, [VMEM] * 2, [(VMEM, sds((ROWS, HID), F32))] * 3)(keep, came)


def raw_kernel(ks, place, *refs):
    n = len(ks)
    ws, first, keep, send, acc, dy, w, sems = refs[n:]
    acc[...] = first[...]
    raw_steps(ks, place, refs[:n], ws, dy, w, acc, sems)
    keep[...] = acc[:, :HID]
    send[...] = acc[:, HID:]


def raw_rest(ks, place, dys, ws, first):
    outs = [(VMEM, sds((ROWS, HID), F32))] * 2
    scratch = [pltpu.VMEM((ROWS, 2 * HID), F32)] + raw_scratch(len(ks))
    ins = [SMEM] + [HBM] * (len(ks) + 1) + [VMEM]
    return call(functools.partial(raw_kernel, ks), ins, outs, scratch, us=3, mib=58)(place, *dys, ws, first)


def gradient_kernel(keep, came, s_ref, slope_ref, h_ref, gate, dab, hs):
    sums = []
    for i in range(ROWS // 128):
        rows = pl.ds(128 * i, 128)
        g, raw, h = gate[rows, 0:1].astype(F32), keep[rows, :] + came[rows, :], h_ref[rows, :]
        value = jnp.sum(h * raw, axis=1, keepdims=True)
        sums.append(jnp.broadcast_to(value, (128, 128)).T[0:1, :])
        dh = g * raw
        dab[rows, :HID] = (dh * slope_ref[rows, :]).astype(BF)
        dab[rows, HID:] = (dh * s_ref[rows, :]).astype(BF)
        hs[rows, :] = (g * h).astype(BF)
    tail = [jnp.concatenate(sums[:4], axis=1), jnp.concatenate([sums[4], jnp.zeros((1, 384), F32)], axis=1)]
    dab[ROWS:, :] = jnp.concatenate(tail + [jnp.zeros((TAIL - 2, 512), F32)], axis=0).astype(BF)


def gradients(keep, came, s, slope, h, gate):
    outs = [(VMEM, sds((ROWS + TAIL, 2 * HID))), (VMEM, sds((ROWS, HID)))]
    return call(gradient_kernel, [VMEM] * 6, outs)(keep, came, s, slope, h, gate)


def input_kernel(k, place, own, other, *refs):
    ws, (out, w, grads, sem) = refs[0], refs[-4:]
    copy = pltpu.make_async_copy(block(ws, place[k]), w, sem)
    copy.start()
    grads[:, : 2 * HID], grads[:, 2 * HID :] = own[:ROWS, :], other[:ROWS, :]
    tail = own[ROWS:, :].astype(F32) + other[ROWS:, :].astype(F32)
    row = jnp.concatenate([tail[0:1, :], tail[1:2, :384]], axis=1)
    out[ROWS:, :] = jnp.concatenate([row, jnp.zeros((TAIL - 1, COLS), F32)], axis=0).astype(BF)
    copy.wait()
    out[:ROWS, :] = nt(grads[...], w[...]).astype(BF)


def input_part(k, place, own, other, ws, *later):
    scratch = [pltpu.VMEM((COLS, 4 * HID), BF), pltpu.VMEM((ROWS, 4 * HID), BF), pltpu.SemaphoreType.DMA]
    outs = [(VMEM, sds((ROWS + TAIL, COLS)))]
    ins = [SMEM, VMEM, VMEM, HBM] + [ANY] * len(later)
    return call(functools.partial(input_kernel, k), ins, outs, scratch, us=4, mib=51)(place, own, other, ws, *later)[0]


def stream(refs, buffer, sems):
    def load(k, src):
        return pltpu.make_async_copy(src, buffer.at[k], sems.at[k])

    for k, ref in enumerate(refs):
        load(k, ref).start()
    return lambda k: load(k, refs[0]).wait()


def other_gradient_kernel(*refs):
    xs, dys, (dab, hs, _, columns, rows, x, dy, c, r, xsems, dsems, sems) = refs[:4], refs[4:8], refs[8:]
    x_ready, dy_ready = stream(xs, x, xsems), stream(dys, dy, dsems)

    def stores(k):
        return [
            pltpu.make_async_copy(c.at[k], columns.at[k], sems.at[0, k]),
            pltpu.make_async_copy(r.at[k], rows.at[k], sems.at[1, k]),
        ]

    hst = hs[...].T

    @pl.loop(0, 4)
    def _(k):
        x_ready(k)
        c[k] = tn(x[k], dab[:ROWS, :]).astype(BF)
        dy_ready(k)
        r[k] = nn(hst, dy[k]).astype(BF)
        for copy in stores(k):
            copy.start()

    @pl.loop(0, 4)
    def _(k):
        for copy in stores(k):
            copy.wait()


PIECES = [pltpu.VMEM((4, ROWS, COLS), BF)] * 2 + [pltpu.VMEM((4, COLS, 2 * HID), BF), pltpu.VMEM((4, HID, COLS), BF)]


def other_gradients(xs, dys, dab, hs, later):
    scratch = PIECES + [pltpu.SemaphoreType.DMA((4,))] * 2 + [pltpu.SemaphoreType.DMA((2, 4))]
    outs = [(HBM, sds((4, COLS, 2 * HID))), (HBM, sds((4, HID, COLS)))]
    ins = [HBM] * 8 + [VMEM] * 2 + [ANY]
    return call(other_gradient_kernel, ins, outs, scratch, us=10, mib=MOST)(*xs, *dys, dab, hs, later)


def own_gradient_kernel(place, other_place, *refs):
    xs, dys, refs = refs[:4], refs[4:8], refs[8:]
    dab, hs, columns, rows, _, g, u, d, token, x, dy, c, r, c_in, r_in, xsems, dsems, isems, sems = refs
    token[...] = jnp.zeros_like(token)
    x_ready, dy_ready = stream(xs, x, xsems), stream(dys, dy, dsems)

    def arrivals(k):
        return [
            pltpu.make_async_copy(columns.at[k], c_in.at[k], isems.at[0, k]),
            pltpu.make_async_copy(rows.at[k], r_in.at[k], isems.at[1, k]),
        ]

    def stores(i, k, cols, part, row):
        return [
            pltpu.make_async_copy(cols.at[k, :, pl.ds(0, HID)], block(g, i), sems.at[row, k]),
            pltpu.make_async_copy(cols.at[k, :, pl.ds(HID, HID)], block(u, i), sems.at[row + 1, k]),
            pltpu.make_async_copy(part.at[k], column_block(d, i), sems.at[row + 2, k]),
        ]

    for k in range(4):
        for copy in arrivals(k):
            copy.start()
    hst = hs[...].T

    @pl.loop(0, 4)
    def _(k):
        x_ready(k)
        c[k] = tn(x[k], dab[:ROWS, :]).astype(BF)
        dy_ready(k)
        r[k] = nn(hst, dy[k]).astype(BF)
        for copy in stores(place[k], k, c, r, 0):
            copy.start()
        for copy in arrivals(k):
            copy.wait()
        for copy in stores(other_place[k], k, c_in, r_in, 3):
            copy.start()

    @pl.loop(0, 4)
    def _(k):
        for copy in stores(place[k], k, c, r, 0) + stores(other_place[k], k, c_in, r_in, 3):
            copy.wait()


def own_gradients(place, other_place, xs, dys, dab, hs, columns, rows, later):
    scratch = PIECES + PIECES[2:] + [pltpu.SemaphoreType.DMA((4,))] * 2
    scratch += [pltpu.SemaphoreType.DMA((2, 4)), pltpu.SemaphoreType.DMA((6, 4))]
    outs = [(HBM, sds((8 * COLS, HID)))] * 2 + [(HBM, sds((HID, 8 * COLS))), (VMEM, sds((8, 128), F32))]
    ins = [SMEM] * 2 + [HBM] * 8 + [VMEM] * 2 + [HBM] * 2 + [ANY]
    kernel = call(own_gradient_kernel, ins, outs, scratch, us=12, mib=MOST)
    return kernel(place, other_place, *xs, *dys, dab, hs, columns, rows, later)


def total_kernel(expert, *refs):
    terms, out = refs[:3], refs[-1]
    lane = lax.broadcasted_iota(jnp.int32, (128, PAD), 1)
    gates = sum(term[ROWS:, :].astype(F32) for term in terms)
    for i in range(ROWS // 128):
        rows = pl.ds(128 * i, 128)
        out[rows, :COLS] = sum(term[rows, :].astype(F32) for term in terms).astype(BF)
        gate = jnp.broadcast_to(gates[0:1, 128 * i : 128 * i + 128], (128, 128)).T
        high = gate.astype(BF).astype(F32)
        spread = jnp.where(lane == expert[0], high, 0.0) + jnp.where(lane == expert[0] + 64, gate - high, 0.0)
        out[rows, COLS:] = spread.astype(BF)


def total(expert, terms, *later):
    outs = [(VMEM, sds((ROWS, COLS + PAD)))]
    ins = [SMEM] + [VMEM] * 3 + [ANY] * len(later)
    return call(total_kernel, ins, outs)(expert, *terms, *later)[0]


def after(v, *later):
    return pl.pallas_call(
        lambda *refs: None,
        in_specs=[HBM] + [ANY] * len(later),
        out_specs=HBM,
        out_shape=sds(v.shape, v.dtype),
        input_output_aliases={0: 0},
    )(v, *later)


def exchange(v):
    return lax.all_to_all(v.reshape(16, ROOM, -1), ("x", "z"), 0, 0, tiled=True).reshape(ROWS, -1)


def ring(v):
    return [v, meet(v, 0), meet(v, 1)]


def add(*terms):
    return sum(term.astype(F32) for term in terms).astype(BF)


def local(tokens, cotangent, ids, gates, wg, wu, wd):
    core, iy = lax.axis_index("core"), lax.axis_index("y")
    expert = (lax.axis_index("x") * 4 + lax.axis_index("z")).astype(jnp.int32).reshape(1)
    ys = [iy, jnp.where(core == 0, iy ^ 1, 3 - iy), jnp.where(core == 0, 3 - iy, iy ^ 1), (iy + 2) % 4]
    place = jnp.stack([2 * y + core for y in ys]).astype(jnp.int32)
    other_place = jnp.stack([2 * ys[k] + 1 - core for k in (0, 2, 1, 3)]).astype(jnp.int32)
    wg, wu, wd = wg[0], wu[0], wd[0]

    send_x, send_dy, onehot = dispatch(ids.T, gates.T.astype(F32), tokens, cotangent)
    ws = (wg, wu, swap(wg), swap(wu))
    ds = (wd, swap(wd))
    xs = ring(after(exchange(send_x), ws[2], ws[3], ds[1]))
    x_last = meet(xs[1], 1)
    came = exchange(after(send_dy, xs[0]))
    gate = came[:, COLS:]
    dys = ring(came[:, :COLS])
    dys[1] = after(dys[1], dys[2])
    dy_last = meet(dys[1], 1)

    ws, ds = pack(*ws, *ds)
    first = first_hidden(range(3), place, xs, ws)
    keep, send, raw = middle(place, x_last, dys, ws, ds, first)
    s, slope, h = activation(keep, swap(send))
    keep, send = raw_rest(range(3, 4), place, [dy_last], ds, raw)
    dab, hs = gradients(keep, swap(send), s, slope, h, gate)
    dab_other, hs_other = swap(dab), swap(hs)

    def part(k, *later):
        return input_part(k, place, dab, dab_other, ws, *later)

    opposite = part(3)
    near = part(2, opposite)
    own = part(1, near)
    opposite, near = meet(opposite, 1), meet(near, 1)
    own = add(own, opposite)
    rest = meet(own, 0)
    xs, dys = xs + [x_last], dys + [dy_last]
    columns, rows = other_gradients(xs, dys, dab_other, hs_other, own)
    columns, rows = swap(columns), swap(rows)
    share = total(expert, (part(0, own), near, rest))
    gate_grad, up_grad, down_grad, done = own_gradients(place, other_place, xs, dys, dab, hs, columns, rows, share)
    input_grad, slot_grad = combine(exchange(share), onehot, ids, done)
    return input_grad, slot_grad, gate_grad[None], up_grad[None], down_grad[None]


def solution(mesh):
    torus = Mesh(mesh.devices.reshape(4, 4, 4, 2), ("x", "z", "y", "core"))
    ep, etp = ("x", "z"), ("y", "core")
    in_specs = (
        P(ep, etp),
        P(ep, etp),
        P(ep, None),
        P(ep, None),
        P(ep, None, etp),
        P(ep, None, etp),
        P(ep, etp, None),
    )
    out_specs = (P(ep, etp), P(ep, None), P(ep, None, etp), P(ep, None, etp), P(ep, etp, None))
    return jax.shard_map(local, mesh=torus, in_specs=in_specs, out_specs=out_specs, check_vma=False)
```

time: 231 us -> 215 us (0.931)
  blocking collectives: 26 us -> 0 us
  Pallas kernels: 60.2 us -> 84.5 us
  local copies, waits for them, and re-layouts: 22.2 us -> 9.38 us
  waiting for transfers between devices: 88.5 us -> 80.9 us
  starting transfers between devices: 26.6 us -> 31.7 us
    all_to_all x1 -> x0, blocking collectives: 26 us -> none  [exchange(): lax.all_to_all(v.reshape(16, ROOM, -1), ('x', 'z'), 0, 0, tiled=True)]
    pallas_call x13 -> x15, Pallas kernels: 60.2 us -> 84.5 us  [the longest x4 16.4 us: input_part(): call(functools.partial(input_kernel, k), ins, outs, scratch, us=4, mib=51)]
    ppermute x9, waiting for transfers between devices: 66.4 us -> 50.1 us  [meet(): return lax.ppermute(v, ('y', 'core'), MEET[step])]
    unnamed x70 -> x30, local copies, waits for them, and re-layouts: 20.9 us -> 5.98 us
    all_to_all x2 -> x3, waiting for transfers between devices: 22.1 us -> 27.9 us  [exchange(): lax.all_to_all(v.reshape(16, ROOM, -1), ('x', 'z'), 0, 0, tiled=True)]
    all_to_all x2 -> x3, starting transfers between devices: 11.1 us -> 16.7 us  [exchange(): lax.all_to_all(v.reshape(16, ROOM, -1), ('x', 'z'), 0, 0, tiled=True)]
    ppermute x12 -> x9, waiting for transfers between devices: 0.03 us -> 2.89 us  [swap(): return lax.ppermute(v, 'core', SWAP)]
    slice x1, local copies, waits for them, and re-layouts: 0.09 us -> 2.47 us  [local(): dys = ring(came[:, :COLS])]
  transfers between devices with their start and end apart: 23 -> 21, of which waited for: 8 -> 10; matrix products, arithmetic and copies ran while one was open for 2% -> 4% of each run, Pallas kernels for 21% -> 38%
where the time goes in v3:
time: 215 us; the launch traced here: 212 us
  Pallas kernels  84.5 us (39%)
  waiting for transfers between devices  80.9 us (38%)
  starting transfers between devices  31.7 us (15%)
  local copies, waits for them, and re-layouts  9.38 us (4%)
  other arithmetic  4.5 us (2%)
    ppermute x9, waiting for transfers between devices, meet(): return lax.ppermute(v, ('y', 'core'), MEET[step])  50.1 us
    all_to_all x3, waiting for transfers between devices, exchange(): lax.all_to_all(v.reshape(16, ROOM, -1), ('x', 'z'), 0, 0, tiled=True)  27.9 us
    all_to_all x3, starting transfers between devices, exchange(): lax.all_to_all(v.reshape(16, ROOM, -1), ('x', 'z'), 0, 0, tiled=True)  16.7 us
    pallas_call x4, Pallas kernels, input_part(): call(functools.partial(input_kernel, k), ins, outs, scratch, us=4, mib=51)  16.4 us
    pallas_call x1, Pallas kernels, pack(): call(pack_kernel, [HBM] * 6, outs, scratch, us=13, mib=MOST)(*weights)  14.7 us
    ppermute x9, starting transfers between devices, meet(): return lax.ppermute(v, ('y', 'core'), MEET[step])  13 us
    pallas_call x1, Pallas kernels, own_gradients(): return kernel(place, other_place, *xs, *dys, dab, hs, columns, rows, later)  12 us
    pallas_call x1, Pallas kernels, other_gradients(): call(other_gradient_kernel, ins, outs, scratch, us=10, mib=MOST)  9.32 us
  transfers between devices with their start and end apart: 21, of which 10 were waited for; matrix products, arithmetic and copies ran while one was open for 4% of the time, Pallas kernels for 38%

profile of v3, /device:TPU:0, one launch (start us, length us, event | category | flops | bytes accessed | tf_op | source)
XLA Modules:
  0.0 211.9 jit_solution(4859567683129590543)
XLA Ops:
  4.5 2.1 shard_map.110
  7.6 8.0 %all-to-all-start = ((bf16[16,40,896]{2,1,0:T(8,128)(2,1)}), bf16[16,40,896]{2,1,0:T(8,128)(2,1)S(1)}, u32[]{:S(2)}, u32[]{:S(2)}) async-start(bf16[16,40,896]{2,1,0:T(8,128)(2,1)} %bitcast.7), calls=%async_computation | async-start | bytes 2293760 | tf_op jit(solution)/shard_map/all_to_all | solution.py:421
  16.3 18.8 %all-to-all-done = bf16[16,40,896]{2,1,0:T(8,128)(2,1)S(1)} async-done(((bf16[16,40,896]{2,1,0:T(8,128)(2,1)}), bf16[16,40,896]{2,1,0:T(8,128)(2,1)S(1)}, u32[]{:S(2)}, u32[]{:S(2)}) %all-to-all-start) | async-done | bytes 1146912 | tf_op jit(solution)/shard_map/all_to_all | solution.py:421
  36.1 1.6 collective-permute-start.6
  37.7 2.2 %collective-permute-start.8 = (bf16[640,896]{1,0:T(8,128)(2,1)}, bf16[640,896]{1,0:T(8,128)(2,1)}, u32[]{:S(2)}, u32[]{:S(2)}) collective-permute-start(bf16[640,896]{1,0:T(8,128)(2,1)} %shard_map.111.refs_1_.refs_0_), channel_id=1, source_target_pairs={{0,6},{1,3},{2,4},{3,1},{4,2},{5,7},{6,0},{7,5},{8,14},{9,11},{10,... | collective-permute-start | bytes 3440648 | tf_op jit(solution)/shard_map/ppermute | solution.py:31
  39.9 4.4 %all-to-all-start.1 = ((bf16[16,40,1024]{2,1,0:T(8,128)(2,1)}), bf16[16,40,1024]{2,1,0:T(8,128)(2,1)}, u32[]{:S(2)}, u32[]{:S(2)}) async-start(bf16[16,40,1024]{2,1,0:T(8,128)(2,1)} %bitcast.24), calls=%async_computation.1 | async-start | bytes 2621440 | tf_op jit(solution)/shard_map/all_to_all | solution.py:421
  44.3 14.7 %shard_map.114 = (bf16[7168,1024]{1,0:T(8,128)(2,1)}, bf16[512,7168]{1,0:T(8,128)(2,1)}) custom-call(bf16[7168,256]{1,0:T(8,128)(2,1)} %bitcast.28, bf16[7168,256]{1,0:T(8,128)(2,1)} %bitcast.30, bf16[7168,256]{1,0:T(8,128)(2,1)} %collective-permute-done.refs_1_.refs_2_, bf16[7168,256]{1,0:T(8,128)(2,1)} %collective-permute-done.1.refs_2_.refs_3_, ...), custom_call_target="tpu_custom_call" | custom-call | flops 389999984640 | bytes 10000 | tf_op jit(solution)/shard_map/pallas_call | solution.py:146
  58.9 5.4 %collective-permute-done.6.refs_1_ = bf16[640,896]{1,0:T(8,128)(2,1)} collective-permute-done((bf16[640,896]{1,0:T(8,128)(2,1)}, bf16[640,896]{1,0:T(8,128)(2,1)}, u32[]{:S(2)}, u32[]{:S(2)}) %collective-permute-start.6) | collective-permute-done | bytes 1146912 | tf_op jit(solution)/shard_map/ppermute | solution.py:31
  65.2 2.5 %slice.8.d0.refs_4_ = bf16[640,896]{1,0:T(8,128)(2,1)} slice(bf16[640,1024]{1,0:T(8,128)(2,1)} %bitcast.13), slice={[0:640], [0:896]} | slice | bytes 2293760 | tf_op jit(solution)/shard_map/slice | solution.py:447
  67.7 2.3 %collective-permute-start.4 = (bf16[640,896]{1,0:T(8,128)(2,1)}, bf16[640,896]{1,0:T(8,128)(2,1)}, u32[]{:S(2)}, u32[]{:S(2)}) collective-permute-start(bf16[640,896]{1,0:T(8,128)(2,1)} %slice.8.d0.refs_4_), channel_id=1, source_target_pairs={{0,6},{1,3},{2,4},{3,1},{4,2},{5,7},{6,0},{7,5},{8,14},{9,11},{10,... | collective-permute-start | bytes 3440648 | tf_op jit(solution)/shard_map/ppermute | solution.py:31
  70.6 8.6 %shard_map.115.refs_2_ = f32[640,1024]{1,0:T(8,128)} custom-call(s32[4]{0:T(128)} %pad_add_fusion.place, bf16[640,896]{1,0:T(8,128)(2,1)} %shard_map.111.refs_1_.refs_0_, bf16[640,896]{1,0:T(8,128)(2,1)} %collective-permute-done.6.refs_1_, bf16[640,896]{1,0:T(8,128)(2,1)} %collective-permute-done.8.refs_2_, bf16[7168,1024]{1,0:T(8,128)(2,1)} %get-tuple-element.31.refs_3_.refs_0_), custom_call_target="tpu_custom_call" | custom-call | flops 240000008192 | bytes 10000 | tf_op jit(solution)/shard_map/pallas_call | solution.py:181
  80.2 25.1 %collective-permute-done.4.refs_1_.d2.refs_6_ = bf16[640,896]{1,0:T(8,128)(2,1)} collective-permute-done((bf16[640,896]{1,0:T(8,128)(2,1)}, bf16[640,896]{1,0:T(8,128)(2,1)}, u32[]{:S(2)}, u32[]{:S(2)}) %collective-permute-start.4) | collective-permute-done | bytes 1146912 | tf_op jit(solution)/shard_map/ppermute | solution.py:31
  105.4 1.8 collective-permute-start.5
  107.2 9.0 %shard_map.116 = (f32[640,512]{1,0:T(8,128)}, f32[640,512]{1,0:T(8,128)}, f32[640,512]{1,0:T(8,128)}) custom-call(s32[4]{0:T(128)} %pad_add_fusion.place, bf16[640,896]{1,0:T(8,128)(2,1)} %collective-permute-done.7.x_last.refs_3_, bf16[640,896]{1,0:T(8,128)(2,1)} %slice.8.d0.refs_4_, bf16[640,896]{1,0:T(8,128)(2,1)} %shard_map.113.d1.refs_5_, ...), custom_call_target="tpu_custom_call" | custom-call | flops 359999995904 | bytes 10000 | tf_op jit(solution)/shard_map/pallas_call | solution.py:219
  116.3 6.4 %collective-permute-done.5.refs_0_.refs_7_ = bf16[640,896]{1,0:T(8,128)(2,1)} collective-permute-done((bf16[640,896]{1,0:T(8,128)(2,1)}, bf16[640,896]{1,0:T(8,128)(2,1)}, u32[]{:S(2)}, u32[]{:S(2)}) %collective-permute-start.5) | collective-permute-done | bytes 1146912 | tf_op jit(solution)/shard_map/ppermute | solution.py:31
  122.7 4.9 %shard_map.117 = (f32[640,256]{1,0:T(8,128)}, f32[640,256]{1,0:T(8,128)}) custom-call(s32[4]{0:T(128)} %pad_add_fusion.place, bf16[640,896]{1,0:T(8,128)(2,1)} %collective-permute-done.5.refs_0_.refs_7_, bf16[512,7168]{1,0:T(8,128)(2,1)} %get-tuple-element.30.refs_1_, f32[640,512]{1,0:T(8,128)} %get-tuple-element.32.refs_2_), custom_call_target="tpu_custom_call" | custom-call | flops 89999998976 | bytes 10000 | tf_op jit(solution)/shard_map/pallas_call | solution.py:251
  128.1 1.9 collective-permute-done.9.came
  133.3 4.6 %shard_map.120.refs_1_ = bf16[656,896]{1,0:T(8,128)(2,1)} custom-call(s32[4]{0:T(128)S(1)} %copy-done.3, bf16[656,512]{1,0:T(8,128)(2,1)S(1)} %get-tuple-element.40.own.refs_8_, bf16[656,512]{1,0:T(8,128)(2,1)S(1)} %collective-permute-done.11.other.refs_8_, bf16[7168,1024]{1,0:T(8,128)(2,1)} %get-tuple-element.31.refs_3_.refs_0_), custom_call_target="tpu_custom_call" | custom-call | flops 120000004096 | bytes 10000 | tf_op jit(solution)/shard_map/pallas_call | solution.py:290
  137.9 2.1 collective-permute-start.12
  140.0 4.6 %shard_map.121.refs_1_ = bf16[656,896]{1,0:T(8,128)(2,1)} custom-call(s32[4]{0:T(128)S(1)} %copy-done.3, bf16[656,512]{1,0:T(8,128)(2,1)S(1)} %get-tuple-element.40.own.refs_8_, bf16[656,512]{1,0:T(8,128)(2,1)S(1)} %collective-permute-done.11.other.refs_8_, bf16[7168,1024]{1,0:T(8,128)(2,1)} %get-tuple-element.31.refs_3_.refs_0_, ...), custom_call_target="tpu_custom_call" | custom-call | flops 120000004096 | bytes 10000 | tf_op jit(solution)/shard_map/pallas_call | solution.py:290
  146.1 3.6 %shard_map.122 = bf16[656,896]{1,0:T(8,128)(2,1)S(1)} custom-call(s32[4]{0:T(128)S(1)} %copy-done.3, bf16[656,512]{1,0:T(8,128)(2,1)S(1)} %get-tuple-element.40.own.refs_8_, bf16[656,512]{1,0:T(8,128)(2,1)S(1)} %collective-permute-done.11.other.refs_8_, bf16[7168,1024]{1,0:T(8,128)(2,1)} %get-tuple-element.31.refs_3_.refs_0_, ...), custom_call_target="tpu_custom_call" | custom-call | flops 120000004096 | bytes 10000 | tf_op jit(solution)/shard_map/pallas_call | solution.py:290
  149.8 6.1 %collective-permute-done.12 = bf16[656,896]{1,0:T(8,128)(2,1)} collective-permute-done((bf16[656,896]{1,0:T(8,128)(2,1)}, bf16[656,896]{1,0:T(8,128)(2,1)}, u32[]{:S(2)}, u32[]{:S(2)}) %collective-permute-start.12) | collective-permute-done | bytes 1175584 | tf_op jit(solution)/shard_map/ppermute | solution.py:31
  155.9 2.6 %add_convert_fusion.refs_1_.refs_10_ = bf16[656,896]{1,0:T(8,128)(2,1)} fusion(bf16[656,896]{1,0:T(8,128)(2,1)} %collective-permute-done.12, bf16[656,896]{1,0:T(8,128)(2,1)S(1)} %shard_map.122), kind=kLoop, calls=%fused_computation | loop fusion | flops 2351104 | bytes 3526656 | tf_op jit(solution)/shard_map/convert_element_type | solution.py:429
  158.5 9.3 %shard_map.125 = (bf16[4,896,512]{2,1,0:T(8,128)(2,1)}, bf16[4,256,896]{2,1,0:T(8,128)(2,1)}) custom-call(bf16[640,896]{1,0:T(8,128)(2,1)} %shard_map.111.refs_1_.refs_0_, bf16[640,896]{1,0:T(8,128)(2,1)} %collective-permute-done.6.refs_1_, bf16[640,896]{1,0:T(8,128)(2,1)} %collective-permute-done.8.refs_2_, ...), custom_call_target="tpu_custom_call" | custom-call | flops 299999985664 | bytes 10000 | tf_op jit(solution)/shard_map/pallas_call | solution.py:336
  168.4 3.6 %shard_map.123.refs_0_ = bf16[656,896]{1,0:T(8,128)(2,1)S(1)} custom-call(s32[4]{0:T(128)S(1)} %copy-done.4, bf16[656,512]{1,0:T(8,128)(2,1)S(1)} %get-tuple-element.40.own.refs_8_, bf16[656,512]{1,0:T(8,128)(2,1)S(1)} %copy-done.7, bf16[7168,1024]{1,0:T(8,128)(2,1)} %get-tuple-element.31.refs_3_.refs_0_, bf16[656,896]{1,0:T(8,128)(2,1)} %add_convert_fusion.refs_1_.refs_10_), custom_call_target="tpu_custom_call" | custom-call | flops 120000004096 | bytes 10000 | tf_op jit(solution)/shard_map/pallas_call | solution.py:290
  172.0 4.2 %collective-permute-done.13.refs_1_ = bf16[656,896]{1,0:T(8,128)(2,1)} collective-permute-done((bf16[656,896]{1,0:T(8,128)(2,1)}, bf16[656,896]{1,0:T(8,128)(2,1)}, u32[]{:S(2)}, u32[]{:S(2)}) %collective-permute-start.13) | collective-permute-done | bytes 1175584 | tf_op jit(solution)/shard_map/ppermute | solution.py:31
  176.2 2.8 %collective-permute-done.14.refs_2_ = bf16[656,896]{1,0:T(8,128)(2,1)} collective-permute-done((bf16[656,896]{1,0:T(8,128)(2,1)}, bf16[656,896]{1,0:T(8,128)(2,1)}, u32[]{:S(2)}, u32[]{:S(2)}) %collective-permute-start.14) | collective-permute-done | bytes 1175584 | tf_op jit(solution)/shard_map/ppermute | solution.py:31
  179.0 3.6 %shard_map.124.refs_12_ = bf16[640,1024]{1,0:T(8,128)(2,1)} custom-call(s32[1]{0:T(128)} %bitcast.expert, bf16[656,896]{1,0:T(8,128)(2,1)S(1)} %shard_map.123.refs_0_, bf16[656,896]{1,0:T(8,128)(2,1)} %collective-permute-done.13.refs_1_, bf16[656,896]{1,0:T(8,128)(2,1)} %collective-permute-done.14.refs_2_), custom_call_target="tpu_custom_call" | custom-call | flops 30000001024 | bytes 10000 | tf_op jit(solution)/shard_map/pallas_call | solution.py:407
  182.6 4.4 %all-to-all-start.2 = ((bf16[16,40,1024]{2,1,0:T(8,128)(2,1)}), bf16[16,40,1024]{2,1,0:T(8,128)(2,1)}, u32[]{:S(2)}, u32[]{:S(2)}) async-start(bf16[16,40,1024]{2,1,0:T(8,128)(2,1)} %bitcast.14), calls=%async_computation.2 | async-start | bytes 2621440 | tf_op jit(solution)/shard_map/all_to_all | solution.py:421
  187.0 12.0 %shard_map.126 = (bf16[7168,256]{1,0:T(8,128)(2,1)}, bf16[7168,256]{1,0:T(8,128)(2,1)}, bf16[256,7168]{1,0:T(8,128)(2,1)}, f32[8,128]{1,0:T(8,128)}) custom-call(s32[4]{0:T(128)} %pad_add_fusion.place, s32[4]{0:T(128)} %pad_add_fusion.1.other_place, bf16[640,896]{1,0:T(8,128)(2,1)} %shard_map.111.refs_1_.refs_0_, ...), custom_call_target="tpu_custom_call" | custom-call | flops 359999995904 | bytes 10000 | tf_op jit(solution)/shard_map/pallas_call | solution.py:388
  199.0 9.1 %all-to-all-done.2 = bf16[16,40,1024]{2,1,0:T(8,128)(2,1)} async-done(((bf16[16,40,1024]{2,1,0:T(8,128)(2,1)}), bf16[16,40,1024]{2,1,0:T(8,128)(2,1)}, u32[]{:S(2)}, u32[]{:S(2)}) %all-to-all-start.2) | async-done | bytes 1310752 | tf_op jit(solution)/shard_map/all_to_all | solution.py:421
  208.8 2.5 %shard_map.127 = (bf16[64,896]{1,0:T(8,128)(2,1)}, f32[64,8]{1,0:T(8,128)S(1)}) custom-call(bf16[640,1024]{1,0:T(8,128)(2,1)} %bitcast.15.back, bf16[640,64]{1,0:T(8,128)(2,1)S(1)} %get-tuple-element.41.onehot, s32[64,8]{1,0:T(8,128)S(1)} %copy.15.ids, f32[8,128]{1,0:T(8,128)S(1)} %copy-done.12), custom_call_target="tpu_custom_call" | custom-call | flops 89999998976 | bytes 10000 | tf_op jit(solution)/shard_map/pallas_call | solution.py:116
  (64 shorter events, 16.2 us)
Async XLA Ops:
  0.6 34.5 %collective-permute-start = (bf16[7168,256]{1,0:T(8,128)(2,1)}, bf16[7168,256]{1,0:T(8,128)(2,1)}, u32[]{:S(2)}, u32[]{:S(2)}) collective-permute-start(bf16[7168,256]{1,0:T(8,128)(2,1)} %bitcast.27), channel_id=1, source_target_pairs={{0,1},{1,0},{2,3},{3,2},{4,5},{5,4},{6,7},{7,6},{8,9},{9,8},{10,11... | collective-permute-start | bytes 11010056 | tf_op jit(solution)/shard_map/ppermute | solution.py:35
  0.7 34.4 %collective-permute-start.1 = (bf16[7168,256]{1,0:T(8,128)(2,1)}, bf16[7168,256]{1,0:T(8,128)(2,1)}, u32[]{:S(2)}, u32[]{:S(2)}) collective-permute-start(bf16[7168,256]{1,0:T(8,128)(2,1)} %bitcast.29), channel_id=1, source_target_pairs={{0,1},{1,0},{2,3},{3,2},{4,5},{5,4},{6,7},{7,6},{8,9},{9,8},{10,11... | collective-permute-start | bytes 11010056 | tf_op jit(solution)/shard_map/ppermute | solution.py:35
  1.2 33.9 %collective-permute-start.2 = (bf16[256,7168]{1,0:T(8,128)(2,1)}, bf16[256,7168]{1,0:T(8,128)(2,1)}, u32[]{:S(2)}, u32[]{:S(2)}) collective-permute-start(bf16[256,7168]{1,0:T(8,128)(2,1)} %bitcast.31), channel_id=1, source_target_pairs={{0,1},{1,0},{2,3},{3,2},{4,5},{5,4},{6,7},{7,6},{8,9},{9,8},{10,11... | collective-permute-start | bytes 11010056 | tf_op jit(solution)/shard_map/ppermute | solution.py:35
  2.7 0.9 copy-start.8
  6.6 1.1 copy-start
  7.6 27.5 %all-to-all-start = ((bf16[16,40,896]{2,1,0:T(8,128)(2,1)}), bf16[16,40,896]{2,1,0:T(8,128)(2,1)S(1)}, u32[]{:S(2)}, u32[]{:S(2)}) async-start(bf16[16,40,896]{2,1,0:T(8,128)(2,1)} %bitcast.7), calls=%async_computation | async-start | bytes 2293760 | tf_op jit(solution)/shard_map/all_to_all | solution.py:421
  35.1 1.0 copy-start.13
  36.1 28.2 %collective-permute-start.6 = (bf16[640,896]{1,0:T(8,128)(2,1)}, bf16[640,896]{1,0:T(8,128)(2,1)}, u32[]{:S(2)}, u32[]{:S(2)}) collective-permute-start(bf16[640,896]{1,0:T(8,128)(2,1)} %shard_map.111.refs_1_.refs_0_), channel_id=1, source_target_pairs={{0,2},{1,7},{2,0},{3,5},{4,6},{5,3},{6,4},{7,1},{8,10},{9,15},{10,... | collective-permute-start | bytes 3440648 | tf_op jit(solution)/shard_map/ppermute | solution.py:31
  37.7 32.9 %collective-permute-start.8 = (bf16[640,896]{1,0:T(8,128)(2,1)}, bf16[640,896]{1,0:T(8,128)(2,1)}, u32[]{:S(2)}, u32[]{:S(2)}) collective-permute-start(bf16[640,896]{1,0:T(8,128)(2,1)} %shard_map.111.refs_1_.refs_0_), channel_id=1, source_target_pairs={{0,6},{1,3},{2,4},{3,1},{4,2},{5,7},{6,0},{7,5},{8,14},{9,11},{10,... | collective-permute-start | bytes 3440648 | tf_op jit(solution)/shard_map/ppermute | solution.py:31
  39.9 25.3 %all-to-all-start.1 = ((bf16[16,40,1024]{2,1,0:T(8,128)(2,1)}), bf16[16,40,1024]{2,1,0:T(8,128)(2,1)}, u32[]{:S(2)}, u32[]{:S(2)}) async-start(bf16[16,40,1024]{2,1,0:T(8,128)(2,1)} %bitcast.24), calls=%async_computation.1 | async-start | bytes 2621440 | tf_op jit(solution)/shard_map/all_to_all | solution.py:421
  64.3 42.9 %collective-permute-start.7 = (bf16[640,896]{1,0:T(8,128)(2,1)}, bf16[640,896]{1,0:T(8,128)(2,1)}, u32[]{:S(2)}, u32[]{:S(2)}) collective-permute-start(bf16[640,896]{1,0:T(8,128)(2,1)} %collective-permute-done.6.refs_1_), channel_id=1, source_target_pairs={{0,6},{1,3},{2,4},{3,1},{4,2},{5,7},{6,0},{7,5},{8,14},{9,11},{10,... | collective-permute-start | bytes 3440648 | tf_op jit(solution)/shard_map/ppermute | solution.py:31
  67.7 37.7 %collective-permute-start.4 = (bf16[640,896]{1,0:T(8,128)(2,1)}, bf16[640,896]{1,0:T(8,128)(2,1)}, u32[]{:S(2)}, u32[]{:S(2)}) collective-permute-start(bf16[640,896]{1,0:T(8,128)(2,1)} %slice.8.d0.refs_4_), channel_id=1, source_target_pairs={{0,6},{1,3},{2,4},{3,1},{4,2},{5,7},{6,0},{7,5},{8,14},{9,11},{10,... | collective-permute-start | bytes 3440648 | tf_op jit(solution)/shard_map/ppermute | solution.py:31
  70.0 35.3 %collective-permute-start.3 = (bf16[640,896]{1,0:T(8,128)(2,1)}, bf16[640,896]{1,0:T(8,128)(2,1)}, u32[]{:S(2)}, u32[]{:S(2)}) collective-permute-start(bf16[640,896]{1,0:T(8,128)(2,1)} %slice.8.d0.refs_4_), channel_id=1, source_target_pairs={{0,2},{1,7},{2,0},{3,5},{4,6},{5,3},{6,4},{7,1},{8,10},{9,15},{10,... | collective-permute-start | bytes 3440648 | tf_op jit(solution)/shard_map/ppermute | solution.py:31
  105.4 17.4 %collective-permute-start.5 = (bf16[640,896]{1,0:T(8,128)(2,1)}, bf16[640,896]{1,0:T(8,128)(2,1)}, u32[]{:S(2)}, u32[]{:S(2)}) collective-permute-start(bf16[640,896]{1,0:T(8,128)(2,1)} %shard_map.113.d1.refs_5_), channel_id=1, source_target_pairs={{0,6},{1,3},{2,4},{3,1},{4,2},{5,7},{6,0},{7,5},{8,14},{9,11},{10,... | collective-permute-start | bytes 3440648 | tf_op jit(solution)/shard_map/ppermute | solution.py:31
  116.2 11.5 %collective-permute-start.10 = (f32[640,512]{1,0:T(8,128)}, f32[640,512]{1,0:T(8,128)S(1)}, u32[]{:S(2)}, u32[]{:S(2)}) collective-permute-start(f32[640,512]{1,0:T(8,128)} %get-tuple-element.36), channel_id=1, source_target_pairs={{0,1},{1,0},{2,3},{3,2},{4,5},{5,4},{6,7},{7,6},{8,9},{9,8},{10,11... | collective-permute-start | bytes 3932168 | tf_op jit(solution)/shard_map/ppermute | solution.py:35
  122.7 5.0 %copy-start.10 = (f32[640,512]{1,0:T(8,128)S(1)}, f32[640,512]{1,0:T(8,128)}, u32[]{:S(2)}) copy-start(f32[640,512]{1,0:T(8,128)} %get-tuple-element.35.keep) | copy-start | bytes 3932164
  127.7 2.4 %collective-permute-start.9 = (f32[640,256]{1,0:T(8,128)}, f32[640,256]{1,0:T(8,128)S(1)}, u32[]{:S(2)}, u32[]{:S(2)}) collective-permute-start(f32[640,256]{1,0:T(8,128)} %get-tuple-element.34), channel_id=1, source_target_pairs={{0,1},{1,0},{2,3},{3,2},{4,5},{5,4},{6,7},{7,6},{8,9},{9,8},{10,11... | collective-permute-start | bytes 1966088 | tf_op jit(solution)/shard_map/ppermute | solution.py:35
  127.8 2.3 %copy-start.11 = (f32[640,256]{1,0:T(8,128)S(1)}, f32[640,256]{1,0:T(8,128)}, u32[]{:S(2)}) copy-start(f32[640,256]{1,0:T(8,128)} %get-tuple-element.33.keep) | copy-start | bytes 1966084
  130.0 1.3 copy-start.2
  130.0 3.3 %copy-start.3 = (s32[4]{0:T(128)S(1)}, s32[4]{0:T(128)}, u32[]{:S(2)}) copy-start(s32[4]{0:T(128)} %pad_add_fusion.place) | copy-start | bytes 52
  131.2 37.2 %copy-start.5 = (bf16[656,512]{1,0:T(8,128)(2,1)}, bf16[656,512]{1,0:T(8,128)(2,1)S(1)}, u32[]{:S(2)}) copy-start(bf16[656,512]{1,0:T(8,128)(2,1)S(1)} %get-tuple-element.40.own.refs_8_) | copy-start | bytes 2015236
  131.2 2.1 %collective-permute-start.11 = (bf16[656,512]{1,0:T(8,128)(2,1)S(1)}, bf16[656,512]{1,0:T(8,128)(2,1)S(1)}, u32[]{:S(2)}, u32[]{:S(2)}) collective-permute-start(bf16[656,512]{1,0:T(8,128)(2,1)S(1)} %get-tuple-element.40.own.refs_8_), channel_id=1, source_target_pairs={{0,1},{1,0},{2,3},{3,2},{4,5},{5,4},{6,7},{7,6},{8,9},{9,8},{10,11... | collective-permute-start | bytes 2015240 | tf_op jit(solution)/shard_map/ppermute | solution.py:35
  132.0 26.5 %collective-permute-start.15 = (bf16[640,256]{1,0:T(8,128)(2,1)}, bf16[640,256]{1,0:T(8,128)(2,1)}, u32[]{:S(2)}, u32[]{:S(2)}) collective-permute-start(bf16[640,256]{1,0:T(8,128)(2,1)} %get-tuple-element.42.refs_9_), channel_id=1, source_target_pairs={{0,1},{1,0},{2,3},{3,2},{4,5},{5,4},{6,7},{7,6},{8,9},{9,8},{10,11... | collective-permute-start | bytes 983048 | tf_op jit(solution)/shard_map/ppermute | solution.py:35
  133.3 12.8 %copy-start.6 = (bf16[656,512]{1,0:T(8,128)(2,1)}, bf16[656,512]{1,0:T(8,128)(2,1)S(1)}, u32[]{:S(2)}) copy-start(bf16[656,512]{1,0:T(8,128)(2,1)S(1)} %collective-permute-done.11.other.refs_8_) | copy-start | bytes 2015236
  137.9 17.9 %collective-permute-start.12 = (bf16[656,896]{1,0:T(8,128)(2,1)}, bf16[656,896]{1,0:T(8,128)(2,1)}, u32[]{:S(2)}, u32[]{:S(2)}) collective-permute-start(bf16[656,896]{1,0:T(8,128)(2,1)} %shard_map.120.refs_1_), channel_id=1, source_target_pairs={{0,6},{1,3},{2,4},{3,1},{4,2},{5,7},{6,0},{7,5},{8,14},{9,11},{10,... | collective-permute-start | bytes 3526664 | tf_op jit(solution)/shard_map/ppermute | solution.py:31
  144.6 31.6 %collective-permute-start.13 = (bf16[656,896]{1,0:T(8,128)(2,1)}, bf16[656,896]{1,0:T(8,128)(2,1)}, u32[]{:S(2)}, u32[]{:S(2)}) collective-permute-start(bf16[656,896]{1,0:T(8,128)(2,1)} %shard_map.121.refs_1_), channel_id=1, source_target_pairs={{0,6},{1,3},{2,4},{3,1},{4,2},{5,7},{6,0},{7,5},{8,14},{9,11},{10,... | collective-permute-start | bytes 3526664 | tf_op jit(solution)/shard_map/ppermute | solution.py:31
  158.5 20.6 %collective-permute-start.14 = (bf16[656,896]{1,0:T(8,128)(2,1)}, bf16[656,896]{1,0:T(8,128)(2,1)}, u32[]{:S(2)}, u32[]{:S(2)}) collective-permute-start(bf16[656,896]{1,0:T(8,128)(2,1)} %add_convert_fusion.refs_1_.refs_10_), channel_id=1, source_target_pairs={{0,2},{1,7},{2,0},{3,5},{4,6},{5,3},{6,4},{7,1},{8,10},{9,15},{10,... | collective-permute-start | bytes 3526664 | tf_op jit(solution)/shard_map/ppermute | solution.py:31
  158.5 9.9 %copy-start.4 = (s32[4]{0:T(128)S(1)}, s32[4]{0:T(128)}, u32[]{:S(2)}) copy-start(s32[4]{0:T(128)} %pad_add_fusion.place) | copy-start | bytes 52
  158.5 9.9 %copy-start.7 = (bf16[656,512]{1,0:T(8,128)(2,1)S(1)}, bf16[656,512]{1,0:T(8,128)(2,1)}, u32[]{:S(2)}) copy-start(bf16[656,512]{1,0:T(8,128)(2,1)} %copy-done.6) | copy-start | bytes 2015236
  167.8 19.2 %collective-permute-start.16 = (bf16[4,896,512]{2,1,0:T(8,128)(2,1)}, bf16[4,896,512]{2,1,0:T(8,128)(2,1)}, u32[]{:S(2)}, u32[]{:S(2)}) collective-permute-start(bf16[4,896,512]{2,1,0:T(8,128)(2,1)} %get-tuple-element.43), channel_id=1, source_target_pairs={{0,1},{1,0},{2,3},{3,2},{4,5},{5,4},{6,7},{7,6},{8,9},{9,8},{10,11... | collective-permute-start | bytes 11010056 | tf_op jit(solution)/shard_map/ppermute | solution.py:35
  167.9 19.1 %collective-permute-start.17 = (bf16[4,256,896]{2,1,0:T(8,128)(2,1)}, bf16[4,256,896]{2,1,0:T(8,128)(2,1)}, u32[]{:S(2)}, u32[]{:S(2)}) collective-permute-start(bf16[4,256,896]{2,1,0:T(8,128)(2,1)} %get-tuple-element.44), channel_id=1, source_target_pairs={{0,1},{1,0},{2,3},{3,2},{4,5},{5,4},{6,7},{7,6},{8,9},{9,8},{10,11... | collective-permute-start | bytes 5505032 | tf_op jit(solution)/shard_map/ppermute | solution.py:35
  182.6 25.5 %all-to-all-start.2 = ((bf16[16,40,1024]{2,1,0:T(8,128)(2,1)}), bf16[16,40,1024]{2,1,0:T(8,128)(2,1)}, u32[]{:S(2)}, u32[]{:S(2)}) async-start(bf16[16,40,1024]{2,1,0:T(8,128)(2,1)} %bitcast.14), calls=%async_computation.2 | async-start | bytes 2621440 | tf_op jit(solution)/shard_map/all_to_all | solution.py:421
  (3 other events, 2.3 us)

commit v4 on v3

--- a/solution.py
+++ b/solution.py
@@ -12,6 +12,8 @@
 SWAP = [(0, 1), (1, 0)]
 ANY = pl.BlockSpec(memory_space=pl.ANY)
 MOST = 61
+DY_CUT = 512
+DY_REST = 896 - DY_CUT
 RATE = 3e10
 VMEM = pl.BlockSpec(memory_space=pltpu.VMEM)
 SMEM = pl.BlockSpec(memory_space=pltpu.SMEM)
@@ -63,10 +65,7 @@
     )
 
 
-def dispatch_kernel(ids, gates, x_ref, dy_ref, send_x, send_dy, onehot, x, dy, sems):
-    copies = [pltpu.make_async_copy(x_ref, x, sems.at[0]), pltpu.make_async_copy(dy_ref, dy, sems.at[1])]
-    for copy in copies:
-        copy.start()
+def dispatch_kernel(ids, gates, x, send_x, onehot, weights):
     expert = lax.broadcasted_iota(jnp.int32, (16, 64), 0)
     named = jnp.zeros((16, 64), F32)
     weight = jnp.zeros((16, 64), F32)
@@ -84,17 +83,28 @@
         sums.append(jnp.sum(pick * weight[e : e + 1, :], axis=1, keepdims=True))
     pick = jnp.concatenate(picks, axis=0).astype(BF)
     onehot[...] = pick
-    for copy in copies:
-        copy.wait()
     send_x[...] = nn(pick, x[...]).astype(BF)
-    send_dy[:, :COLS] = nn(pick, dy[...]).astype(BF)
-    send_dy[:, COLS:] = jnp.broadcast_to(jnp.concatenate(sums, axis=0), (ROWS, PAD)).astype(BF)
-
-
-def dispatch(ids, gates, x, dy):
-    outs = [(VMEM, sds((ROWS, COLS))), (VMEM, sds((ROWS, COLS + PAD))), (VMEM, sds((ROWS, 64)))]
-    scratch = [pltpu.VMEM((64, COLS), BF)] * 2 + [pltpu.SemaphoreType.DMA((2,))]
-    return call(dispatch_kernel, [VMEM] * 2 + [HBM] * 2, outs, scratch, us=4)(ids, gates, x, dy)
+    weights[...] = jnp.broadcast_to(jnp.concatenate(sums, axis=0), (ROWS, PAD)).astype(BF)
+
+
+def dispatch(ids, gates, x):
+    outs = [(VMEM, sds((ROWS, COLS))), (VMEM, sds((ROWS, 64))), (VMEM, sds((ROWS, PAD)))]
+    return call(dispatch_kernel, [VMEM] * 3, outs, us=3)(ids, gates, x)
+
+
+def second_dispatch_kernel(onehot, weights, dy, *refs):
+    rests, out = refs[:4], refs[4]
+    pick = onehot[...]
+    out[:, :DY_CUT] = nn(pick, dy[:, :DY_CUT]).astype(BF)
+    for k in range(4):
+        lo = DY_CUT + DY_REST * k
+        out[:, lo : lo + DY_REST] = nn(pick, rests[k][...]).astype(BF)
+    out[:, -PAD:] = weights[...]
+
+
+def second_dispatch(onehot, weights, dy, rests):
+    outs = [(VMEM, sds((ROWS, DY_CUT + 4 * DY_REST + PAD)))]
+    return call(second_dispatch_kernel, [VMEM] * 7, outs, us=3)(onehot, weights, dy, *rests)[0]
 
 
 def combine_kernel(back, onehot, ids, *refs):
@@ -181,11 +191,19 @@
     return call(kernel, ins, outs, hidden_scratch(len(ks)), us=8, mib=MOST)(place, *xs, ws)[0]
 
 
-def raw_steps(ks, place, dys, ws, dy, w, acc, sems):
+def dy_copies(k, ring_part, came, out, sems):
+    rest = came.at[:, pl.ds(pl.multiple_of(DY_CUT + DY_REST * k, 128), DY_REST)]
+    return [
+        pltpu.make_async_copy(ring_part, out.at[:, pl.ds(0, DY_CUT)], sems.at[0]),
+        pltpu.make_async_copy(rest, out.at[:, pl.ds(DY_CUT, DY_REST)], sems.at[1]),
+    ]
+
+
+def raw_steps(ks, place, dys, came, ws, dy, w, acc, sems):
     def copies(n, src):
         i = place[ks[0] + n]
-        first = pltpu.make_async_copy(src, dy.at[n], sems.at[1, n])
-        return [first, pltpu.make_async_copy(column_block(ws, i), w.at[n], sems.at[0, n])]
+        pieces = dy_copies(ks[0] + n, src, came, dy.at[n], sems.at[n])
+        return pieces + [pltpu.make_async_copy(column_block(ws, i), w.at[n], sems.at[n, 2])]
 
     for n in range(len(ks)):
         for copy in copies(n, dys[n]):
@@ -199,24 +217,24 @@
 
 
 def raw_scratch(n):
-    return [pltpu.VMEM((n, ROWS, COLS), BF), pltpu.VMEM((n, 2 * HID, COLS), BF), pltpu.SemaphoreType.DMA((2, n))]
-
-
-def middle_kernel(place, x_last, d0, d1, d2, *refs):
+    return [pltpu.VMEM((n, ROWS, COLS), BF), pltpu.VMEM((n, 2 * HID, COLS), BF), pltpu.SemaphoreType.DMA((n, 3))]
+
+
+def middle_kernel(place, x_last, d0, d1, d2, came, *refs):
     ws, ds, first, keep, send, raw, acc, x, w, sems, dy, v, dsems = refs
     acc[...] = first[...]
     hidden_steps(range(3, 4), place, [x_last], ws, x, w, acc, sems)
     keep[...] = acc[:, : 2 * HID]
     send[...] = acc[:, 2 * HID :]
     raw[...] = jnp.zeros_like(raw)
-    raw_steps(range(3), place, [d0, d1, d2], ds, dy, v, raw, dsems)
-
-
-def middle(place, x_last, dys, ws, ds, first):
+    raw_steps(range(3), place, [d0, d1, d2], came, ds, dy, v, raw, dsems)
+
+
+def middle(place, x_last, dys, came, ws, ds, first):
     outs = [(VMEM, sds((ROWS, 2 * HID), F32))] * 3
     scratch = [pltpu.VMEM((ROWS, 4 * HID), F32)] + hidden_scratch(1) + raw_scratch(3)
-    ins = [SMEM] + [HBM] * 6 + [VMEM]
-    return call(middle_kernel, ins, outs, scratch, us=12, mib=MOST)(place, x_last, *dys, ws, ds, first)
+    ins = [SMEM] + [HBM] * 7 + [VMEM]
+    return call(middle_kernel, ins, outs, scratch, us=12, mib=MOST)(place, x_last, *dys, came, ws, ds, first)
 
 
 def activation_kernel(keep, came, s_ref, slope_ref, h_ref):
@@ -237,18 +255,18 @@
 
 def raw_kernel(ks, place, *refs):
     n = len(ks)
-    ws, first, keep, send, acc, dy, w, sems = refs[n:]
+    came, ws, first, keep, send, acc, dy, w, sems = refs[n:]
     acc[...] = first[...]
-    raw_steps(ks, place, refs[:n], ws, dy, w, acc, sems)
+    raw_steps(ks, place, refs[:n], came, ws, dy, w, acc, sems)
     keep[...] = acc[:, :HID]
     send[...] = acc[:, HID:]
 
 
-def raw_rest(ks, place, dys, ws, first):
+def raw_rest(ks, place, dys, came, ws, first):
     outs = [(VMEM, sds((ROWS, HID), F32))] * 2
     scratch = [pltpu.VMEM((ROWS, 2 * HID), F32)] + raw_scratch(len(ks))
-    ins = [SMEM] + [HBM] * (len(ks) + 1) + [VMEM]
-    return call(functools.partial(raw_kernel, ks), ins, outs, scratch, us=3, mib=58)(place, *dys, ws, first)
+    ins = [SMEM] + [HBM] * (len(ks) + 2) + [VMEM]
+    return call(functools.partial(raw_kernel, ks), ins, outs, scratch, us=3, mib=58)(place, *dys, came, ws, first)
 
 
 def gradient_kernel(keep, came, s_ref, slope_ref, h_ref, gate, dab, hs):
@@ -299,9 +317,21 @@
     return lambda k: load(k, refs[0]).wait()
 
 
+def dy_stream(refs, came, buffer, sems):
+    for k, ref in enumerate(refs):
+        for copy in dy_copies(k, ref, came, buffer.at[k], sems.at[k]):
+            copy.start()
+
+    def ready(k):
+        for copy in dy_copies(k, refs[0], came, buffer.at[k], sems.at[k]):
+            copy.wait()
+
+    return ready
+
+
 def other_gradient_kernel(*refs):
-    xs, dys, (dab, hs, _, columns, rows, x, dy, c, r, xsems, dsems, sems) = refs[:4], refs[4:8], refs[8:]
-    x_ready, dy_ready = stream(xs, x, xsems), stream(dys, dy, dsems)
+    xs, dys, (came, dab, hs, _, columns, rows, x, dy, c, r, xsems, dsems, sems) = refs[:4], refs[4:8], refs[8:]
+    x_ready, dy_ready = stream(xs, x, xsems), dy_stream(dys, came, dy, dsems)
 
     def stores(k):
         return [
@@ -329,18 +359,18 @@
 PIECES = [pltpu.VMEM((4, ROWS, COLS), BF)] * 2 + [pltpu.VMEM((4, COLS, 2 * HID), BF), pltpu.VMEM((4, HID, COLS), BF)]
 
 
-def other_gradients(xs, dys, dab, hs, later):
-    scratch = PIECES + [pltpu.SemaphoreType.DMA((4,))] * 2 + [pltpu.SemaphoreType.DMA((2, 4))]
+def other_gradients(xs, dys, came, dab, hs, later):
+    scratch = PIECES + [pltpu.SemaphoreType.DMA((4,)), pltpu.SemaphoreType.DMA((4, 2)), pltpu.SemaphoreType.DMA((2, 4))]
     outs = [(HBM, sds((4, COLS, 2 * HID))), (HBM, sds((4, HID, COLS)))]
-    ins = [HBM] * 8 + [VMEM] * 2 + [ANY]
-    return call(other_gradient_kernel, ins, outs, scratch, us=10, mib=MOST)(*xs, *dys, dab, hs, later)
+    ins = [HBM] * 9 + [VMEM] * 2 + [ANY]
+    return call(other_gradient_kernel, ins, outs, scratch, us=10, mib=MOST)(*xs, *dys, came, dab, hs, later)
 
 
 def own_gradient_kernel(place, other_place, *refs):
-    xs, dys, refs = refs[:4], refs[4:8], refs[8:]
+    xs, dys, came, refs = refs[:4], refs[4:8], refs[8], refs[9:]
     dab, hs, columns, rows, _, g, u, d, token, x, dy, c, r, c_in, r_in, xsems, dsems, isems, sems = refs
     token[...] = jnp.zeros_like(token)
-    x_ready, dy_ready = stream(xs, x, xsems), stream(dys, dy, dsems)
+    x_ready, dy_ready = stream(xs, x, xsems), dy_stream(dys, came, dy, dsems)
 
     def arrivals(k):
         return [
@@ -379,13 +409,13 @@
             copy.wait()
 
 
-def own_gradients(place, other_place, xs, dys, dab, hs, columns, rows, later):
-    scratch = PIECES + PIECES[2:] + [pltpu.SemaphoreType.DMA((4,))] * 2
+def own_gradients(place, other_place, xs, dys, came, dab, hs, columns, rows, later):
+    scratch = PIECES + PIECES[2:] + [pltpu.SemaphoreType.DMA((4,)), pltpu.SemaphoreType.DMA((4, 2))]
     scratch += [pltpu.SemaphoreType.DMA((2, 4)), pltpu.SemaphoreType.DMA((6, 4))]
     outs = [(HBM, sds((8 * COLS, HID)))] * 2 + [(HBM, sds((HID, 8 * COLS))), (VMEM, sds((8, 128), F32))]
-    ins = [SMEM] * 2 + [HBM] * 8 + [VMEM] * 2 + [HBM] * 2 + [ANY]
+    ins = [SMEM] * 2 + [HBM] * 9 + [VMEM] * 2 + [HBM] * 2 + [ANY]
     kernel = call(own_gradient_kernel, ins, outs, scratch, us=12, mib=MOST)
-    return kernel(place, other_place, *xs, *dys, dab, hs, columns, rows, later)
+    return kernel(place, other_place, *xs, *dys, came, dab, hs, columns, rows, later)
 
 
 def total_kernel(expert, *refs):
@@ -437,22 +467,25 @@
     other_place = jnp.stack([2 * ys[k] + 1 - core for k in (0, 2, 1, 3)]).astype(jnp.int32)
     wg, wu, wd = wg[0], wu[0], wd[0]
 
-    send_x, send_dy, onehot = dispatch(ids.T, gates.T.astype(F32), tokens, cotangent)
+    send_x, onehot, weights = dispatch(ids.T, gates.T.astype(F32), tokens)
+    rests = ring(cotangent[:, DY_CUT:])
+    rests.append(meet(rests[1], 1))
+    send_dy = second_dispatch(onehot, weights, cotangent, rests)
     ws = (wg, wu, swap(wg), swap(wu))
     ds = (wd, swap(wd))
     xs = ring(after(exchange(send_x), ws[2], ws[3], ds[1]))
     x_last = meet(xs[1], 1)
     came = exchange(after(send_dy, xs[0]))
-    gate = came[:, COLS:]
-    dys = ring(came[:, :COLS])
+    gate = came[:, -PAD:]
+    dys = ring(came[:, :DY_CUT])
     dys[1] = after(dys[1], dys[2])
     dy_last = meet(dys[1], 1)
 
     ws, ds = pack(*ws, *ds)
     first = first_hidden(range(3), place, xs, ws)
-    keep, send, raw = middle(place, x_last, dys, ws, ds, first)
+    keep, send, raw = middle(place, x_last, dys, came, ws, ds, first)
     s, slope, h = activation(keep, swap(send))
-    keep, send = raw_rest(range(3, 4), place, [dy_last], ds, raw)
+    keep, send = raw_rest(range(3, 4), place, [dy_last], came, ds, raw)
     dab, hs = gradients(keep, swap(send), s, slope, h, gate)
     dab_other, hs_other = swap(dab), swap(hs)
 
@@ -466,10 +499,10 @@
     own = add(own, opposite)
     rest = meet(own, 0)
     xs, dys = xs + [x_last], dys + [dy_last]
-    columns, rows = other_gradients(xs, dys, dab_other, hs_other, own)
+    columns, rows = other_gradients(xs, dys, came, dab_other, hs_other, own)
     columns, rows = swap(columns), swap(rows)
     share = total(expert, (part(0, own), near, rest))
-    gate_grad, up_grad, down_grad, done = own_gradients(place, other_place, xs, dys, dab, hs, columns, rows, share)
+    gate_grad, up_grad, down_grad, done = own_gradients(place, other_place, xs, dys, came, dab, hs, columns, rows, share)
     input_grad, slot_grad = combine(exchange(share), onehot, ids, done)
     return input_grad, slot_grad, gate_grad[None], up_grad[None], down_grad[None]
 

time: 215 us -> 203 us (0.944)
  waiting for transfers between devices: 80.9 us -> 62.8 us
  starting transfers between devices: 31.7 us -> 37.7 us
    ppermute x9 -> x12, waiting for transfers between devices: 50.1 us -> 25.2 us  [meet(): return lax.ppermute(v, ('y', 'core'), MEET[step])]
    all_to_all x3, waiting for transfers between devices: 27.9 us -> 34.8 us  [exchange(): lax.all_to_all(v.reshape(16, ROOM, -1), ('x', 'z'), 0, 0, tiled=True)]
    ppermute x9 -> x12, starting transfers between devices: 13 us -> 17.9 us  [meet(): return lax.ppermute(v, ('y', 'core'), MEET[step])]
    pallas_call x2 -> x3, Pallas kernels: 14 us -> 14.7 us  [the longest x1 12.3 us: own_gradients(): kernel(place, other_place, *xs, *dys, came, dab, hs, columns, rows, later)]
    unnamed x30 -> x34, local copies, waits for them, and re-layouts: 5.98 us -> 5.56 us
  transfers between devices with their start and end apart: 21 -> 24, of which waited for: 10 -> 12; matrix products, arithmetic and copies ran while one was open for 4% -> 4% of each run, Pallas kernels for 38% -> 41%
where the time goes in v4:
time: 203 us; the launch traced here: 201 us
  Pallas kernels  85.9 us (42%)
  waiting for transfers between devices  62.8 us (31%)
  starting transfers between devices  37.7 us (19%)
  local copies, waits for them, and re-layouts  9.28 us (5%)
  other arithmetic  4.55 us (2%)
    all_to_all x3, waiting for transfers between devices, exchange(): lax.all_to_all(v.reshape(16, ROOM, -1), ('x', 'z'), 0, 0, tiled=True)  34.8 us
    ppermute x12, waiting for transfers between devices, meet(): return lax.ppermute(v, ('y', 'core'), MEET[step])  25.2 us
    all_to_all x3, starting transfers between devices, exchange(): lax.all_to_all(v.reshape(16, ROOM, -1), ('x', 'z'), 0, 0, tiled=True)  18 us
    ppermute x12, starting transfers between devices, meet(): return lax.ppermute(v, ('y', 'core'), MEET[step])  17.9 us
    pallas_call x4, Pallas kernels, input_part(): call(functools.partial(input_kernel, k), ins, outs, scratch, us=4, mib=51)  16.4 us
    pallas_call x1, Pallas kernels, pack(): call(pack_kernel, [HBM] * 6, outs, scratch, us=13, mib=MOST)(*weights)  14.7 us
    pallas_call x1, Pallas kernels, own_gradients(): kernel(place, other_place, *xs, *dys, came, dab, hs, columns, rows, later)  12.3 us
    pallas_call x1, Pallas kernels, other_gradients(): call(other_gradient_kernel, ins, outs, scratch, us=10, mib=MOST)  10.1 us
  transfers between devices with their start and end apart: 24, of which 12 were waited for; matrix products, arithmetic and copies ran while one was open for 4% of the time, Pallas kernels for 41%

profile of v4, /device:TPU:0, one launch (start us, length us, event | category | flops | bytes accessed | tf_op | source)
XLA Modules:
  0.0 201.1 jit_solution(12437624511595599284)
XLA Ops:
  3.1 2.2 %collective-permute-start.1 = (bf16[64,384]{1,0:T(8,128)(2,1)S(1)}, bf16[64,384]{1,0:T(8,128)(2,1)S(1)}, u32[]{:S(2)}, u32[]{:S(2)}) collective-permute-start(bf16[64,384]{1,0:T(8,128)(2,1)S(1)} %slice.9.refs_0_), channel_id=1, source_target_pairs={{0,6},{1,3},{2,4},{3,1},{4,2},{5,7},{6,0},{7,5},{8,14},{9,11},{10,... | collective-permute-start | bytes 147464 | tf_op jit(solution)/shard_map/ppermute | solution.py:33
  9.6 8.0 %all-to-all-start = ((bf16[16,40,896]{2,1,0:T(8,128)(2,1)}), bf16[16,40,896]{2,1,0:T(8,128)(2,1)S(1)}, u32[]{:S(2)}, u32[]{:S(2)}) async-start(bf16[16,40,896]{2,1,0:T(8,128)(2,1)} %bitcast.7), calls=%async_computation | async-start | bytes 2293760 | tf_op jit(solution)/shard_map/all_to_all | solution.py:451
  19.5 3.6 %collective-permute-done.2.refs_3_ = bf16[64,384]{1,0:T(8,128)(2,1)S(1)} collective-permute-done((bf16[64,384]{1,0:T(8,128)(2,1)S(1)}, bf16[64,384]{1,0:T(8,128)(2,1)S(1)}, u32[]{:S(2)}, u32[]{:S(2)}) %collective-permute-start.2) | collective-permute-done | bytes 49184 | tf_op jit(solution)/shard_map/ppermute | solution.py:33
  25.5 11.9 %all-to-all-done = bf16[16,40,896]{2,1,0:T(8,128)(2,1)S(1)} async-done(((bf16[16,40,896]{2,1,0:T(8,128)(2,1)}), bf16[16,40,896]{2,1,0:T(8,128)(2,1)S(1)}, u32[]{:S(2)}, u32[]{:S(2)}) %all-to-all-start) | async-done | bytes 1146912 | tf_op jit(solution)/shard_map/all_to_all | solution.py:451
  39.6 4.5 %all-to-all-start.1 = ((bf16[16,40,2176]{2,1,0:T(8,128)(2,1)}), bf16[16,40,2176]{2,1,0:T(8,128)(2,1)}, u32[]{:S(2)}, u32[]{:S(2)}) async-start(bf16[16,40,2176]{2,1,0:T(8,128)(2,1)} %bitcast.24), calls=%async_computation.1 | async-start | bytes 5570560 | tf_op jit(solution)/shard_map/all_to_all | solution.py:451
  44.1 14.7 %shard_map.115 = (bf16[7168,1024]{1,0:T(8,128)(2,1)}, bf16[512,7168]{1,0:T(8,128)(2,1)}) custom-call(bf16[7168,256]{1,0:T(8,128)(2,1)} %bitcast.28, bf16[7168,256]{1,0:T(8,128)(2,1)} %bitcast.30, bf16[7168,256]{1,0:T(8,128)(2,1)} %collective-permute-done.3.refs_1_.refs_2_, bf16[7168,256]{1,0:T(8,128)(2,1)} %collective-permute-done.4.refs_2_.refs_3_, ...), custom_call_target="tpu_custom_call" | custom-call | flops 389999984640 | bytes 10000 | tf_op jit(solution)/shard_map/pallas_call | solution.py:156
  58.7 6.7 %collective-permute-done.9.refs_1_ = bf16[640,896]{1,0:T(8,128)(2,1)} collective-permute-done((bf16[640,896]{1,0:T(8,128)(2,1)}, bf16[640,896]{1,0:T(8,128)(2,1)}, u32[]{:S(2)}, u32[]{:S(2)}) %collective-permute-start.9) | collective-permute-done | bytes 1146912 | tf_op jit(solution)/shard_map/ppermute | solution.py:33
  65.4 2.2 %collective-permute-start.10 = (bf16[640,896]{1,0:T(8,128)(2,1)}, bf16[640,896]{1,0:T(8,128)(2,1)}, u32[]{:S(2)}, u32[]{:S(2)}) collective-permute-start(bf16[640,896]{1,0:T(8,128)(2,1)} %collective-permute-done.9.refs_1_), channel_id=1, source_target_pairs={{0,6},{1,3},{2,4},{3,1},{4,2},{5,7},{6,0},{7,5},{8,14},{9,11},{10,... | collective-permute-start | bytes 3440648 | tf_op jit(solution)/shard_map/ppermute | solution.py:33
  67.6 13.2 %all-to-all-done.1 = bf16[16,40,2176]{2,1,0:T(8,128)(2,1)} async-done(((bf16[16,40,2176]{2,1,0:T(8,128)(2,1)}), bf16[16,40,2176]{2,1,0:T(8,128)(2,1)}, u32[]{:S(2)}, u32[]{:S(2)}) %all-to-all-start.1) | async-done | bytes 2785312 | tf_op jit(solution)/shard_map/all_to_all | solution.py:451
  80.8 2.0 slice.12.d0.refs_4_
  82.7 1.9 collective-permute-start.7
  84.6 2.0 collective-permute-start.6
  86.6 8.6 %shard_map.116.refs_2_ = f32[640,1024]{1,0:T(8,128)} custom-call(s32[4]{0:T(128)} %pad_add_fusion.place, bf16[640,896]{1,0:T(8,128)(2,1)} %shard_map.112.refs_1_.refs_0_, bf16[640,896]{1,0:T(8,128)(2,1)} %collective-permute-done.9.refs_1_, bf16[640,896]{1,0:T(8,128)(2,1)} %collective-permute-done.11.refs_2_, bf16[7168,1024]{1,0:T(8,128)(2,1)} %get-tuple-element.32.refs_3_.refs_0_), custom_call_target="tpu_custom_call" | custom-call | flops 240000008192 | bytes 10000 | tf_op jit(solution)/shard_map/pallas_call | solution.py:191
  97.9 2.2 %collective-permute-start.8 = (bf16[640,512]{1,0:T(8,128)(2,1)}, bf16[640,512]{1,0:T(8,128)(2,1)}, u32[]{:S(2)}, u32[]{:S(2)}) collective-permute-start(bf16[640,512]{1,0:T(8,128)(2,1)} %shard_map.114.d1.refs_5_), channel_id=1, source_target_pairs={{0,6},{1,3},{2,4},{3,1},{4,2},{5,7},{6,0},{7,5},{8,14},{9,11},{10,... | collective-permute-start | bytes 1966088 | tf_op jit(solution)/shard_map/ppermute | solution.py:33
  100.1 9.0 %shard_map.117 = (f32[640,512]{1,0:T(8,128)}, f32[640,512]{1,0:T(8,128)}, f32[640,512]{1,0:T(8,128)}) custom-call(s32[4]{0:T(128)} %pad_add_fusion.place, bf16[640,896]{1,0:T(8,128)(2,1)} %collective-permute-done.10.x_last.refs_3_, bf16[640,512]{1,0:T(8,128)(2,1)} %slice.12.d0.refs_4_, bf16[640,512]{1,0:T(8,128)(2,1)} %shard_map.114.d1.refs_5_, ...), custom_call_target="tpu_custom_call" | custom-call | flops 359999995904 | bytes 10000 | tf_op jit(solution)/shard_map/pallas_call | solution.py:237
  110.0 4.9 %shard_map.118 = (f32[640,256]{1,0:T(8,128)}, f32[640,256]{1,0:T(8,128)}) custom-call(s32[4]{0:T(128)} %pad_add_fusion.place, bf16[640,512]{1,0:T(8,128)(2,1)} %collective-permute-done.8.refs_0_.refs_7_, bf16[640,2176]{1,0:T(8,128)(2,1)} %bitcast.13.came.refs_1_.refs_8_, bf16[512,7168]{1,0:T(8,128)(2,1)} %get-tuple-element.31.refs_1_.refs_2_, ...), custom_call_target="tpu_custom_call" | custom-call | flops 89999998976 | bytes 10000 | tf_op jit(solution)/shard_map/pallas_call | solution.py:269
  115.4 1.9 collective-permute-done.12.came
  120.6 4.6 %shard_map.121.refs_1_ = bf16[656,896]{1,0:T(8,128)(2,1)} custom-call(s32[4]{0:T(128)S(1)} %copy-done.4, bf16[656,512]{1,0:T(8,128)(2,1)S(1)} %get-tuple-element.41.own.refs_9_, bf16[656,512]{1,0:T(8,128)(2,1)S(1)} %collective-permute-done.14.other.refs_9_, bf16[7168,1024]{1,0:T(8,128)(2,1)} %get-tuple-element.32.refs_3_.refs_0_), custom_call_target="tpu_custom_call" | custom-call | flops 120000004096 | bytes 10000 | tf_op jit(solution)/shard_map/pallas_call | solution.py:308
  125.3 2.3 %collective-permute-start.15 = (bf16[656,896]{1,0:T(8,128)(2,1)}, bf16[656,896]{1,0:T(8,128)(2,1)}, u32[]{:S(2)}, u32[]{:S(2)}) collective-permute-start(bf16[656,896]{1,0:T(8,128)(2,1)} %shard_map.121.refs_1_), channel_id=1, source_target_pairs={{0,6},{1,3},{2,4},{3,1},{4,2},{5,7},{6,0},{7,5},{8,14},{9,11},{10,... | collective-permute-start | bytes 3526664 | tf_op jit(solution)/shard_map/ppermute | solution.py:33
  127.5 4.6 %shard_map.122.refs_1_ = bf16[656,896]{1,0:T(8,128)(2,1)} custom-call(s32[4]{0:T(128)S(1)} %copy-done.4, bf16[656,512]{1,0:T(8,128)(2,1)S(1)} %get-tuple-element.41.own.refs_9_, bf16[656,512]{1,0:T(8,128)(2,1)S(1)} %collective-permute-done.14.other.refs_9_, bf16[7168,1024]{1,0:T(8,128)(2,1)} %get-tuple-element.32.refs_3_.refs_0_, ...), custom_call_target="tpu_custom_call" | custom-call | flops 120000004096 | bytes 10000 | tf_op jit(solution)/shard_map/pallas_call | solution.py:308
  133.3 3.6 %shard_map.123 = bf16[656,896]{1,0:T(8,128)(2,1)S(1)} custom-call(s32[4]{0:T(128)S(1)} %copy-done.4, bf16[656,512]{1,0:T(8,128)(2,1)S(1)} %get-tuple-element.41.own.refs_9_, bf16[656,512]{1,0:T(8,128)(2,1)S(1)} %collective-permute-done.14.other.refs_9_, bf16[7168,1024]{1,0:T(8,128)(2,1)} %get-tuple-element.32.refs_3_.refs_0_, ...), custom_call_target="tpu_custom_call" | custom-call | flops 120000004096 | bytes 10000 | tf_op jit(solution)/shard_map/pallas_call | solution.py:308
  136.9 6.1 %collective-permute-done.15 = bf16[656,896]{1,0:T(8,128)(2,1)} collective-permute-done((bf16[656,896]{1,0:T(8,128)(2,1)}, bf16[656,896]{1,0:T(8,128)(2,1)}, u32[]{:S(2)}, u32[]{:S(2)}) %collective-permute-start.15) | collective-permute-done | bytes 1175584 | tf_op jit(solution)/shard_map/ppermute | solution.py:33
  143.0 2.6 %add_convert_fusion.refs_1_.refs_11_ = bf16[656,896]{1,0:T(8,128)(2,1)} fusion(bf16[656,896]{1,0:T(8,128)(2,1)} %collective-permute-done.15, bf16[656,896]{1,0:T(8,128)(2,1)S(1)} %shard_map.123), kind=kLoop, calls=%fused_computation | loop fusion | flops 2351104 | bytes 3526656 | tf_op jit(solution)/shard_map/convert_element_type | solution.py:459
  145.6 10.1 %shard_map.126 = (bf16[4,896,512]{2,1,0:T(8,128)(2,1)}, bf16[4,256,896]{2,1,0:T(8,128)(2,1)}) custom-call(bf16[640,896]{1,0:T(8,128)(2,1)} %shard_map.112.refs_1_.refs_0_, bf16[640,896]{1,0:T(8,128)(2,1)} %collective-permute-done.9.refs_1_, bf16[640,896]{1,0:T(8,128)(2,1)} %collective-permute-done.11.refs_2_, ...), custom_call_target="tpu_custom_call" | custom-call | flops 299999985664 | bytes 10000 | tf_op jit(solution)/shard_map/pallas_call | solution.py:366
  156.3 3.6 %shard_map.124.refs_0_ = bf16[656,896]{1,0:T(8,128)(2,1)S(1)} custom-call(s32[4]{0:T(128)S(1)} %copy-done.5, bf16[656,512]{1,0:T(8,128)(2,1)S(1)} %get-tuple-element.41.own.refs_9_, bf16[656,512]{1,0:T(8,128)(2,1)S(1)} %copy-done.8, bf16[7168,1024]{1,0:T(8,128)(2,1)} %get-tuple-element.32.refs_3_.refs_0_, bf16[656,896]{1,0:T(8,128)(2,1)} %add_convert_fusion.refs_1_.refs_11_), custom_call_target="tpu_custom_call" | custom-call | flops 120000004096 | bytes 10000 | tf_op jit(solution)/shard_map/pallas_call | solution.py:308
  159.9 3.5 %collective-permute-done.16.refs_1_ = bf16[656,896]{1,0:T(8,128)(2,1)} collective-permute-done((bf16[656,896]{1,0:T(8,128)(2,1)}, bf16[656,896]{1,0:T(8,128)(2,1)}, u32[]{:S(2)}, u32[]{:S(2)}) %collective-permute-start.16) | collective-permute-done | bytes 1175584 | tf_op jit(solution)/shard_map/ppermute | solution.py:33
  163.4 2.8 %collective-permute-done.17.refs_2_ = bf16[656,896]{1,0:T(8,128)(2,1)} collective-permute-done((bf16[656,896]{1,0:T(8,128)(2,1)}, bf16[656,896]{1,0:T(8,128)(2,1)}, u32[]{:S(2)}, u32[]{:S(2)}) %collective-permute-start.17) | collective-permute-done | bytes 1175584 | tf_op jit(solution)/shard_map/ppermute | solution.py:33
  166.2 3.5 %shard_map.125.refs_13_ = bf16[640,1024]{1,0:T(8,128)(2,1)} custom-call(s32[1]{0:T(128)} %bitcast.expert, bf16[656,896]{1,0:T(8,128)(2,1)S(1)} %shard_map.124.refs_0_, bf16[656,896]{1,0:T(8,128)(2,1)} %collective-permute-done.16.refs_1_, bf16[656,896]{1,0:T(8,128)(2,1)} %collective-permute-done.17.refs_2_), custom_call_target="tpu_custom_call" | custom-call | flops 30000001024 | bytes 10000 | tf_op jit(solution)/shard_map/pallas_call | solution.py:437
  169.7 5.5 %all-to-all-start.2 = ((bf16[16,40,1024]{2,1,0:T(8,128)(2,1)}), bf16[16,40,1024]{2,1,0:T(8,128)(2,1)}, u32[]{:S(2)}, u32[]{:S(2)}) async-start(bf16[16,40,1024]{2,1,0:T(8,128)(2,1)} %bitcast.14), calls=%async_computation.2 | async-start | bytes 2621440 | tf_op jit(solution)/shard_map/all_to_all | solution.py:451
  175.2 12.3 %shard_map.127 = (bf16[7168,256]{1,0:T(8,128)(2,1)}, bf16[7168,256]{1,0:T(8,128)(2,1)}, bf16[256,7168]{1,0:T(8,128)(2,1)}, f32[8,128]{1,0:T(8,128)}) custom-call(s32[4]{0:T(128)} %pad_add_fusion.place, s32[4]{0:T(128)} %pad_add_fusion.1.other_place, bf16[640,896]{1,0:T(8,128)(2,1)} %shard_map.112.refs_1_.refs_0_, ...), custom_call_target="tpu_custom_call" | custom-call | flops 359999995904 | bytes 10000 | tf_op jit(solution)/shard_map/pallas_call | solution.py:418
  187.5 9.8 %all-to-all-done.2 = bf16[16,40,1024]{2,1,0:T(8,128)(2,1)} async-done(((bf16[16,40,1024]{2,1,0:T(8,128)(2,1)}), bf16[16,40,1024]{2,1,0:T(8,128)(2,1)}, u32[]{:S(2)}, u32[]{:S(2)}) %all-to-all-start.2) | async-done | bytes 1310752 | tf_op jit(solution)/shard_map/all_to_all | solution.py:451
  198.0 2.5 %shard_map.128 = (bf16[64,896]{1,0:T(8,128)(2,1)}, f32[64,8]{1,0:T(8,128)S(1)}) custom-call(bf16[640,1024]{1,0:T(8,128)(2,1)} %bitcast.15.back, bf16[640,64]{1,0:T(8,128)(2,1)S(1)} %copy-done.13, s32[64,8]{1,0:T(8,128)S(1)} %copy.15.ids, f32[8,128]{1,0:T(8,128)S(1)} %copy-done.14), custom_call_target="tpu_custom_call" | custom-call | flops 89999998976 | bytes 10000 | tf_op jit(solution)/shard_map/pallas_call | solution.py:126
  (76 shorter events, 23.5 us)
Async XLA Ops:
  1.4 16.3 %collective-permute-start = (bf16[64,384]{1,0:T(8,128)(2,1)S(1)}, bf16[64,384]{1,0:T(8,128)(2,1)S(1)}, u32[]{:S(2)}, u32[]{:S(2)}) collective-permute-start(bf16[64,384]{1,0:T(8,128)(2,1)S(1)} %slice.9.refs_0_), channel_id=1, source_target_pairs={{0,2},{1,7},{2,0},{3,5},{4,6},{5,3},{6,4},{7,1},{8,10},{9,15},{10,... | collective-permute-start | bytes 147464 | tf_op jit(solution)/shard_map/ppermute | solution.py:33
  3.1 16.4 %collective-permute-start.1 = (bf16[64,384]{1,0:T(8,128)(2,1)S(1)}, bf16[64,384]{1,0:T(8,128)(2,1)S(1)}, u32[]{:S(2)}, u32[]{:S(2)}) collective-permute-start(bf16[64,384]{1,0:T(8,128)(2,1)S(1)} %slice.9.refs_0_), channel_id=1, source_target_pairs={{0,6},{1,3},{2,4},{3,1},{4,2},{5,7},{6,0},{7,5},{8,14},{9,11},{10,... | collective-permute-start | bytes 147464 | tf_op jit(solution)/shard_map/ppermute | solution.py:33
  5.3 32.0 %collective-permute-start.3 = (bf16[7168,256]{1,0:T(8,128)(2,1)}, bf16[7168,256]{1,0:T(8,128)(2,1)}, u32[]{:S(2)}, u32[]{:S(2)}) collective-permute-start(bf16[7168,256]{1,0:T(8,128)(2,1)} %bitcast.27), channel_id=1, source_target_pairs={{0,1},{1,0},{2,3},{3,2},{4,5},{5,4},{6,7},{7,6},{8,9},{9,8},{10,11... | collective-permute-start | bytes 11010056 | tf_op jit(solution)/shard_map/ppermute | solution.py:37
  5.3 32.0 %collective-permute-start.4 = (bf16[7168,256]{1,0:T(8,128)(2,1)}, bf16[7168,256]{1,0:T(8,128)(2,1)}, u32[]{:S(2)}, u32[]{:S(2)}) collective-permute-start(bf16[7168,256]{1,0:T(8,128)(2,1)} %bitcast.29), channel_id=1, source_target_pairs={{0,1},{1,0},{2,3},{3,2},{4,5},{5,4},{6,7},{7,6},{8,9},{9,8},{10,11... | collective-permute-start | bytes 11010056 | tf_op jit(solution)/shard_map/ppermute | solution.py:37
  5.8 31.5 %collective-permute-start.5 = (bf16[256,7168]{1,0:T(8,128)(2,1)}, bf16[256,7168]{1,0:T(8,128)(2,1)}, u32[]{:S(2)}, u32[]{:S(2)}) collective-permute-start(bf16[256,7168]{1,0:T(8,128)(2,1)} %bitcast.31), channel_id=1, source_target_pairs={{0,1},{1,0},{2,3},{3,2},{4,5},{5,4},{6,7},{7,6},{8,9},{9,8},{10,11... | collective-permute-start | bytes 11010056 | tf_op jit(solution)/shard_map/ppermute | solution.py:37
  9.6 14.3 %copy-start.12 = (bf16[640,64]{1,0:T(8,128)(2,1)}, bf16[640,64]{1,0:T(8,128)(2,1)S(1)}, u32[]{:S(2)}) copy-start(bf16[640,64]{1,0:T(8,128)(2,1)S(1)} %get-tuple-element.28.onehot) | copy-start | bytes 245764
  9.6 13.4 %copy-start.1 = (bf16[64,896]{1,0:T(8,128)(2,1)S(1)}, bf16[64,896]{1,0:T(8,128)(2,1)}, u32[]{:S(2)}) copy-start(bf16[64,896]{1,0:T(8,128)(2,1)} %dy.1) | copy-start | bytes 344068
  9.6 27.7 %all-to-all-start = ((bf16[16,40,896]{2,1,0:T(8,128)(2,1)}), bf16[16,40,896]{2,1,0:T(8,128)(2,1)S(1)}, u32[]{:S(2)}, u32[]{:S(2)}) async-start(bf16[16,40,896]{2,1,0:T(8,128)(2,1)} %bitcast.7), calls=%async_computation | async-start | bytes 2293760 | tf_op jit(solution)/shard_map/all_to_all | solution.py:451
  17.7 5.4 %collective-permute-start.2 = (bf16[64,384]{1,0:T(8,128)(2,1)S(1)}, bf16[64,384]{1,0:T(8,128)(2,1)S(1)}, u32[]{:S(2)}, u32[]{:S(2)}) collective-permute-start(bf16[64,384]{1,0:T(8,128)(2,1)S(1)} %collective-permute-done.refs_1_), channel_id=1, source_target_pairs={{0,6},{1,3},{2,4},{3,1},{4,2},{5,7},{6,0},{7,5},{8,14},{9,11},{10,... | collective-permute-start | bytes 147464 | tf_op jit(solution)/shard_map/ppermute | solution.py:33
  38.3 27.1 %collective-permute-start.9 = (bf16[640,896]{1,0:T(8,128)(2,1)}, bf16[640,896]{1,0:T(8,128)(2,1)}, u32[]{:S(2)}, u32[]{:S(2)}) collective-permute-start(bf16[640,896]{1,0:T(8,128)(2,1)} %shard_map.112.refs_1_.refs_0_), channel_id=1, source_target_pairs={{0,2},{1,7},{2,0},{3,5},{4,6},{5,3},{6,4},{7,1},{8,10},{9,15},{10,... | collective-permute-start | bytes 3440648 | tf_op jit(solution)/shard_map/ppermute | solution.py:33
  39.0 47.7 %collective-permute-start.11 = (bf16[640,896]{1,0:T(8,128)(2,1)}, bf16[640,896]{1,0:T(8,128)(2,1)}, u32[]{:S(2)}, u32[]{:S(2)}) collective-permute-start(bf16[640,896]{1,0:T(8,128)(2,1)} %shard_map.112.refs_1_.refs_0_), channel_id=1, source_target_pairs={{0,6},{1,3},{2,4},{3,1},{4,2},{5,7},{6,0},{7,5},{8,14},{9,11},{10,... | collective-permute-start | bytes 3440648 | tf_op jit(solution)/shard_map/ppermute | solution.py:33
  39.6 41.2 %all-to-all-start.1 = ((bf16[16,40,2176]{2,1,0:T(8,128)(2,1)}), bf16[16,40,2176]{2,1,0:T(8,128)(2,1)}, u32[]{:S(2)}, u32[]{:S(2)}) async-start(bf16[16,40,2176]{2,1,0:T(8,128)(2,1)} %bitcast.24), calls=%async_computation.1 | async-start | bytes 5570560 | tf_op jit(solution)/shard_map/all_to_all | solution.py:451
  65.4 34.7 %collective-permute-start.10 = (bf16[640,896]{1,0:T(8,128)(2,1)}, bf16[640,896]{1,0:T(8,128)(2,1)}, u32[]{:S(2)}, u32[]{:S(2)}) collective-permute-start(bf16[640,896]{1,0:T(8,128)(2,1)} %collective-permute-done.9.refs_1_), channel_id=1, source_target_pairs={{0,6},{1,3},{2,4},{3,1},{4,2},{5,7},{6,0},{7,5},{8,14},{9,11},{10,... | collective-permute-start | bytes 3440648 | tf_op jit(solution)/shard_map/ppermute | solution.py:33
  82.7 15.1 %collective-permute-start.7 = (bf16[640,512]{1,0:T(8,128)(2,1)}, bf16[640,512]{1,0:T(8,128)(2,1)}, u32[]{:S(2)}, u32[]{:S(2)}) collective-permute-start(bf16[640,512]{1,0:T(8,128)(2,1)} %slice.12.d0.refs_4_), channel_id=1, source_target_pairs={{0,6},{1,3},{2,4},{3,1},{4,2},{5,7},{6,0},{7,5},{8,14},{9,11},{10,... | collective-permute-start | bytes 1966088 | tf_op jit(solution)/shard_map/ppermute | solution.py:33
  84.6 13.3 %collective-permute-start.6 = (bf16[640,512]{1,0:T(8,128)(2,1)}, bf16[640,512]{1,0:T(8,128)(2,1)}, u32[]{:S(2)}, u32[]{:S(2)}) collective-permute-start(bf16[640,512]{1,0:T(8,128)(2,1)} %slice.12.d0.refs_4_), channel_id=1, source_target_pairs={{0,2},{1,7},{2,0},{3,5},{4,6},{5,3},{6,4},{7,1},{8,10},{9,15},{10,... | collective-permute-start | bytes 1966088 | tf_op jit(solution)/shard_map/ppermute | solution.py:33
  97.9 12.1 %collective-permute-start.8 = (bf16[640,512]{1,0:T(8,128)(2,1)}, bf16[640,512]{1,0:T(8,128)(2,1)}, u32[]{:S(2)}, u32[]{:S(2)}) collective-permute-start(bf16[640,512]{1,0:T(8,128)(2,1)} %shard_map.114.d1.refs_5_), channel_id=1, source_target_pairs={{0,6},{1,3},{2,4},{3,1},{4,2},{5,7},{6,0},{7,5},{8,14},{9,11},{10,... | collective-permute-start | bytes 1966088 | tf_op jit(solution)/shard_map/ppermute | solution.py:33
  109.1 5.9 %collective-permute-start.13 = (f32[640,512]{1,0:T(8,128)}, f32[640,512]{1,0:T(8,128)S(1)}, u32[]{:S(2)}, u32[]{:S(2)}) collective-permute-start(f32[640,512]{1,0:T(8,128)} %get-tuple-element.37), channel_id=1, source_target_pairs={{0,1},{1,0},{2,3},{3,2},{4,5},{5,4},{6,7},{7,6},{8,9},{9,8},{10,11... | collective-permute-start | bytes 3932168 | tf_op jit(solution)/shard_map/ppermute | solution.py:37
  110.0 5.1 %copy-start.10 = (f32[640,512]{1,0:T(8,128)S(1)}, f32[640,512]{1,0:T(8,128)}, u32[]{:S(2)}) copy-start(f32[640,512]{1,0:T(8,128)} %get-tuple-element.36.keep) | copy-start | bytes 3932164
  114.9 2.4 %collective-permute-start.12 = (f32[640,256]{1,0:T(8,128)}, f32[640,256]{1,0:T(8,128)S(1)}, u32[]{:S(2)}, u32[]{:S(2)}) collective-permute-start(f32[640,256]{1,0:T(8,128)} %get-tuple-element.35), channel_id=1, source_target_pairs={{0,1},{1,0},{2,3},{3,2},{4,5},{5,4},{6,7},{7,6},{8,9},{9,8},{10,11... | collective-permute-start | bytes 1966088 | tf_op jit(solution)/shard_map/ppermute | solution.py:37
  118.5 37.8 %copy-start.6 = (bf16[656,512]{1,0:T(8,128)(2,1)}, bf16[656,512]{1,0:T(8,128)(2,1)S(1)}, u32[]{:S(2)}) copy-start(bf16[656,512]{1,0:T(8,128)(2,1)S(1)} %get-tuple-element.41.own.refs_9_) | copy-start | bytes 2015236
  118.5 2.1 %collective-permute-start.14 = (bf16[656,512]{1,0:T(8,128)(2,1)S(1)}, bf16[656,512]{1,0:T(8,128)(2,1)S(1)}, u32[]{:S(2)}, u32[]{:S(2)}) collective-permute-start(bf16[656,512]{1,0:T(8,128)(2,1)S(1)} %get-tuple-element.41.own.refs_9_), channel_id=1, source_target_pairs={{0,1},{1,0},{2,3},{3,2},{4,5},{5,4},{6,7},{7,6},{8,9},{9,8},{10,11... | collective-permute-start | bytes 2015240 | tf_op jit(solution)/shard_map/ppermute | solution.py:37
  119.4 26.2 %collective-permute-start.18 = (bf16[640,256]{1,0:T(8,128)(2,1)}, bf16[640,256]{1,0:T(8,128)(2,1)}, u32[]{:S(2)}, u32[]{:S(2)}) collective-permute-start(bf16[640,256]{1,0:T(8,128)(2,1)} %get-tuple-element.42.refs_10_), channel_id=1, source_target_pairs={{0,1},{1,0},{2,3},{3,2},{4,5},{5,4},{6,7},{7,6},{8,9},{9,8},{10,11... | collective-permute-start | bytes 983048 | tf_op jit(solution)/shard_map/ppermute | solution.py:37
  120.6 12.6 %copy-start.7 = (bf16[656,512]{1,0:T(8,128)(2,1)}, bf16[656,512]{1,0:T(8,128)(2,1)S(1)}, u32[]{:S(2)}) copy-start(bf16[656,512]{1,0:T(8,128)(2,1)S(1)} %collective-permute-done.14.other.refs_9_) | copy-start | bytes 2015236
  125.3 17.8 %collective-permute-start.15 = (bf16[656,896]{1,0:T(8,128)(2,1)}, bf16[656,896]{1,0:T(8,128)(2,1)}, u32[]{:S(2)}, u32[]{:S(2)}) collective-permute-start(bf16[656,896]{1,0:T(8,128)(2,1)} %shard_map.121.refs_1_), channel_id=1, source_target_pairs={{0,6},{1,3},{2,4},{3,1},{4,2},{5,7},{6,0},{7,5},{8,14},{9,11},{10,... | collective-permute-start | bytes 3526664 | tf_op jit(solution)/shard_map/ppermute | solution.py:33
  132.1 31.2 %collective-permute-start.16 = (bf16[656,896]{1,0:T(8,128)(2,1)}, bf16[656,896]{1,0:T(8,128)(2,1)}, u32[]{:S(2)}, u32[]{:S(2)}) collective-permute-start(bf16[656,896]{1,0:T(8,128)(2,1)} %shard_map.122.refs_1_), channel_id=1, source_target_pairs={{0,6},{1,3},{2,4},{3,1},{4,2},{5,7},{6,0},{7,5},{8,14},{9,11},{10,... | collective-permute-start | bytes 3526664 | tf_op jit(solution)/shard_map/ppermute | solution.py:33
  145.6 20.6 %collective-permute-start.17 = (bf16[656,896]{1,0:T(8,128)(2,1)}, bf16[656,896]{1,0:T(8,128)(2,1)}, u32[]{:S(2)}, u32[]{:S(2)}) collective-permute-start(bf16[656,896]{1,0:T(8,128)(2,1)} %add_convert_fusion.refs_1_.refs_11_), channel_id=1, source_target_pairs={{0,2},{1,7},{2,0},{3,5},{4,6},{5,3},{6,4},{7,1},{8,10},{9,15},{10,... | collective-permute-start | bytes 3526664 | tf_op jit(solution)/shard_map/ppermute | solution.py:33
  145.6 10.7 %copy-start.5 = (s32[4]{0:T(128)S(1)}, s32[4]{0:T(128)}, u32[]{:S(2)}) copy-start(s32[4]{0:T(128)} %pad_add_fusion.place) | copy-start | bytes 52
  145.6 10.7 %copy-start.8 = (bf16[656,512]{1,0:T(8,128)(2,1)S(1)}, bf16[656,512]{1,0:T(8,128)(2,1)}, u32[]{:S(2)}) copy-start(bf16[656,512]{1,0:T(8,128)(2,1)} %copy-done.7) | copy-start | bytes 2015236
  155.7 19.5 %collective-permute-start.19 = (bf16[4,896,512]{2,1,0:T(8,128)(2,1)}, bf16[4,896,512]{2,1,0:T(8,128)(2,1)}, u32[]{:S(2)}, u32[]{:S(2)}) collective-permute-start(bf16[4,896,512]{2,1,0:T(8,128)(2,1)} %get-tuple-element.43), channel_id=1, source_target_pairs={{0,1},{1,0},{2,3},{3,2},{4,5},{5,4},{6,7},{7,6},{8,9},{9,8},{10,11... | collective-permute-start | bytes 11010056 | tf_op jit(solution)/shard_map/ppermute | solution.py:37
  155.8 19.4 %collective-permute-start.20 = (bf16[4,256,896]{2,1,0:T(8,128)(2,1)}, bf16[4,256,896]{2,1,0:T(8,128)(2,1)}, u32[]{:S(2)}, u32[]{:S(2)}) collective-permute-start(bf16[4,256,896]{2,1,0:T(8,128)(2,1)} %get-tuple-element.44), channel_id=1, source_target_pairs={{0,1},{1,0},{2,3},{3,2},{4,5},{5,4},{6,7},{7,6},{8,9},{9,8},{10,11... | collective-permute-start | bytes 5505032 | tf_op jit(solution)/shard_map/ppermute | solution.py:37
  169.7 27.7 %all-to-all-start.2 = ((bf16[16,40,1024]{2,1,0:T(8,128)(2,1)}), bf16[16,40,1024]{2,1,0:T(8,128)(2,1)}, u32[]{:S(2)}, u32[]{:S(2)}) async-start(bf16[16,40,1024]{2,1,0:T(8,128)(2,1)} %bitcast.14), calls=%async_computation.2 | async-start | bytes 2621440 | tf_op jit(solution)/shard_map/all_to_all | solution.py:451
  175.2 22.2 %copy-start.13 = (bf16[640,64]{1,0:T(8,128)(2,1)S(1)}, bf16[640,64]{1,0:T(8,128)(2,1)}, u32[]{:S(2)}) copy-start(bf16[640,64]{1,0:T(8,128)(2,1)} %copy-done.12) | copy-start | bytes 245764
  (8 other events, 11.7 us)

commit v5 on v4

--- a/solution.py
+++ b/solution.py
@@ -14,6 +14,8 @@
 MOST = 61
 DY_CUT = 512
 DY_REST = 896 - DY_CUT
+OUT_CUT = 640
+OUT_REST = 896 - OUT_CUT
 RATE = 3e10
 VMEM = pl.BlockSpec(memory_space=pltpu.VMEM)
 SMEM = pl.BlockSpec(memory_space=pltpu.SMEM)
@@ -93,25 +95,37 @@
 
 
 def second_dispatch_kernel(onehot, weights, dy, *refs):
-    rests, out = refs[:4], refs[4]
+    rests, out = refs[:2], refs[2]
     pick = onehot[...]
     out[:, :DY_CUT] = nn(pick, dy[:, :DY_CUT]).astype(BF)
     for k in range(4):
         lo = DY_CUT + DY_REST * k
-        out[:, lo : lo + DY_REST] = nn(pick, rests[k][...]).astype(BF)
+        out[:, lo : lo + DY_REST] = nn(pick, rests[k // 2][64 * (k % 2) : 64 * (k % 2) + 64, :]).astype(BF)
     out[:, -PAD:] = weights[...]
 
 
 def second_dispatch(onehot, weights, dy, rests):
     outs = [(VMEM, sds((ROWS, DY_CUT + 4 * DY_REST + PAD)))]
-    return call(second_dispatch_kernel, [VMEM] * 7, outs, us=3)(onehot, weights, dy, *rests)[0]
-
-
-def combine_kernel(back, onehot, ids, *refs):
+    return call(second_dispatch_kernel, [VMEM] * 5, outs, us=3)(onehot, weights, dy, *rests)[0]
+
+
+def first_combine_kernel(back, onehot, _, *outs):
+    pick = onehot[...]
+    for k in range(4):
+        outs[k // 2][64 * (k % 2) : 64 * (k % 2) + 64, :] = tn(pick, back[:, OUT_REST * k : OUT_REST * k + OUT_REST])
+
+
+def first_combine(back, onehot, later):
+    outs = [(VMEM, sds((128, OUT_REST), F32))] * 2
+    return call(first_combine_kernel, [VMEM] * 2 + [ANY], outs, us=2)(back, onehot, later)
+
+
+def combine_kernel(back, onehot, ids, one, two, *refs):
     grad, gate = refs[-2:]
     pick = onehot[...]
-    grad[...] = tn(pick, back[:, :COLS]).astype(BF)
-    sums = tn(pick, back[:, COLS:])
+    grad[:, :OUT_CUT] = tn(pick, back[:, :OUT_CUT]).astype(BF)
+    grad[:, OUT_CUT:] = (one[...] + two[...]).astype(BF)
+    sums = tn(pick, back[:, OUT_CUT:])
     lane = lax.broadcasted_iota(jnp.int32, (64, PAD), 1)
     total = jnp.zeros((64, PAD), F32)
     for k in range(8):
@@ -121,9 +135,9 @@
     gate[...] = total[:, :8]
 
 
-def combine(back, onehot, ids, later):
+def combine(back, onehot, ids, terms, later):
     outs = [(VMEM, sds((64, COLS))), (VMEM, sds((64, 8), F32))]
-    return call(combine_kernel, [VMEM] * 3 + [ANY], outs, us=3)(back, onehot, ids, later)
+    return call(combine_kernel, [VMEM] * 5 + [ANY], outs, us=3)(back, onehot, ids, *terms, later)
 
 
 def block(ref, i):
@@ -291,21 +305,41 @@
 
 def input_kernel(k, place, own, other, *refs):
     ws, (out, w, grads, sem) = refs[0], refs[-4:]
-    copy = pltpu.make_async_copy(block(ws, place[k]), w, sem)
+    start = pl.multiple_of(place[k] * COLS, COLS)
+    copy = pltpu.make_async_copy(ws.at[pl.ds(start, OUT_CUT), :], w, sem)
     copy.start()
     grads[:, : 2 * HID], grads[:, 2 * HID :] = own[:ROWS, :], other[:ROWS, :]
     tail = own[ROWS:, :].astype(F32) + other[ROWS:, :].astype(F32)
-    row = jnp.concatenate([tail[0:1, :], tail[1:2, :384]], axis=1)
-    out[ROWS:, :] = jnp.concatenate([row, jnp.zeros((TAIL - 1, COLS), F32)], axis=0).astype(BF)
+    row = jnp.concatenate([tail[0:1, :], tail[1:2, :128]], axis=1)
+    out[ROWS:, :] = jnp.concatenate([row, jnp.zeros((TAIL - 1, OUT_CUT), F32)], axis=0).astype(BF)
     copy.wait()
     out[:ROWS, :] = nt(grads[...], w[...]).astype(BF)
 
 
 def input_part(k, place, own, other, ws, *later):
-    scratch = [pltpu.VMEM((COLS, 4 * HID), BF), pltpu.VMEM((ROWS, 4 * HID), BF), pltpu.SemaphoreType.DMA]
-    outs = [(VMEM, sds((ROWS + TAIL, COLS)))]
+    scratch = [pltpu.VMEM((OUT_CUT, 4 * HID), BF), pltpu.VMEM((ROWS, 4 * HID), BF), pltpu.SemaphoreType.DMA]
+    outs = [(VMEM, sds((ROWS + TAIL, OUT_CUT)))]
     ins = [SMEM, VMEM, VMEM, HBM] + [ANY] * len(later)
     return call(functools.partial(input_kernel, k), ins, outs, scratch, us=4, mib=51)(place, own, other, ws, *later)[0]
+
+
+def rest_kernel(place, own, other, ws, _, out, w, grads, sems):
+    copies = []
+    for k in range(4):
+        start = pl.multiple_of(place[k] * COLS + OUT_CUT, 128)
+        copies.append(pltpu.make_async_copy(ws.at[pl.ds(start, OUT_REST), :], w.at[k], sems.at[k]))
+    for copy in copies:
+        copy.start()
+    grads[:, : 2 * HID], grads[:, 2 * HID :] = own[:ROWS, :], other[:ROWS, :]
+    for k in range(4):
+        copies[k].wait()
+        out[:, OUT_REST * k : OUT_REST * k + OUT_REST] = nt(grads[...], w[k]).astype(BF)
+
+
+def rest_parts(place, own, other, ws, later):
+    scratch = [pltpu.VMEM((4, OUT_REST, 4 * HID), BF), pltpu.VMEM((ROWS, 4 * HID), BF), pltpu.SemaphoreType.DMA((4,))]
+    outs = [(VMEM, sds((ROWS, 4 * OUT_REST)))]
+    return call(rest_kernel, [SMEM, VMEM, VMEM, HBM, ANY], outs, scratch, us=4, mib=51)(place, own, other, ws, later)[0]
 
 
 def stream(refs, buffer, sems):
@@ -424,15 +458,15 @@
     gates = sum(term[ROWS:, :].astype(F32) for term in terms)
     for i in range(ROWS // 128):
         rows = pl.ds(128 * i, 128)
-        out[rows, :COLS] = sum(term[rows, :].astype(F32) for term in terms).astype(BF)
+        out[rows, :OUT_CUT] = sum(term[rows, :].astype(F32) for term in terms).astype(BF)
         gate = jnp.broadcast_to(gates[0:1, 128 * i : 128 * i + 128], (128, 128)).T
         high = gate.astype(BF).astype(F32)
         spread = jnp.where(lane == expert[0], high, 0.0) + jnp.where(lane == expert[0] + 64, gate - high, 0.0)
-        out[rows, COLS:] = spread.astype(BF)
+        out[rows, OUT_CUT:] = spread.astype(BF)
 
 
 def total(expert, terms, *later):
-    outs = [(VMEM, sds((ROWS, COLS + PAD)))]
+    outs = [(VMEM, sds((ROWS, OUT_CUT + PAD)))]
     ins = [SMEM] + [VMEM] * 3 + [ANY] * len(later)
     return call(total_kernel, ins, outs)(expert, *terms, *later)[0]
 
@@ -468,8 +502,9 @@
     wg, wu, wd = wg[0], wu[0], wd[0]
 
     send_x, onehot, weights = dispatch(ids.T, gates.T.astype(F32), tokens)
-    rests = ring(cotangent[:, DY_CUT:])
-    rests.append(meet(rests[1], 1))
+    pair = cotangent[:, DY_CUT:]
+    pair = jnp.concatenate([pair, meet(pair, 0)])
+    rests = [pair, meet(pair, 1)]
     send_dy = second_dispatch(onehot, weights, cotangent, rests)
     ws = (wg, wu, swap(wg), swap(wu))
     ds = (wd, swap(wd))
@@ -494,6 +529,7 @@
 
     opposite = part(3)
     near = part(2, opposite)
+    rest_back = exchange(rest_parts(place, dab, dab_other, ws, near))
     own = part(1, near)
     opposite, near = meet(opposite, 1), meet(near, 1)
     own = add(own, opposite)
@@ -503,7 +539,10 @@
     columns, rows = swap(columns), swap(rows)
     share = total(expert, (part(0, own), near, rest))
     gate_grad, up_grad, down_grad, done = own_gradients(place, other_place, xs, dys, came, dab, hs, columns, rows, share)
-    input_grad, slot_grad = combine(exchange(share), onehot, ids, done)
+    ends = first_combine(rest_back, onehot, share)
+    ends = ends[0] + meet(ends[1], 1)
+    ends = (ends[:64], meet(ends[64:], 0))
+    input_grad, slot_grad = combine(exchange(share), onehot, ids, ends, done)
     return input_grad, slot_grad, gate_grad[None], up_grad[None], down_grad[None]
 
 

time: 203 us -> 201 us (level)
  waiting for transfers between devices: 62.8 us -> 46.7 us
  starting transfers between devices: 37.7 us -> 46.9 us
  Pallas kernels: 85.9 us -> 90.7 us
    ppermute x12 -> x13, waiting for transfers between devices: 25.2 us -> 13.2 us  [meet(): return lax.ppermute(v, ('y', 'core'), MEET[step])]
    all_to_all x3 -> x4, starting transfers between devices: 18 us -> 27.7 us  [exchange(): lax.all_to_all(v.reshape(16, ROOM, -1), ('x', 'z'), 0, 0, tiled=True)]
    pallas_call x2 -> x4, Pallas kernels: 3.27 us -> 11 us  [the longest x1 6.11 us: rest_parts(): call(rest_kernel, [SMEM, VMEM, VMEM, HBM, ANY], outs, scratch, us=4, mib=51)]
    all_to_all x3 -> x4, waiting for transfers between devices: 34.8 us -> 29.9 us  [exchange(): lax.all_to_all(v.reshape(16, ROOM, -1), ('x', 'z'), 0, 0, tiled=True)]
    pallas_call x4, Pallas kernels: 16.4 us -> 14.1 us  [input_part(): call(functools.partial(input_kernel, k), ins, outs, scratch, us=4, mib=51)]
    ppermute x12 -> x13, starting transfers between devices: 17.9 us -> 16.5 us  [meet(): return lax.ppermute(v, ('y', 'core'), MEET[step])]
    unnamed x34 -> x36, local copies, waits for them, and re-layouts: 5.56 us -> 5.58 us
  transfers between devices with their start and end apart: 24 -> 26, of which waited for: 12 -> 9; matrix products, arithmetic and copies ran while one was open for 4% -> 4% of each run, Pallas kernels for 41% -> 44%
where the time goes in v5:
time: 201 us; the launch traced here: 199 us
  Pallas kernels  90.7 us (45%)
  starting transfers between devices  46.9 us (23%)
  waiting for transfers between devices  46.7 us (23%)
  local copies, waits for them, and re-layouts  9.93 us (5%)
  other arithmetic  4.23 us (2%)
    all_to_all x4, waiting for transfers between devices, exchange(): lax.all_to_all(v.reshape(16, ROOM, -1), ('x', 'z'), 0, 0, tiled=True)  29.9 us
    all_to_all x4, starting transfers between devices, exchange(): lax.all_to_all(v.reshape(16, ROOM, -1), ('x', 'z'), 0, 0, tiled=True)  27.7 us
    ppermute x13, starting transfers between devices, meet(): return lax.ppermute(v, ('y', 'core'), MEET[step])  16.5 us
    pallas_call x1, Pallas kernels, pack(): call(pack_kernel, [HBM] * 6, outs, scratch, us=13, mib=MOST)(*weights)  14.6 us
    pallas_call x4, Pallas kernels, input_part(): call(functools.partial(input_kernel, k), ins, outs, scratch, us=4, mib=51)  14.1 us
    ppermute x13, waiting for transfers between devices, meet(): return lax.ppermute(v, ('y', 'core'), MEET[step])  13.2 us
    pallas_call x1, Pallas kernels, own_gradients(): kernel(place, other_place, *xs, *dys, came, dab, hs, columns, rows, later)  12.3 us
    pallas_call x1, Pallas kernels, other_gradients(): call(other_gradient_kernel, ins, outs, scratch, us=10, mib=MOST)  10.1 us
  transfers between devices with their start and end apart: 26, of which 9 were waited for; matrix products, arithmetic and copies ran while one was open for 4% of the time, Pallas kernels for 44%

profile of v5, /device:TPU:0, one launch (start us, length us, event | category | flops | bytes accessed | tf_op | source)
XLA Modules:
  0.0 199.4 jit_solution(12117026409164188927)
XLA Ops:
  1.4 1.7 collective-permute-start
  6.9 7.9 %all-to-all-start = ((bf16[16,40,896]{2,1,0:T(8,128)(2,1)}), bf16[16,40,896]{2,1,0:T(8,128)(2,1)S(1)}, u32[]{:S(2)}, u32[]{:S(2)}) async-start(bf16[16,40,896]{2,1,0:T(8,128)(2,1)} %bitcast.7), calls=%async_computation | async-start | bytes 2293760 | tf_op jit(solution)/shard_map/all_to_all | solution.py:485
  18.4 3.6 %collective-permute-done.1.refs_1_ = bf16[128,384]{1,0:T(8,128)(2,1)S(1)} collective-permute-done((bf16[128,384]{1,0:T(8,128)(2,1)S(1)}, bf16[128,384]{1,0:T(8,128)(2,1)S(1)}, u32[]{:S(2)}, u32[]{:S(2)}) %collective-permute-start.1) | collective-permute-done | bytes 98336 | tf_op jit(solution)/shard_map/ppermute | solution.py:35
  24.4 11.1 %all-to-all-done = bf16[16,40,896]{2,1,0:T(8,128)(2,1)S(1)} async-done(((bf16[16,40,896]{2,1,0:T(8,128)(2,1)}), bf16[16,40,896]{2,1,0:T(8,128)(2,1)S(1)}, u32[]{:S(2)}, u32[]{:S(2)}) %all-to-all-start) | async-done | bytes 1146912 | tf_op jit(solution)/shard_map/all_to_all | solution.py:485
  36.6 6.2 %all-to-all-start.1 = ((bf16[16,40,2176]{2,1,0:T(8,128)(2,1)}), bf16[16,40,2176]{2,1,0:T(8,128)(2,1)}, u32[]{:S(2)}, u32[]{:S(2)}) async-start(bf16[16,40,2176]{2,1,0:T(8,128)(2,1)} %bitcast.26), calls=%async_computation.1 | async-start | bytes 5570560 | tf_op jit(solution)/shard_map/all_to_all | solution.py:485
  42.8 14.6 %shard_map.115 = (bf16[7168,1024]{1,0:T(8,128)(2,1)}, bf16[512,7168]{1,0:T(8,128)(2,1)}) custom-call(bf16[7168,256]{1,0:T(8,128)(2,1)} %bitcast.31, bf16[7168,256]{1,0:T(8,128)(2,1)} %bitcast.33, bf16[7168,256]{1,0:T(8,128)(2,1)} %collective-permute-done.2.refs_1_.refs_2_, bf16[7168,256]{1,0:T(8,128)(2,1)} %collective-permute-done.3.refs_2_.refs_3_, ...), custom_call_target="tpu_custom_call" | custom-call | flops 389999984640 | bytes 10000 | tf_op jit(solution)/shard_map/pallas_call | solution.py:170
  57.5 6.0 %collective-permute-done.8.refs_1_ = bf16[640,896]{1,0:T(8,128)(2,1)} collective-permute-done((bf16[640,896]{1,0:T(8,128)(2,1)}, bf16[640,896]{1,0:T(8,128)(2,1)}, u32[]{:S(2)}, u32[]{:S(2)}) %collective-permute-start.8) | collective-permute-done | bytes 1146912 | tf_op jit(solution)/shard_map/ppermute | solution.py:35
  63.5 16.8 %all-to-all-done.1 = bf16[16,40,2176]{2,1,0:T(8,128)(2,1)} async-done(((bf16[16,40,2176]{2,1,0:T(8,128)(2,1)}), bf16[16,40,2176]{2,1,0:T(8,128)(2,1)}, u32[]{:S(2)}, u32[]{:S(2)}) %all-to-all-start.1) | async-done | bytes 2785312 | tf_op jit(solution)/shard_map/all_to_all | solution.py:485
  80.3 2.0 slice.20.d0.refs_4_
  83.4 3.3 %collective-permute-start.6 = (bf16[640,512]{1,0:T(8,128)(2,1)}, bf16[640,512]{1,0:T(8,128)(2,1)}, u32[]{:S(2)}, u32[]{:S(2)}) collective-permute-start(bf16[640,512]{1,0:T(8,128)(2,1)} %slice.20.d0.refs_4_), channel_id=1, source_target_pairs={{0,6},{1,3},{2,4},{3,1},{4,2},{5,7},{6,0},{7,5},{8,14},{9,11},{10,... | collective-permute-start | bytes 1966088 | tf_op jit(solution)/shard_map/ppermute | solution.py:35
  86.7 8.6 %shard_map.116.refs_2_ = f32[640,1024]{1,0:T(8,128)} custom-call(s32[4]{0:T(128)} %pad_add_fusion.place, bf16[640,896]{1,0:T(8,128)(2,1)} %shard_map.112.refs_1_.refs_0_, bf16[640,896]{1,0:T(8,128)(2,1)} %collective-permute-done.8.refs_1_, bf16[640,896]{1,0:T(8,128)(2,1)} %collective-permute-done.10.refs_2_, ...), custom_call_target="tpu_custom_call" | custom-call | flops 240000008192 | bytes 10000 | tf_op jit(solution)/shard_map/pallas_call | solution.py:205
  96.2 1.9 collective-permute-done.5.refs_0_
  99.6 9.0 %shard_map.117 = (f32[640,512]{1,0:T(8,128)}, f32[640,512]{1,0:T(8,128)}, f32[640,512]{1,0:T(8,128)}) custom-call(s32[4]{0:T(128)} %pad_add_fusion.place, bf16[640,896]{1,0:T(8,128)(2,1)} %collective-permute-done.9.x_last.refs_3_, bf16[640,512]{1,0:T(8,128)(2,1)} %slice.20.d0.refs_4_, bf16[640,512]{1,0:T(8,128)(2,1)} %shard_map.114.d1.refs_5_, ...), custom_call_target="tpu_custom_call" | custom-call | flops 359999995904 | bytes 10000 | tf_op jit(solution)/shard_map/pallas_call | solution.py:251
  110.3 4.9 %shard_map.118 = (f32[640,256]{1,0:T(8,128)}, f32[640,256]{1,0:T(8,128)}) custom-call(s32[4]{0:T(128)} %pad_add_fusion.place, bf16[640,512]{1,0:T(8,128)(2,1)} %collective-permute-done.7.refs_0_.refs_7_, bf16[640,2176]{1,0:T(8,128)(2,1)} %bitcast.13.came.refs_1_.refs_8_, bf16[512,7168]{1,0:T(8,128)(2,1)} %get-tuple-element.33.refs_1_.refs_2_, ...), custom_call_target="tpu_custom_call" | custom-call | flops 89999998976 | bytes 10000 | tf_op jit(solution)/shard_map/pallas_call | solution.py:283
  115.7 1.9 collective-permute-done.11.came
  120.9 4.0 %shard_map.121.refs_1_ = bf16[656,640]{1,0:T(8,128)(2,1)} custom-call(s32[4]{0:T(128)S(1)} %copy-done.4, bf16[656,512]{1,0:T(8,128)(2,1)S(1)} %get-tuple-element.43.own.refs_9_, bf16[656,512]{1,0:T(8,128)(2,1)S(1)} %collective-permute-done.13.other.refs_9_, bf16[7168,1024]{1,0:T(8,128)(2,1)} %get-tuple-element.34.refs_3_.refs_0_.ws), custom_call_target="tpu_custom_call" | custom-call | flops 120000004096 | bytes 10000 | tf_op jit(solution)/shard_map/pallas_call | solution.py:323
  124.9 1.7 collective-permute-start.14
  126.5 4.0 %shard_map.122.refs_1_._ = bf16[656,640]{1,0:T(8,128)(2,1)} custom-call(s32[4]{0:T(128)S(1)} %copy-done.4, bf16[656,512]{1,0:T(8,128)(2,1)S(1)} %get-tuple-element.43.own.refs_9_, bf16[656,512]{1,0:T(8,128)(2,1)S(1)} %collective-permute-done.13.other.refs_9_, bf16[7168,1024]{1,0:T(8,128)(2,1)} %get-tuple-element.34.refs_3_.refs_0_.ws, ...), custom_call_target="tpu_custom_call" | custom-call | flops 120000004096 | bytes 10000 | tf_op jit(solution)/shard_map/pallas_call | solution.py:323
  130.5 1.9 collective-permute-start.15
  132.5 6.1 %shard_map.126 = bf16[640,1024]{1,0:T(8,128)(2,1)} custom-call(s32[4]{0:T(128)S(1)} %copy-done.4, bf16[656,512]{1,0:T(8,128)(2,1)S(1)} %get-tuple-element.43.own.refs_9_, bf16[656,512]{1,0:T(8,128)(2,1)S(1)} %collective-permute-done.13.other.refs_9_, bf16[7168,1024]{1,0:T(8,128)(2,1)} %get-tuple-element.34.refs_3_.refs_0_.ws, ...), custom_call_target="tpu_custom_call" | custom-call | flops 120000004096 | bytes 10000 | tf_op jit(solution)/shard_map/pallas_call | solution.py:342
  138.6 6.4 %all-to-all-start.3 = ((bf16[16,40,1024]{2,1,0:T(8,128)(2,1)}), bf16[16,40,1024]{2,1,0:T(8,128)(2,1)}, u32[]{:S(2)}, u32[]{:S(2)}) async-start(bf16[16,40,1024]{2,1,0:T(8,128)(2,1)} %bitcast.29), calls=%async_computation.3 | async-start | bytes 2621440 | tf_op jit(solution)/shard_map/all_to_all | solution.py:485
  145.0 3.1 %shard_map.123 = bf16[656,640]{1,0:T(8,128)(2,1)S(1)} custom-call(s32[4]{0:T(128)S(1)} %copy-done.4, bf16[656,512]{1,0:T(8,128)(2,1)S(1)} %get-tuple-element.43.own.refs_9_, bf16[656,512]{1,0:T(8,128)(2,1)S(1)} %collective-permute-done.13.other.refs_9_, bf16[7168,1024]{1,0:T(8,128)(2,1)} %get-tuple-element.34.refs_3_.refs_0_.ws, ...), custom_call_target="tpu_custom_call" | custom-call | flops 120000004096 | bytes 10000 | tf_op jit(solution)/shard_map/pallas_call | solution.py:323
  148.1 2.3 %add_convert_fusion.refs_1_.refs_11_ = bf16[656,640]{1,0:T(8,128)(2,1)} fusion(bf16[656,640]{1,0:T(8,128)(2,1)} %collective-permute-done.14, bf16[656,640]{1,0:T(8,128)(2,1)S(1)} %shard_map.123), kind=kLoop, calls=%fused_computation | loop fusion | flops 1679360 | bytes 2519040 | tf_op jit(solution)/shard_map/convert_element_type | solution.py:493
  150.4 10.1 %shard_map.128 = (bf16[4,896,512]{2,1,0:T(8,128)(2,1)}, bf16[4,256,896]{2,1,0:T(8,128)(2,1)}) custom-call(bf16[640,896]{1,0:T(8,128)(2,1)} %shard_map.112.refs_1_.refs_0_, bf16[640,896]{1,0:T(8,128)(2,1)} %collective-permute-done.8.refs_1_, bf16[640,896]{1,0:T(8,128)(2,1)} %collective-permute-done.10.refs_2_, ...), custom_call_target="tpu_custom_call" | custom-call | flops 299999985664 | bytes 10000 | tf_op jit(solution)/shard_map/pallas_call | solution.py:400
  161.0 3.1 %shard_map.124.refs_0_ = bf16[656,640]{1,0:T(8,128)(2,1)S(1)} custom-call(s32[4]{0:T(128)S(1)} %copy-done.5, bf16[656,512]{1,0:T(8,128)(2,1)S(1)} %get-tuple-element.43.own.refs_9_, bf16[656,512]{1,0:T(8,128)(2,1)S(1)} %copy-done.8, bf16[7168,1024]{1,0:T(8,128)(2,1)} %get-tuple-element.34.refs_3_.refs_0_.ws, bf16[656,640]{1,0:T(8,128)(2,1)} %add_convert_fusion.refs_1_.refs_11_), custom_call_target="tpu_custom_call" | custom-call | flops 120000004096 | bytes 10000 | tf_op jit(solution)/shard_map/pallas_call | solution.py:323
  164.2 3.0 %shard_map.125._.refs_13_ = bf16[640,768]{1,0:T(8,128)(2,1)} custom-call(s32[1]{0:T(128)} %bitcast.expert, bf16[656,640]{1,0:T(8,128)(2,1)S(1)} %shard_map.124.refs_0_, bf16[656,640]{1,0:T(8,128)(2,1)} %collective-permute-done.15.refs_1_, bf16[656,640]{1,0:T(8,128)(2,1)} %collective-permute-done.16.refs_2_), custom_call_target="tpu_custom_call" | custom-call | flops 30000001024 | bytes 10000 | tf_op jit(solution)/shard_map/pallas_call | solution.py:471
  167.1 1.7 shard_map.127
  168.8 2.4 %collective-permute-start.17 = (f32[128,256]{1,0:T(8,128)S(1)}, f32[128,256]{1,0:T(8,128)S(1)}, u32[]{:S(2)}, u32[]{:S(2)}) collective-permute-start(f32[128,256]{1,0:T(8,128)S(1)} %get-tuple-element.45), channel_id=1, source_target_pairs={{0,6},{1,3},{2,4},{3,1},{4,2},{5,7},{6,0},{7,5},{8,14},{9,11},{10,... | collective-permute-start | bytes 393224 | tf_op jit(solution)/shard_map/ppermute | solution.py:35
  172.0 7.2 %all-to-all-start.2 = ((bf16[16,40,768]{2,1,0:T(8,128)(2,1)}), bf16[16,40,768]{2,1,0:T(8,128)(2,1)}, u32[]{:S(2)}, u32[]{:S(2)}) async-start(bf16[16,40,768]{2,1,0:T(8,128)(2,1)} %bitcast.14), calls=%async_computation.2 | async-start | bytes 1966080 | tf_op jit(solution)/shard_map/all_to_all | solution.py:485
  181.3 12.3 %shard_map.129 = (bf16[7168,256]{1,0:T(8,128)(2,1)}, bf16[7168,256]{1,0:T(8,128)(2,1)}, bf16[256,7168]{1,0:T(8,128)(2,1)}, f32[8,128]{1,0:T(8,128)}) custom-call(s32[4]{0:T(128)} %pad_add_fusion.place, s32[4]{0:T(128)} %pad_add_fusion.1.other_place, bf16[640,896]{1,0:T(8,128)(2,1)} %shard_map.112.refs_1_.refs_0_, ...), custom_call_target="tpu_custom_call" | custom-call | flops 359999995904 | bytes 10000 | tf_op jit(solution)/shard_map/pallas_call | solution.py:452
  193.7 2.0 all-to-all-done.2
  196.3 2.4 %shard_map.130 = (bf16[64,896]{1,0:T(8,128)(2,1)}, f32[64,8]{1,0:T(8,128)S(1)}) custom-call(bf16[640,768]{1,0:T(8,128)(2,1)} %bitcast.15.back, bf16[640,64]{1,0:T(8,128)(2,1)S(1)} %copy-done.14, s32[64,8]{1,0:T(8,128)S(1)} %copy.15.ids, f32[64,256]{1,0:T(8,128)S(1)} %get-tuple-element.61.one, f32[64,256]{1,0:T(8,128)} %collective-permute-done.18.two, ...), custom_call_target="tpu_custom_call" | custom-call | flops 89999998976 | bytes 10000 | tf_op jit(solution)/shard_map/pallas_call | solution.py:140
  (87 shorter events, 25.2 us)
Async XLA Ops:
  1.4 14.7 %collective-permute-start = (bf16[64,384]{1,0:T(8,128)(2,1)S(1)}, bf16[64,384]{1,0:T(8,128)(2,1)S(1)}, u32[]{:S(2)}, u32[]{:S(2)}) collective-permute-start(bf16[64,384]{1,0:T(8,128)(2,1)S(1)} %slice.15), channel_id=1, source_target_pairs={{0,2},{1,7},{2,0},{3,5},{4,6},{5,3},{6,4},{7,1},{8,10},{9,15},{10,... | collective-permute-start | bytes 147464 | tf_op jit(solution)/shard_map/ppermute | solution.py:35
  5.4 16.7 %copy-start.1 = (bf16[64,896]{1,0:T(8,128)(2,1)S(1)}, bf16[64,896]{1,0:T(8,128)(2,1)}, u32[]{:S(2)}) copy-start(bf16[64,896]{1,0:T(8,128)(2,1)} %dy.1) | copy-start | bytes 344068
  6.9 15.9 %copy-start.12 = (bf16[640,64]{1,0:T(8,128)(2,1)}, bf16[640,64]{1,0:T(8,128)(2,1)S(1)}, u32[]{:S(2)}) copy-start(bf16[640,64]{1,0:T(8,128)(2,1)S(1)} %get-tuple-element.30.onehot) | copy-start | bytes 245764
  6.9 28.6 %all-to-all-start = ((bf16[16,40,896]{2,1,0:T(8,128)(2,1)}), bf16[16,40,896]{2,1,0:T(8,128)(2,1)S(1)}, u32[]{:S(2)}, u32[]{:S(2)}) async-start(bf16[16,40,896]{2,1,0:T(8,128)(2,1)} %bitcast.7), calls=%async_computation | async-start | bytes 2293760 | tf_op jit(solution)/shard_map/all_to_all | solution.py:485
  14.8 20.7 %collective-permute-start.2 = (bf16[7168,256]{1,0:T(8,128)(2,1)}, bf16[7168,256]{1,0:T(8,128)(2,1)}, u32[]{:S(2)}, u32[]{:S(2)}) collective-permute-start(bf16[7168,256]{1,0:T(8,128)(2,1)} %bitcast.30), channel_id=1, source_target_pairs={{0,1},{1,0},{2,3},{3,2},{4,5},{5,4},{6,7},{7,6},{8,9},{9,8},{10,11... | collective-permute-start | bytes 11010056 | tf_op jit(solution)/shard_map/ppermute | solution.py:39
  15.6 20.0 %collective-permute-start.3 = (bf16[7168,256]{1,0:T(8,128)(2,1)}, bf16[7168,256]{1,0:T(8,128)(2,1)}, u32[]{:S(2)}, u32[]{:S(2)}) collective-permute-start(bf16[7168,256]{1,0:T(8,128)(2,1)} %bitcast.32), channel_id=1, source_target_pairs={{0,1},{1,0},{2,3},{3,2},{4,5},{5,4},{6,7},{7,6},{8,9},{9,8},{10,11... | collective-permute-start | bytes 11010056 | tf_op jit(solution)/shard_map/ppermute | solution.py:39
  15.7 19.9 %collective-permute-start.4 = (bf16[256,7168]{1,0:T(8,128)(2,1)}, bf16[256,7168]{1,0:T(8,128)(2,1)}, u32[]{:S(2)}, u32[]{:S(2)}) collective-permute-start(bf16[256,7168]{1,0:T(8,128)(2,1)} %bitcast.34), channel_id=1, source_target_pairs={{0,1},{1,0},{2,3},{3,2},{4,5},{5,4},{6,7},{7,6},{8,9},{9,8},{10,11... | collective-permute-start | bytes 11010056 | tf_op jit(solution)/shard_map/ppermute | solution.py:39
  16.2 5.9 %collective-permute-start.1 = (bf16[128,384]{1,0:T(8,128)(2,1)S(1)}, bf16[128,384]{1,0:T(8,128)(2,1)S(1)}, u32[]{:S(2)}, u32[]{:S(2)}) collective-permute-start(bf16[128,384]{1,0:T(8,128)(2,1)S(1)} %pad_maximum_fusion.refs_0_), channel_id=1, source_target_pairs={{0,6},{1,3},{2,4},{3,1},{4,2},{5,7},{6,0},{7,5},{8,14},{9,11},{10,... | collective-permute-start | bytes 294920 | tf_op jit(solution)/shard_map/ppermute | solution.py:35
  36.6 26.9 %collective-permute-start.8 = (bf16[640,896]{1,0:T(8,128)(2,1)}, bf16[640,896]{1,0:T(8,128)(2,1)}, u32[]{:S(2)}, u32[]{:S(2)}) collective-permute-start(bf16[640,896]{1,0:T(8,128)(2,1)} %shard_map.112.refs_1_.refs_0_), channel_id=1, source_target_pairs={{0,2},{1,7},{2,0},{3,5},{4,6},{5,3},{6,4},{7,1},{8,10},{9,15},{10,... | collective-permute-start | bytes 3440648 | tf_op jit(solution)/shard_map/ppermute | solution.py:35
  36.6 50.1 %collective-permute-start.10 = (bf16[640,896]{1,0:T(8,128)(2,1)}, bf16[640,896]{1,0:T(8,128)(2,1)}, u32[]{:S(2)}, u32[]{:S(2)}) collective-permute-start(bf16[640,896]{1,0:T(8,128)(2,1)} %shard_map.112.refs_1_.refs_0_), channel_id=1, source_target_pairs={{0,6},{1,3},{2,4},{3,1},{4,2},{5,7},{6,0},{7,5},{8,14},{9,11},{10,... | collective-permute-start | bytes 3440648 | tf_op jit(solution)/shard_map/ppermute | solution.py:35
  36.6 43.7 %all-to-all-start.1 = ((bf16[16,40,2176]{2,1,0:T(8,128)(2,1)}), bf16[16,40,2176]{2,1,0:T(8,128)(2,1)}, u32[]{:S(2)}, u32[]{:S(2)}) async-start(bf16[16,40,2176]{2,1,0:T(8,128)(2,1)} %bitcast.26), calls=%async_computation.1 | async-start | bytes 5570560 | tf_op jit(solution)/shard_map/all_to_all | solution.py:485
  63.5 36.1 %collective-permute-start.9 = (bf16[640,896]{1,0:T(8,128)(2,1)}, bf16[640,896]{1,0:T(8,128)(2,1)}, u32[]{:S(2)}, u32[]{:S(2)}) collective-permute-start(bf16[640,896]{1,0:T(8,128)(2,1)} %collective-permute-done.8.refs_1_), channel_id=1, source_target_pairs={{0,6},{1,3},{2,4},{3,1},{4,2},{5,7},{6,0},{7,5},{8,14},{9,11},{10,... | collective-permute-start | bytes 3440648 | tf_op jit(solution)/shard_map/ppermute | solution.py:35
  82.3 15.9 %collective-permute-start.5 = (bf16[640,512]{1,0:T(8,128)(2,1)}, bf16[640,512]{1,0:T(8,128)(2,1)}, u32[]{:S(2)}, u32[]{:S(2)}) collective-permute-start(bf16[640,512]{1,0:T(8,128)(2,1)} %slice.20.d0.refs_4_), channel_id=1, source_target_pairs={{0,2},{1,7},{2,0},{3,5},{4,6},{5,3},{6,4},{7,1},{8,10},{9,15},{10,... | collective-permute-start | bytes 1966088 | tf_op jit(solution)/shard_map/ppermute | solution.py:35
  83.4 14.8 %collective-permute-start.6 = (bf16[640,512]{1,0:T(8,128)(2,1)}, bf16[640,512]{1,0:T(8,128)(2,1)}, u32[]{:S(2)}, u32[]{:S(2)}) collective-permute-start(bf16[640,512]{1,0:T(8,128)(2,1)} %slice.20.d0.refs_4_), channel_id=1, source_target_pairs={{0,6},{1,3},{2,4},{3,1},{4,2},{5,7},{6,0},{7,5},{8,14},{9,11},{10,... | collective-permute-start | bytes 1966088 | tf_op jit(solution)/shard_map/ppermute | solution.py:35
  98.2 12.1 %collective-permute-start.7 = (bf16[640,512]{1,0:T(8,128)(2,1)}, bf16[640,512]{1,0:T(8,128)(2,1)}, u32[]{:S(2)}, u32[]{:S(2)}) collective-permute-start(bf16[640,512]{1,0:T(8,128)(2,1)} %shard_map.114.d1.refs_5_), channel_id=1, source_target_pairs={{0,6},{1,3},{2,4},{3,1},{4,2},{5,7},{6,0},{7,5},{8,14},{9,11},{10,... | collective-permute-start | bytes 1966088 | tf_op jit(solution)/shard_map/ppermute | solution.py:35
  108.6 6.7 %collective-permute-start.12 = (f32[640,512]{1,0:T(8,128)}, f32[640,512]{1,0:T(8,128)S(1)}, u32[]{:S(2)}, u32[]{:S(2)}) collective-permute-start(f32[640,512]{1,0:T(8,128)} %get-tuple-element.39), channel_id=1, source_target_pairs={{0,1},{1,0},{2,3},{3,2},{4,5},{5,4},{6,7},{7,6},{8,9},{9,8},{10,11... | collective-permute-start | bytes 3932168 | tf_op jit(solution)/shard_map/ppermute | solution.py:39
  115.2 2.4 %collective-permute-start.11 = (f32[640,256]{1,0:T(8,128)}, f32[640,256]{1,0:T(8,128)S(1)}, u32[]{:S(2)}, u32[]{:S(2)}) collective-permute-start(f32[640,256]{1,0:T(8,128)} %get-tuple-element.37), channel_id=1, source_target_pairs={{0,1},{1,0},{2,3},{3,2},{4,5},{5,4},{6,7},{7,6},{8,9},{9,8},{10,11... | collective-permute-start | bytes 1966088 | tf_op jit(solution)/shard_map/ppermute | solution.py:39
  118.8 42.3 %copy-start.6 = (bf16[656,512]{1,0:T(8,128)(2,1)}, bf16[656,512]{1,0:T(8,128)(2,1)S(1)}, u32[]{:S(2)}) copy-start(bf16[656,512]{1,0:T(8,128)(2,1)S(1)} %get-tuple-element.43.own.refs_9_) | copy-start | bytes 2015236
  118.8 2.1 %collective-permute-start.13 = (bf16[656,512]{1,0:T(8,128)(2,1)S(1)}, bf16[656,512]{1,0:T(8,128)(2,1)S(1)}, u32[]{:S(2)}, u32[]{:S(2)}) collective-permute-start(bf16[656,512]{1,0:T(8,128)(2,1)S(1)} %get-tuple-element.43.own.refs_9_), channel_id=1, source_target_pairs={{0,1},{1,0},{2,3},{3,2},{4,5},{5,4},{6,7},{7,6},{8,9},{9,8},{10,11... | collective-permute-start | bytes 2015240 | tf_op jit(solution)/shard_map/ppermute | solution.py:39
  118.9 31.5 %collective-permute-start.19 = (bf16[640,256]{1,0:T(8,128)(2,1)}, bf16[640,256]{1,0:T(8,128)(2,1)}, u32[]{:S(2)}, u32[]{:S(2)}) collective-permute-start(bf16[640,256]{1,0:T(8,128)(2,1)} %get-tuple-element.46.refs_10_), channel_id=1, source_target_pairs={{0,1},{1,0},{2,3},{3,2},{4,5},{5,4},{6,7},{7,6},{8,9},{9,8},{10,11... | collective-permute-start | bytes 983048 | tf_op jit(solution)/shard_map/ppermute | solution.py:39
  120.9 24.1 %copy-start.7 = (bf16[656,512]{1,0:T(8,128)(2,1)}, bf16[656,512]{1,0:T(8,128)(2,1)S(1)}, u32[]{:S(2)}) copy-start(bf16[656,512]{1,0:T(8,128)(2,1)S(1)} %collective-permute-done.13.other.refs_9_) | copy-start | bytes 2015236
  124.9 23.2 %collective-permute-start.14 = (bf16[656,640]{1,0:T(8,128)(2,1)}, bf16[656,640]{1,0:T(8,128)(2,1)}, u32[]{:S(2)}, u32[]{:S(2)}) collective-permute-start(bf16[656,640]{1,0:T(8,128)(2,1)} %shard_map.121.refs_1_), channel_id=1, source_target_pairs={{0,6},{1,3},{2,4},{3,1},{4,2},{5,7},{6,0},{7,5},{8,14},{9,11},{10,... | collective-permute-start | bytes 2519048 | tf_op jit(solution)/shard_map/ppermute | solution.py:35
  130.5 33.6 %collective-permute-start.15 = (bf16[656,640]{1,0:T(8,128)(2,1)}, bf16[656,640]{1,0:T(8,128)(2,1)}, u32[]{:S(2)}, u32[]{:S(2)}) collective-permute-start(bf16[656,640]{1,0:T(8,128)(2,1)} %shard_map.122.refs_1_._), channel_id=1, source_target_pairs={{0,6},{1,3},{2,4},{3,1},{4,2},{5,7},{6,0},{7,5},{8,14},{9,11},{10,... | collective-permute-start | bytes 2519048 | tf_op jit(solution)/shard_map/ppermute | solution.py:35
  138.6 28.6 %all-to-all-start.3 = ((bf16[16,40,1024]{2,1,0:T(8,128)(2,1)}), bf16[16,40,1024]{2,1,0:T(8,128)(2,1)}, u32[]{:S(2)}, u32[]{:S(2)}) async-start(bf16[16,40,1024]{2,1,0:T(8,128)(2,1)} %bitcast.29), calls=%async_computation.3 | async-start | bytes 2621440 | tf_op jit(solution)/shard_map/all_to_all | solution.py:485
  150.4 13.8 %collective-permute-start.16 = (bf16[656,640]{1,0:T(8,128)(2,1)}, bf16[656,640]{1,0:T(8,128)(2,1)}, u32[]{:S(2)}, u32[]{:S(2)}) collective-permute-start(bf16[656,640]{1,0:T(8,128)(2,1)} %add_convert_fusion.refs_1_.refs_11_), channel_id=1, source_target_pairs={{0,2},{1,7},{2,0},{3,5},{4,6},{5,3},{6,4},{7,1},{8,10},{9,15},{10,... | collective-permute-start | bytes 2519048 | tf_op jit(solution)/shard_map/ppermute | solution.py:35
  150.4 10.7 %copy-start.5 = (s32[4]{0:T(128)S(1)}, s32[4]{0:T(128)}, u32[]{:S(2)}) copy-start(s32[4]{0:T(128)} %pad_add_fusion.place) | copy-start | bytes 52
  160.4 20.9 %collective-permute-start.20 = (bf16[4,896,512]{2,1,0:T(8,128)(2,1)}, bf16[4,896,512]{2,1,0:T(8,128)(2,1)}, u32[]{:S(2)}, u32[]{:S(2)}) collective-permute-start(bf16[4,896,512]{2,1,0:T(8,128)(2,1)} %get-tuple-element.47), channel_id=1, source_target_pairs={{0,1},{1,0},{2,3},{3,2},{4,5},{5,4},{6,7},{7,6},{8,9},{9,8},{10,11... | collective-permute-start | bytes 11010056 | tf_op jit(solution)/shard_map/ppermute | solution.py:39
  160.7 20.7 %collective-permute-start.21 = (bf16[4,256,896]{2,1,0:T(8,128)(2,1)}, bf16[4,256,896]{2,1,0:T(8,128)(2,1)}, u32[]{:S(2)}, u32[]{:S(2)}) collective-permute-start(bf16[4,256,896]{2,1,0:T(8,128)(2,1)} %get-tuple-element.48), channel_id=1, source_target_pairs={{0,1},{1,0},{2,3},{3,2},{4,5},{5,4},{6,7},{7,6},{8,9},{9,8},{10,11... | collective-permute-start | bytes 5505032 | tf_op jit(solution)/shard_map/ppermute | solution.py:39
  168.8 10.4 %collective-permute-start.17 = (f32[128,256]{1,0:T(8,128)S(1)}, f32[128,256]{1,0:T(8,128)S(1)}, u32[]{:S(2)}, u32[]{:S(2)}) collective-permute-start(f32[128,256]{1,0:T(8,128)S(1)} %get-tuple-element.45), channel_id=1, source_target_pairs={{0,6},{1,3},{2,4},{3,1},{4,2},{5,7},{6,0},{7,5},{8,14},{9,11},{10,... | collective-permute-start | bytes 393224 | tf_op jit(solution)/shard_map/ppermute | solution.py:35
  172.0 23.6 %all-to-all-start.2 = ((bf16[16,40,768]{2,1,0:T(8,128)(2,1)}), bf16[16,40,768]{2,1,0:T(8,128)(2,1)}, u32[]{:S(2)}, u32[]{:S(2)}) async-start(bf16[16,40,768]{2,1,0:T(8,128)(2,1)} %bitcast.14), calls=%async_computation.2 | async-start | bytes 1966080 | tf_op jit(solution)/shard_map/all_to_all | solution.py:485
  179.9 13.7 %collective-permute-start.18 = (f32[64,256]{1,0:T(8,128)}, f32[64,256]{1,0:T(8,128)}, u32[]{:S(2)}, u32[]{:S(2)}) collective-permute-start(f32[64,256]{1,0:T(8,128)} %get-tuple-element.60), channel_id=1, source_target_pairs={{0,2},{1,7},{2,0},{3,5},{4,6},{5,3},{6,4},{7,1},{8,10},{9,15},{10,... | collective-permute-start | bytes 196616 | tf_op jit(solution)/shard_map/ppermute | solution.py:35
  181.3 14.3 %copy-start.14 = (bf16[640,64]{1,0:T(8,128)(2,1)S(1)}, bf16[640,64]{1,0:T(8,128)(2,1)}, u32[]{:S(2)}) copy-start(bf16[640,64]{1,0:T(8,128)(2,1)} %copy-done.12) | copy-start | bytes 245764
  (11 other events, 33.2 us)

commit v6 on v5

--- a/solution.py
+++ b/solution.py
@@ -448,7 +448,7 @@
     scratch += [pltpu.SemaphoreType.DMA((2, 4)), pltpu.SemaphoreType.DMA((6, 4))]
     outs = [(HBM, sds((8 * COLS, HID)))] * 2 + [(HBM, sds((HID, 8 * COLS))), (VMEM, sds((8, 128), F32))]
     ins = [SMEM] * 2 + [HBM] * 9 + [VMEM] * 2 + [HBM] * 2 + [ANY]
-    kernel = call(own_gradient_kernel, ins, outs, scratch, us=12, mib=MOST)
+    kernel = call(own_gradient_kernel, ins, outs, scratch, us=1, mib=MOST)
     return kernel(place, other_place, *xs, *dys, came, dab, hs, columns, rows, later)
 
 

time: 201 us -> 199 us (0.990)
    unnamed x36 -> x34, local copies, waits for them, and re-layouts: 5.58 us -> 5.59 us
where the time goes in v6:
time: 199 us; the launch traced here: 198 us
  Pallas kernels  89.5 us (45%)
  waiting for transfers between devices  47.2 us (24%)
  starting transfers between devices  46.9 us (24%)
  local copies, waits for them, and re-layouts  9.31 us (5%)
  other arithmetic  4.15 us (2%)
    all_to_all x4, waiting for transfers between devices, exchange(): lax.all_to_all(v.reshape(16, ROOM, -1), ('x', 'z'), 0, 0, tiled=True)  30.4 us
    all_to_all x4, starting transfers between devices, exchange(): lax.all_to_all(v.reshape(16, ROOM, -1), ('x', 'z'), 0, 0, tiled=True)  27.7 us
    ppermute x13, starting transfers between devices, meet(): return lax.ppermute(v, ('y', 'core'), MEET[step])  16.6 us
    pallas_call x1, Pallas kernels, pack(): call(pack_kernel, [HBM] * 6, outs, scratch, us=13, mib=MOST)(*weights)  14.6 us
    pallas_call x4, Pallas kernels, input_part(): call(functools.partial(input_kernel, k), ins, outs, scratch, us=4, mib=51)  14.1 us
    ppermute x13, waiting for transfers between devices, meet(): return lax.ppermute(v, ('y', 'core'), MEET[step])  13.2 us
    pallas_call x1, Pallas kernels, own_gradients(): kernel(place, other_place, *xs, *dys, came, dab, hs, columns, rows, later)  12.3 us
    pallas_call x1, Pallas kernels, other_gradients(): call(other_gradient_kernel, ins, outs, scratch, us=10, mib=MOST)  10.1 us
  transfers between devices with their start and end apart: 26, of which 9 were waited for; matrix products, arithmetic and copies ran while one was open for 4% of the time, Pallas kernels for 44%

profile of v6, /device:TPU:0, one launch (start us, length us, event | category | flops | bytes accessed | tf_op | source)
XLA Modules:
  0.0 198.0 jit_solution(5947936923585874871)
XLA Ops:
  1.4 1.7 collective-permute-start
  6.9 7.9 %all-to-all-start = ((bf16[16,40,896]{2,1,0:T(8,128)(2,1)}), bf16[16,40,896]{2,1,0:T(8,128)(2,1)S(1)}, u32[]{:S(2)}, u32[]{:S(2)}) async-start(bf16[16,40,896]{2,1,0:T(8,128)(2,1)} %bitcast.7), calls=%async_computation | async-start | bytes 2293760 | tf_op jit(solution)/shard_map/all_to_all | solution.py:485
  16.2 1.6 collective-permute-start.1
  18.4 3.7 %collective-permute-done.1.refs_1_ = bf16[128,384]{1,0:T(8,128)(2,1)S(1)} collective-permute-done((bf16[128,384]{1,0:T(8,128)(2,1)S(1)}, bf16[128,384]{1,0:T(8,128)(2,1)S(1)}, u32[]{:S(2)}, u32[]{:S(2)}) %collective-permute-start.1) | collective-permute-done | bytes 98336 | tf_op jit(solution)/shard_map/ppermute | solution.py:35
  24.4 11.1 %all-to-all-done = bf16[16,40,896]{2,1,0:T(8,128)(2,1)S(1)} async-done(((bf16[16,40,896]{2,1,0:T(8,128)(2,1)}), bf16[16,40,896]{2,1,0:T(8,128)(2,1)S(1)}, u32[]{:S(2)}, u32[]{:S(2)}) %all-to-all-start) | async-done | bytes 1146912 | tf_op jit(solution)/shard_map/all_to_all | solution.py:485
  36.6 6.2 %all-to-all-start.1 = ((bf16[16,40,2176]{2,1,0:T(8,128)(2,1)}), bf16[16,40,2176]{2,1,0:T(8,128)(2,1)}, u32[]{:S(2)}, u32[]{:S(2)}) async-start(bf16[16,40,2176]{2,1,0:T(8,128)(2,1)} %bitcast.26), calls=%async_computation.1 | async-start | bytes 5570560 | tf_op jit(solution)/shard_map/all_to_all | solution.py:485
  42.8 14.6 %shard_map.115 = (bf16[7168,1024]{1,0:T(8,128)(2,1)}, bf16[512,7168]{1,0:T(8,128)(2,1)}) custom-call(bf16[7168,256]{1,0:T(8,128)(2,1)} %bitcast.32, bf16[7168,256]{1,0:T(8,128)(2,1)} %bitcast.34, bf16[7168,256]{1,0:T(8,128)(2,1)} %collective-permute-done.2.refs_1_.refs_2_, bf16[7168,256]{1,0:T(8,128)(2,1)} %collective-permute-done.3.refs_2_.refs_3_, ...), custom_call_target="tpu_custom_call" | custom-call | flops 389999984640 | bytes 10000 | tf_op jit(solution)/shard_map/pallas_call | solution.py:170
  57.5 6.0 %collective-permute-done.8.refs_1_ = bf16[640,896]{1,0:T(8,128)(2,1)} collective-permute-done((bf16[640,896]{1,0:T(8,128)(2,1)}, bf16[640,896]{1,0:T(8,128)(2,1)}, u32[]{:S(2)}, u32[]{:S(2)}) %collective-permute-start.8) | collective-permute-done | bytes 1146912 | tf_op jit(solution)/shard_map/ppermute | solution.py:35
  63.5 16.8 %all-to-all-done.1 = bf16[16,40,2176]{2,1,0:T(8,128)(2,1)} async-done(((bf16[16,40,2176]{2,1,0:T(8,128)(2,1)}), bf16[16,40,2176]{2,1,0:T(8,128)(2,1)}, u32[]{:S(2)}, u32[]{:S(2)}) %all-to-all-start.1) | async-done | bytes 2785312 | tf_op jit(solution)/shard_map/all_to_all | solution.py:485
  80.3 2.0 slice.20.d0.refs_4_
  83.4 3.3 %collective-permute-start.6 = (bf16[640,512]{1,0:T(8,128)(2,1)}, bf16[640,512]{1,0:T(8,128)(2,1)}, u32[]{:S(2)}, u32[]{:S(2)}) collective-permute-start(bf16[640,512]{1,0:T(8,128)(2,1)} %slice.20.d0.refs_4_), channel_id=1, source_target_pairs={{0,6},{1,3},{2,4},{3,1},{4,2},{5,7},{6,0},{7,5},{8,14},{9,11},{10,... | collective-permute-start | bytes 1966088 | tf_op jit(solution)/shard_map/ppermute | solution.py:35
  86.7 8.6 %shard_map.116.refs_2_ = f32[640,1024]{1,0:T(8,128)} custom-call(s32[4]{0:T(128)} %pad_add_fusion.place, bf16[640,896]{1,0:T(8,128)(2,1)} %shard_map.112.refs_1_.refs_0_, bf16[640,896]{1,0:T(8,128)(2,1)} %collective-permute-done.8.refs_1_, bf16[640,896]{1,0:T(8,128)(2,1)} %collective-permute-done.10.refs_2_, ...), custom_call_target="tpu_custom_call" | custom-call | flops 240000008192 | bytes 10000 | tf_op jit(solution)/shard_map/pallas_call | solution.py:205
  96.3 1.9 collective-permute-done.5.refs_0_
  99.6 9.0 %shard_map.117 = (f32[640,512]{1,0:T(8,128)}, f32[640,512]{1,0:T(8,128)}, f32[640,512]{1,0:T(8,128)}) custom-call(s32[4]{0:T(128)} %pad_add_fusion.place, bf16[640,896]{1,0:T(8,128)(2,1)} %collective-permute-done.9.x_last.refs_3_, bf16[640,512]{1,0:T(8,128)(2,1)} %slice.20.d0.refs_4_, bf16[640,512]{1,0:T(8,128)(2,1)} %shard_map.114.d1.refs_5_, ...), custom_call_target="tpu_custom_call" | custom-call | flops 359999995904 | bytes 10000 | tf_op jit(solution)/shard_map/pallas_call | solution.py:251
  110.3 4.9 %shard_map.118 = (f32[640,256]{1,0:T(8,128)}, f32[640,256]{1,0:T(8,128)}) custom-call(s32[4]{0:T(128)} %pad_add_fusion.place, bf16[640,512]{1,0:T(8,128)(2,1)} %collective-permute-done.7.refs_0_.refs_7_, bf16[640,2176]{1,0:T(8,128)(2,1)} %bitcast.13.came.refs_1_.refs_8_, bf16[512,7168]{1,0:T(8,128)(2,1)} %get-tuple-element.33.refs_1_.refs_2_, ...), custom_call_target="tpu_custom_call" | custom-call | flops 89999998976 | bytes 10000 | tf_op jit(solution)/shard_map/pallas_call | solution.py:283
  115.7 1.9 collective-permute-done.11.came
  120.9 4.0 %shard_map.121.refs_1_ = bf16[656,640]{1,0:T(8,128)(2,1)} custom-call(s32[4]{0:T(128)S(1)} %copy-done.4, bf16[656,512]{1,0:T(8,128)(2,1)S(1)} %get-tuple-element.43.own.refs_9_, bf16[656,512]{1,0:T(8,128)(2,1)S(1)} %collective-permute-done.13.other.refs_9_, bf16[7168,1024]{1,0:T(8,128)(2,1)} %get-tuple-element.34.refs_3_.refs_0_.ws), custom_call_target="tpu_custom_call" | custom-call | flops 120000004096 | bytes 10000 | tf_op jit(solution)/shard_map/pallas_call | solution.py:323
  124.9 1.7 collective-permute-start.14
  126.6 4.0 %shard_map.122.refs_1_._ = bf16[656,640]{1,0:T(8,128)(2,1)} custom-call(s32[4]{0:T(128)S(1)} %copy-done.4, bf16[656,512]{1,0:T(8,128)(2,1)S(1)} %get-tuple-element.43.own.refs_9_, bf16[656,512]{1,0:T(8,128)(2,1)S(1)} %collective-permute-done.13.other.refs_9_, bf16[7168,1024]{1,0:T(8,128)(2,1)} %get-tuple-element.34.refs_3_.refs_0_.ws, ...), custom_call_target="tpu_custom_call" | custom-call | flops 120000004096 | bytes 10000 | tf_op jit(solution)/shard_map/pallas_call | solution.py:323
  130.6 1.9 collective-permute-start.15
  132.5 6.1 %shard_map.126 = bf16[640,1024]{1,0:T(8,128)(2,1)} custom-call(s32[4]{0:T(128)S(1)} %copy-done.4, bf16[656,512]{1,0:T(8,128)(2,1)S(1)} %get-tuple-element.43.own.refs_9_, bf16[656,512]{1,0:T(8,128)(2,1)S(1)} %collective-permute-done.13.other.refs_9_, bf16[7168,1024]{1,0:T(8,128)(2,1)} %get-tuple-element.34.refs_3_.refs_0_.ws, ...), custom_call_target="tpu_custom_call" | custom-call | flops 120000004096 | bytes 10000 | tf_op jit(solution)/shard_map/pallas_call | solution.py:342
  138.6 6.4 %all-to-all-start.3 = ((bf16[16,40,1024]{2,1,0:T(8,128)(2,1)}), bf16[16,40,1024]{2,1,0:T(8,128)(2,1)}, u32[]{:S(2)}, u32[]{:S(2)}) async-start(bf16[16,40,1024]{2,1,0:T(8,128)(2,1)} %bitcast.30), calls=%async_computation.3 | async-start | bytes 2621440 | tf_op jit(solution)/shard_map/all_to_all | solution.py:485
  145.0 3.1 %shard_map.123 = bf16[656,640]{1,0:T(8,128)(2,1)S(1)} custom-call(s32[4]{0:T(128)S(1)} %copy-done.4, bf16[656,512]{1,0:T(8,128)(2,1)S(1)} %get-tuple-element.43.own.refs_9_, bf16[656,512]{1,0:T(8,128)(2,1)S(1)} %collective-permute-done.13.other.refs_9_, bf16[7168,1024]{1,0:T(8,128)(2,1)} %get-tuple-element.34.refs_3_.refs_0_.ws, ...), custom_call_target="tpu_custom_call" | custom-call | flops 120000004096 | bytes 10000 | tf_op jit(solution)/shard_map/pallas_call | solution.py:323
  148.1 2.2 %add_convert_fusion.refs_1_.refs_11_ = bf16[656,640]{1,0:T(8,128)(2,1)} fusion(bf16[656,640]{1,0:T(8,128)(2,1)} %collective-permute-done.14, bf16[656,640]{1,0:T(8,128)(2,1)S(1)} %shard_map.123), kind=kLoop, calls=%fused_computation | loop fusion | flops 1679360 | bytes 2519040 | tf_op jit(solution)/shard_map/convert_element_type | solution.py:493
  150.4 10.1 %shard_map.128 = (bf16[4,896,512]{2,1,0:T(8,128)(2,1)}, bf16[4,256,896]{2,1,0:T(8,128)(2,1)}) custom-call(bf16[640,896]{1,0:T(8,128)(2,1)} %shard_map.112.refs_1_.refs_0_, bf16[640,896]{1,0:T(8,128)(2,1)} %collective-permute-done.8.refs_1_, bf16[640,896]{1,0:T(8,128)(2,1)} %collective-permute-done.10.refs_2_, ...), custom_call_target="tpu_custom_call" | custom-call | flops 299999985664 | bytes 10000 | tf_op jit(solution)/shard_map/pallas_call | solution.py:400
  161.0 3.1 %shard_map.124.refs_0_ = bf16[656,640]{1,0:T(8,128)(2,1)S(1)} custom-call(s32[4]{0:T(128)S(1)} %copy-done.5, bf16[656,512]{1,0:T(8,128)(2,1)S(1)} %get-tuple-element.43.own.refs_9_, bf16[656,512]{1,0:T(8,128)(2,1)S(1)} %copy-done.8, bf16[7168,1024]{1,0:T(8,128)(2,1)} %get-tuple-element.34.refs_3_.refs_0_.ws, bf16[656,640]{1,0:T(8,128)(2,1)} %add_convert_fusion.refs_1_.refs_11_), custom_call_target="tpu_custom_call" | custom-call | flops 120000004096 | bytes 10000 | tf_op jit(solution)/shard_map/pallas_call | solution.py:323
  164.2 3.0 %shard_map.125._.refs_13_ = bf16[640,768]{1,0:T(8,128)(2,1)} custom-call(s32[1]{0:T(128)} %bitcast.expert, bf16[656,640]{1,0:T(8,128)(2,1)S(1)} %shard_map.124.refs_0_, bf16[656,640]{1,0:T(8,128)(2,1)} %collective-permute-done.15.refs_1_, bf16[656,640]{1,0:T(8,128)(2,1)} %collective-permute-done.16.refs_2_), custom_call_target="tpu_custom_call" | custom-call | flops 30000001024 | bytes 10000 | tf_op jit(solution)/shard_map/pallas_call | solution.py:471
  167.2 1.7 shard_map.127
  168.9 2.4 %collective-permute-start.17 = (f32[128,256]{1,0:T(8,128)S(1)}, f32[128,256]{1,0:T(8,128)S(1)}, u32[]{:S(2)}, u32[]{:S(2)}) collective-permute-start(f32[128,256]{1,0:T(8,128)S(1)} %get-tuple-element.45), channel_id=1, source_target_pairs={{0,6},{1,3},{2,4},{3,1},{4,2},{5,7},{6,0},{7,5},{8,14},{9,11},{10,... | collective-permute-start | bytes 393224 | tf_op jit(solution)/shard_map/ppermute | solution.py:35
  172.0 7.2 %all-to-all-start.2 = ((bf16[16,40,768]{2,1,0:T(8,128)(2,1)}), bf16[16,40,768]{2,1,0:T(8,128)(2,1)S(1)}, u32[]{:S(2)}, u32[]{:S(2)}) async-start(bf16[16,40,768]{2,1,0:T(8,128)(2,1)} %bitcast.14), calls=%async_computation.2 | async-start | bytes 1966080 | tf_op jit(solution)/shard_map/all_to_all | solution.py:485
  180.7 12.3 %shard_map.129 = (bf16[7168,256]{1,0:T(8,128)(2,1)}, bf16[7168,256]{1,0:T(8,128)(2,1)}, bf16[256,7168]{1,0:T(8,128)(2,1)}, f32[8,128]{1,0:T(8,128)}) custom-call(s32[4]{0:T(128)} %pad_add_fusion.place, s32[4]{0:T(128)} %pad_add_fusion.1.other_place, bf16[640,896]{1,0:T(8,128)(2,1)} %shard_map.112.refs_1_.refs_0_, ...), custom_call_target="tpu_custom_call" | custom-call | flops 30000001024 | bytes 10000 | tf_op jit(solution)/shard_map/pallas_call | solution.py:452
  193.0 2.5 %all-to-all-done.2 = bf16[16,40,768]{2,1,0:T(8,128)(2,1)S(1)} async-done(((bf16[16,40,768]{2,1,0:T(8,128)(2,1)}), bf16[16,40,768]{2,1,0:T(8,128)(2,1)S(1)}, u32[]{:S(2)}, u32[]{:S(2)}) %all-to-all-start.2) | async-done | bytes 983072 | tf_op jit(solution)/shard_map/all_to_all | solution.py:485
  (85 shorter events, 24.1 us)
Async XLA Ops:
  1.4 14.7 %collective-permute-start = (bf16[64,384]{1,0:T(8,128)(2,1)S(1)}, bf16[64,384]{1,0:T(8,128)(2,1)S(1)}, u32[]{:S(2)}, u32[]{:S(2)}) collective-permute-start(bf16[64,384]{1,0:T(8,128)(2,1)S(1)} %slice.15), channel_id=1, source_target_pairs={{0,2},{1,7},{2,0},{3,5},{4,6},{5,3},{6,4},{7,1},{8,10},{9,15},{10,... | collective-permute-start | bytes 147464 | tf_op jit(solution)/shard_map/ppermute | solution.py:35
  5.4 16.7 %copy-start.1 = (bf16[64,896]{1,0:T(8,128)(2,1)S(1)}, bf16[64,896]{1,0:T(8,128)(2,1)}, u32[]{:S(2)}) copy-start(bf16[64,896]{1,0:T(8,128)(2,1)} %dy.1) | copy-start | bytes 344068
  6.9 15.9 %copy-start.12 = (bf16[640,64]{1,0:T(8,128)(2,1)}, bf16[640,64]{1,0:T(8,128)(2,1)S(1)}, u32[]{:S(2)}) copy-start(bf16[640,64]{1,0:T(8,128)(2,1)S(1)} %get-tuple-element.30.onehot) | copy-start | bytes 245764
  6.9 28.6 %all-to-all-start = ((bf16[16,40,896]{2,1,0:T(8,128)(2,1)}), bf16[16,40,896]{2,1,0:T(8,128)(2,1)S(1)}, u32[]{:S(2)}, u32[]{:S(2)}) async-start(bf16[16,40,896]{2,1,0:T(8,128)(2,1)} %bitcast.7), calls=%async_computation | async-start | bytes 2293760 | tf_op jit(solution)/shard_map/all_to_all | solution.py:485
  14.8 20.7 %collective-permute-start.2 = (bf16[7168,256]{1,0:T(8,128)(2,1)}, bf16[7168,256]{1,0:T(8,128)(2,1)}, u32[]{:S(2)}, u32[]{:S(2)}) collective-permute-start(bf16[7168,256]{1,0:T(8,128)(2,1)} %bitcast.31), channel_id=1, source_target_pairs={{0,1},{1,0},{2,3},{3,2},{4,5},{5,4},{6,7},{7,6},{8,9},{9,8},{10,11... | collective-permute-start | bytes 11010056 | tf_op jit(solution)/shard_map/ppermute | solution.py:39
  15.6 20.0 %collective-permute-start.3 = (bf16[7168,256]{1,0:T(8,128)(2,1)}, bf16[7168,256]{1,0:T(8,128)(2,1)}, u32[]{:S(2)}, u32[]{:S(2)}) collective-permute-start(bf16[7168,256]{1,0:T(8,128)(2,1)} %bitcast.33), channel_id=1, source_target_pairs={{0,1},{1,0},{2,3},{3,2},{4,5},{5,4},{6,7},{7,6},{8,9},{9,8},{10,11... | collective-permute-start | bytes 11010056 | tf_op jit(solution)/shard_map/ppermute | solution.py:39
  15.7 19.9 %collective-permute-start.4 = (bf16[256,7168]{1,0:T(8,128)(2,1)}, bf16[256,7168]{1,0:T(8,128)(2,1)}, u32[]{:S(2)}, u32[]{:S(2)}) collective-permute-start(bf16[256,7168]{1,0:T(8,128)(2,1)} %bitcast.35), channel_id=1, source_target_pairs={{0,1},{1,0},{2,3},{3,2},{4,5},{5,4},{6,7},{7,6},{8,9},{9,8},{10,11... | collective-permute-start | bytes 11010056 | tf_op jit(solution)/shard_map/ppermute | solution.py:39
  16.2 5.9 %collective-permute-start.1 = (bf16[128,384]{1,0:T(8,128)(2,1)S(1)}, bf16[128,384]{1,0:T(8,128)(2,1)S(1)}, u32[]{:S(2)}, u32[]{:S(2)}) collective-permute-start(bf16[128,384]{1,0:T(8,128)(2,1)S(1)} %pad_maximum_fusion.refs_0_), channel_id=1, source_target_pairs={{0,6},{1,3},{2,4},{3,1},{4,2},{5,7},{6,0},{7,5},{8,14},{9,11},{10,... | collective-permute-start | bytes 294920 | tf_op jit(solution)/shard_map/ppermute | solution.py:35
  36.6 26.9 %collective-permute-start.8 = (bf16[640,896]{1,0:T(8,128)(2,1)}, bf16[640,896]{1,0:T(8,128)(2,1)}, u32[]{:S(2)}, u32[]{:S(2)}) collective-permute-start(bf16[640,896]{1,0:T(8,128)(2,1)} %shard_map.112.refs_1_.refs_0_), channel_id=1, source_target_pairs={{0,2},{1,7},{2,0},{3,5},{4,6},{5,3},{6,4},{7,1},{8,10},{9,15},{10,... | collective-permute-start | bytes 3440648 | tf_op jit(solution)/shard_map/ppermute | solution.py:35
  36.6 50.1 %collective-permute-start.10 = (bf16[640,896]{1,0:T(8,128)(2,1)}, bf16[640,896]{1,0:T(8,128)(2,1)}, u32[]{:S(2)}, u32[]{:S(2)}) collective-permute-start(bf16[640,896]{1,0:T(8,128)(2,1)} %shard_map.112.refs_1_.refs_0_), channel_id=1, source_target_pairs={{0,6},{1,3},{2,4},{3,1},{4,2},{5,7},{6,0},{7,5},{8,14},{9,11},{10,... | collective-permute-start | bytes 3440648 | tf_op jit(solution)/shard_map/ppermute | solution.py:35
  36.6 43.7 %all-to-all-start.1 = ((bf16[16,40,2176]{2,1,0:T(8,128)(2,1)}), bf16[16,40,2176]{2,1,0:T(8,128)(2,1)}, u32[]{:S(2)}, u32[]{:S(2)}) async-start(bf16[16,40,2176]{2,1,0:T(8,128)(2,1)} %bitcast.26), calls=%async_computation.1 | async-start | bytes 5570560 | tf_op jit(solution)/shard_map/all_to_all | solution.py:485
  63.5 36.1 %collective-permute-start.9 = (bf16[640,896]{1,0:T(8,128)(2,1)}, bf16[640,896]{1,0:T(8,128)(2,1)}, u32[]{:S(2)}, u32[]{:S(2)}) collective-permute-start(bf16[640,896]{1,0:T(8,128)(2,1)} %collective-permute-done.8.refs_1_), channel_id=1, source_target_pairs={{0,6},{1,3},{2,4},{3,1},{4,2},{5,7},{6,0},{7,5},{8,14},{9,11},{10,... | collective-permute-start | bytes 3440648 | tf_op jit(solution)/shard_map/ppermute | solution.py:35
  82.3 15.9 %collective-permute-start.5 = (bf16[640,512]{1,0:T(8,128)(2,1)}, bf16[640,512]{1,0:T(8,128)(2,1)}, u32[]{:S(2)}, u32[]{:S(2)}) collective-permute-start(bf16[640,512]{1,0:T(8,128)(2,1)} %slice.20.d0.refs_4_), channel_id=1, source_target_pairs={{0,2},{1,7},{2,0},{3,5},{4,6},{5,3},{6,4},{7,1},{8,10},{9,15},{10,... | collective-permute-start | bytes 1966088 | tf_op jit(solution)/shard_map/ppermute | solution.py:35
  83.4 14.8 %collective-permute-start.6 = (bf16[640,512]{1,0:T(8,128)(2,1)}, bf16[640,512]{1,0:T(8,128)(2,1)}, u32[]{:S(2)}, u32[]{:S(2)}) collective-permute-start(bf16[640,512]{1,0:T(8,128)(2,1)} %slice.20.d0.refs_4_), channel_id=1, source_target_pairs={{0,6},{1,3},{2,4},{3,1},{4,2},{5,7},{6,0},{7,5},{8,14},{9,11},{10,... | collective-permute-start | bytes 1966088 | tf_op jit(solution)/shard_map/ppermute | solution.py:35
  98.2 12.1 %collective-permute-start.7 = (bf16[640,512]{1,0:T(8,128)(2,1)}, bf16[640,512]{1,0:T(8,128)(2,1)}, u32[]{:S(2)}, u32[]{:S(2)}) collective-permute-start(bf16[640,512]{1,0:T(8,128)(2,1)} %shard_map.114.d1.refs_5_), channel_id=1, source_target_pairs={{0,6},{1,3},{2,4},{3,1},{4,2},{5,7},{6,0},{7,5},{8,14},{9,11},{10,... | collective-permute-start | bytes 1966088 | tf_op jit(solution)/shard_map/ppermute | solution.py:35
  108.7 6.7 %collective-permute-start.12 = (f32[640,512]{1,0:T(8,128)}, f32[640,512]{1,0:T(8,128)S(1)}, u32[]{:S(2)}, u32[]{:S(2)}) collective-permute-start(f32[640,512]{1,0:T(8,128)} %get-tuple-element.39), channel_id=1, source_target_pairs={{0,1},{1,0},{2,3},{3,2},{4,5},{5,4},{6,7},{7,6},{8,9},{9,8},{10,11... | collective-permute-start | bytes 3932168 | tf_op jit(solution)/shard_map/ppermute | solution.py:39
  115.2 2.4 %collective-permute-start.11 = (f32[640,256]{1,0:T(8,128)}, f32[640,256]{1,0:T(8,128)S(1)}, u32[]{:S(2)}, u32[]{:S(2)}) collective-permute-start(f32[640,256]{1,0:T(8,128)} %get-tuple-element.37), channel_id=1, source_target_pairs={{0,1},{1,0},{2,3},{3,2},{4,5},{5,4},{6,7},{7,6},{8,9},{9,8},{10,11... | collective-permute-start | bytes 1966088 | tf_op jit(solution)/shard_map/ppermute | solution.py:39
  118.8 42.3 %copy-start.6 = (bf16[656,512]{1,0:T(8,128)(2,1)}, bf16[656,512]{1,0:T(8,128)(2,1)S(1)}, u32[]{:S(2)}) copy-start(bf16[656,512]{1,0:T(8,128)(2,1)S(1)} %get-tuple-element.43.own.refs_9_) | copy-start | bytes 2015236
  118.8 2.1 %collective-permute-start.13 = (bf16[656,512]{1,0:T(8,128)(2,1)S(1)}, bf16[656,512]{1,0:T(8,128)(2,1)S(1)}, u32[]{:S(2)}, u32[]{:S(2)}) collective-permute-start(bf16[656,512]{1,0:T(8,128)(2,1)S(1)} %get-tuple-element.43.own.refs_9_), channel_id=1, source_target_pairs={{0,1},{1,0},{2,3},{3,2},{4,5},{5,4},{6,7},{7,6},{8,9},{9,8},{10,11... | collective-permute-start | bytes 2015240 | tf_op jit(solution)/shard_map/ppermute | solution.py:39
  118.9 31.5 %collective-permute-start.19 = (bf16[640,256]{1,0:T(8,128)(2,1)}, bf16[640,256]{1,0:T(8,128)(2,1)}, u32[]{:S(2)}, u32[]{:S(2)}) collective-permute-start(bf16[640,256]{1,0:T(8,128)(2,1)} %get-tuple-element.46.refs_10_), channel_id=1, source_target_pairs={{0,1},{1,0},{2,3},{3,2},{4,5},{5,4},{6,7},{7,6},{8,9},{9,8},{10,11... | collective-permute-start | bytes 983048 | tf_op jit(solution)/shard_map/ppermute | solution.py:39
  120.9 24.1 %copy-start.7 = (bf16[656,512]{1,0:T(8,128)(2,1)}, bf16[656,512]{1,0:T(8,128)(2,1)S(1)}, u32[]{:S(2)}) copy-start(bf16[656,512]{1,0:T(8,128)(2,1)S(1)} %collective-permute-done.13.other.refs_9_) | copy-start | bytes 2015236
  124.9 23.2 %collective-permute-start.14 = (bf16[656,640]{1,0:T(8,128)(2,1)}, bf16[656,640]{1,0:T(8,128)(2,1)}, u32[]{:S(2)}, u32[]{:S(2)}) collective-permute-start(bf16[656,640]{1,0:T(8,128)(2,1)} %shard_map.121.refs_1_), channel_id=1, source_target_pairs={{0,6},{1,3},{2,4},{3,1},{4,2},{5,7},{6,0},{7,5},{8,14},{9,11},{10,... | collective-permute-start | bytes 2519048 | tf_op jit(solution)/shard_map/ppermute | solution.py:35
  130.6 33.6 %collective-permute-start.15 = (bf16[656,640]{1,0:T(8,128)(2,1)}, bf16[656,640]{1,0:T(8,128)(2,1)}, u32[]{:S(2)}, u32[]{:S(2)}) collective-permute-start(bf16[656,640]{1,0:T(8,128)(2,1)} %shard_map.122.refs_1_._), channel_id=1, source_target_pairs={{0,6},{1,3},{2,4},{3,1},{4,2},{5,7},{6,0},{7,5},{8,14},{9,11},{10,... | collective-permute-start | bytes 2519048 | tf_op jit(solution)/shard_map/ppermute | solution.py:35
  138.6 28.6 %all-to-all-start.3 = ((bf16[16,40,1024]{2,1,0:T(8,128)(2,1)}), bf16[16,40,1024]{2,1,0:T(8,128)(2,1)}, u32[]{:S(2)}, u32[]{:S(2)}) async-start(bf16[16,40,1024]{2,1,0:T(8,128)(2,1)} %bitcast.30), calls=%async_computation.3 | async-start | bytes 2621440 | tf_op jit(solution)/shard_map/all_to_all | solution.py:485
  150.4 13.8 %collective-permute-start.16 = (bf16[656,640]{1,0:T(8,128)(2,1)}, bf16[656,640]{1,0:T(8,128)(2,1)}, u32[]{:S(2)}, u32[]{:S(2)}) collective-permute-start(bf16[656,640]{1,0:T(8,128)(2,1)} %add_convert_fusion.refs_1_.refs_11_), channel_id=1, source_target_pairs={{0,2},{1,7},{2,0},{3,5},{4,6},{5,3},{6,4},{7,1},{8,10},{9,15},{10,... | collective-permute-start | bytes 2519048 | tf_op jit(solution)/shard_map/ppermute | solution.py:35
  150.4 10.7 %copy-start.5 = (s32[4]{0:T(128)S(1)}, s32[4]{0:T(128)}, u32[]{:S(2)}) copy-start(s32[4]{0:T(128)} %pad_add_fusion.place) | copy-start | bytes 52
  150.4 10.7 %copy-start.8 = (bf16[656,512]{1,0:T(8,128)(2,1)S(1)}, bf16[656,512]{1,0:T(8,128)(2,1)}, u32[]{:S(2)}) copy-start(bf16[656,512]{1,0:T(8,128)(2,1)} %copy-done.7) | copy-start | bytes 2015236
  160.4 20.3 %collective-permute-start.20 = (bf16[4,896,512]{2,1,0:T(8,128)(2,1)}, bf16[4,896,512]{2,1,0:T(8,128)(2,1)}, u32[]{:S(2)}, u32[]{:S(2)}) collective-permute-start(bf16[4,896,512]{2,1,0:T(8,128)(2,1)} %get-tuple-element.47), channel_id=1, source_target_pairs={{0,1},{1,0},{2,3},{3,2},{4,5},{5,4},{6,7},{7,6},{8,9},{9,8},{10,11... | collective-permute-start | bytes 11010056 | tf_op jit(solution)/shard_map/ppermute | solution.py:39
  160.7 20.0 %collective-permute-start.21 = (bf16[4,256,896]{2,1,0:T(8,128)(2,1)}, bf16[4,256,896]{2,1,0:T(8,128)(2,1)}, u32[]{:S(2)}, u32[]{:S(2)}) collective-permute-start(bf16[4,256,896]{2,1,0:T(8,128)(2,1)} %get-tuple-element.48), channel_id=1, source_target_pairs={{0,1},{1,0},{2,3},{3,2},{4,5},{5,4},{6,7},{7,6},{8,9},{9,8},{10,11... | collective-permute-start | bytes 5505032 | tf_op jit(solution)/shard_map/ppermute | solution.py:39
  168.9 10.3 %collective-permute-start.17 = (f32[128,256]{1,0:T(8,128)S(1)}, f32[128,256]{1,0:T(8,128)S(1)}, u32[]{:S(2)}, u32[]{:S(2)}) collective-permute-start(f32[128,256]{1,0:T(8,128)S(1)} %get-tuple-element.45), channel_id=1, source_target_pairs={{0,6},{1,3},{2,4},{3,1},{4,2},{5,7},{6,0},{7,5},{8,14},{9,11},{10,... | collective-permute-start | bytes 393224 | tf_op jit(solution)/shard_map/ppermute | solution.py:35
  172.0 23.5 %all-to-all-start.2 = ((bf16[16,40,768]{2,1,0:T(8,128)(2,1)}), bf16[16,40,768]{2,1,0:T(8,128)(2,1)S(1)}, u32[]{:S(2)}, u32[]{:S(2)}) async-start(bf16[16,40,768]{2,1,0:T(8,128)(2,1)} %bitcast.14), calls=%async_computation.2 | async-start | bytes 1966080 | tf_op jit(solution)/shard_map/all_to_all | solution.py:485
  179.2 13.8 %collective-permute-start.18 = (f32[64,256]{1,0:T(8,128)S(1)}, f32[64,256]{1,0:T(8,128)S(1)}, u32[]{:S(2)}, u32[]{:S(2)}) collective-permute-start(f32[64,256]{1,0:T(8,128)S(1)} %get-tuple-element.60), channel_id=1, source_target_pairs={{0,2},{1,7},{2,0},{3,5},{4,6},{5,3},{6,4},{7,1},{8,10},{9,15},{10,... | collective-permute-start | bytes 196616 | tf_op jit(solution)/shard_map/ppermute | solution.py:35
  (10 other events, 22.5 us)

commit v7 on v6

--- a/solution.py
+++ b/solution.py
@@ -137,7 +137,7 @@
 
 def combine(back, onehot, ids, terms, later):
     outs = [(VMEM, sds((64, COLS))), (VMEM, sds((64, 8), F32))]
-    return call(combine_kernel, [VMEM] * 5 + [ANY], outs, us=3)(back, onehot, ids, *terms, later)
+    return call(combine_kernel, [VMEM] * 6, outs, us=3)(back, onehot, ids, *terms, later)
 
 
 def block(ref, i):

time: 199 us -> 199 us (level)
  no operation moved by 1% of the time
where the time goes in v7:
time: 199 us; the launch traced here: 198 us
  Pallas kernels  89.5 us (45%)
  waiting for transfers between devices  47.2 us (24%)
  starting transfers between devices  46.9 us (24%)
  local copies, waits for them, and re-layouts  9.31 us (5%)
  other arithmetic  4.15 us (2%)
    all_to_all x4, waiting for transfers between devices, exchange(): lax.all_to_all(v.reshape(16, ROOM, -1), ('x', 'z'), 0, 0, tiled=True)  30.4 us
    all_to_all x4, starting transfers between devices, exchange(): lax.all_to_all(v.reshape(16, ROOM, -1), ('x', 'z'), 0, 0, tiled=True)  27.7 us
    ppermute x13, starting transfers between devices, meet(): return lax.ppermute(v, ('y', 'core'), MEET[step])  16.6 us
    pallas_call x1, Pallas kernels, pack(): call(pack_kernel, [HBM] * 6, outs, scratch, us=13, mib=MOST)(*weights)  14.6 us
    pallas_call x4, Pallas kernels, input_part(): call(functools.partial(input_kernel, k), ins, outs, scratch, us=4, mib=51)  14.1 us
    ppermute x13, waiting for transfers between devices, meet(): return lax.ppermute(v, ('y', 'core'), MEET[step])  13.2 us
    pallas_call x1, Pallas kernels, own_gradients(): kernel(place, other_place, *xs, *dys, came, dab, hs, columns, rows, later)  12.3 us
    pallas_call x1, Pallas kernels, other_gradients(): call(other_gradient_kernel, ins, outs, scratch, us=10, mib=MOST)  10.1 us
  transfers between devices with their start and end apart: 26, of which 9 were waited for; matrix products, arithmetic and copies ran while one was open for 4% of the time, Pallas kernels for 44%

profile of v7, /device:TPU:0, one launch (start us, length us, event | category | flops | bytes accessed | tf_op | source)
XLA Modules:
  0.0 198.0 jit_solution(5947936923585874871)
XLA Ops:
  1.4 1.7 collective-permute-start
  6.9 7.9 %all-to-all-start = ((bf16[16,40,896]{2,1,0:T(8,128)(2,1)}), bf16[16,40,896]{2,1,0:T(8,128)(2,1)S(1)}, u32[]{:S(2)}, u32[]{:S(2)}) async-start(bf16[16,40,896]{2,1,0:T(8,128)(2,1)} %bitcast.7), calls=%async_computation | async-start | bytes 2293760 | tf_op jit(solution)/shard_map/all_to_all | solution.py:485
  16.2 1.6 collective-permute-start.1
  18.4 3.7 %collective-permute-done.1.refs_1_ = bf16[128,384]{1,0:T(8,128)(2,1)S(1)} collective-permute-done((bf16[128,384]{1,0:T(8,128)(2,1)S(1)}, bf16[128,384]{1,0:T(8,128)(2,1)S(1)}, u32[]{:S(2)}, u32[]{:S(2)}) %collective-permute-start.1) | collective-permute-done | bytes 98336 | tf_op jit(solution)/shard_map/ppermute | solution.py:35
  24.4 11.1 %all-to-all-done = bf16[16,40,896]{2,1,0:T(8,128)(2,1)S(1)} async-done(((bf16[16,40,896]{2,1,0:T(8,128)(2,1)}), bf16[16,40,896]{2,1,0:T(8,128)(2,1)S(1)}, u32[]{:S(2)}, u32[]{:S(2)}) %all-to-all-start) | async-done | bytes 1146912 | tf_op jit(solution)/shard_map/all_to_all | solution.py:485
  36.6 6.2 %all-to-all-start.1 = ((bf16[16,40,2176]{2,1,0:T(8,128)(2,1)}), bf16[16,40,2176]{2,1,0:T(8,128)(2,1)}, u32[]{:S(2)}, u32[]{:S(2)}) async-start(bf16[16,40,2176]{2,1,0:T(8,128)(2,1)} %bitcast.26), calls=%async_computation.1 | async-start | bytes 5570560 | tf_op jit(solution)/shard_map/all_to_all | solution.py:485
  42.8 14.6 %shard_map.115 = (bf16[7168,1024]{1,0:T(8,128)(2,1)}, bf16[512,7168]{1,0:T(8,128)(2,1)}) custom-call(bf16[7168,256]{1,0:T(8,128)(2,1)} %bitcast.32, bf16[7168,256]{1,0:T(8,128)(2,1)} %bitcast.34, bf16[7168,256]{1,0:T(8,128)(2,1)} %collective-permute-done.2.refs_1_.refs_2_, bf16[7168,256]{1,0:T(8,128)(2,1)} %collective-permute-done.3.refs_2_.refs_3_, ...), custom_call_target="tpu_custom_call" | custom-call | flops 389999984640 | bytes 10000 | tf_op jit(solution)/shard_map/pallas_call | solution.py:170
  57.5 6.0 %collective-permute-done.8.refs_1_ = bf16[640,896]{1,0:T(8,128)(2,1)} collective-permute-done((bf16[640,896]{1,0:T(8,128)(2,1)}, bf16[640,896]{1,0:T(8,128)(2,1)}, u32[]{:S(2)}, u32[]{:S(2)}) %collective-permute-start.8) | collective-permute-done | bytes 1146912 | tf_op jit(solution)/shard_map/ppermute | solution.py:35
  63.5 16.8 %all-to-all-done.1 = bf16[16,40,2176]{2,1,0:T(8,128)(2,1)} async-done(((bf16[16,40,2176]{2,1,0:T(8,128)(2,1)}), bf16[16,40,2176]{2,1,0:T(8,128)(2,1)}, u32[]{:S(2)}, u32[]{:S(2)}) %all-to-all-start.1) | async-done | bytes 2785312 | tf_op jit(solution)/shard_map/all_to_all | solution.py:485
  80.3 2.0 slice.20.d0.refs_4_
  83.4 3.3 %collective-permute-start.6 = (bf16[640,512]{1,0:T(8,128)(2,1)}, bf16[640,512]{1,0:T(8,128)(2,1)}, u32[]{:S(2)}, u32[]{:S(2)}) collective-permute-start(bf16[640,512]{1,0:T(8,128)(2,1)} %slice.20.d0.refs_4_), channel_id=1, source_target_pairs={{0,6},{1,3},{2,4},{3,1},{4,2},{5,7},{6,0},{7,5},{8,14},{9,11},{10,... | collective-permute-start | bytes 1966088 | tf_op jit(solution)/shard_map/ppermute | solution.py:35
  86.7 8.6 %shard_map.116.refs_2_ = f32[640,1024]{1,0:T(8,128)} custom-call(s32[4]{0:T(128)} %pad_add_fusion.place, bf16[640,896]{1,0:T(8,128)(2,1)} %shard_map.112.refs_1_.refs_0_, bf16[640,896]{1,0:T(8,128)(2,1)} %collective-permute-done.8.refs_1_, bf16[640,896]{1,0:T(8,128)(2,1)} %collective-permute-done.10.refs_2_, ...), custom_call_target="tpu_custom_call" | custom-call | flops 240000008192 | bytes 10000 | tf_op jit(solution)/shard_map/pallas_call | solution.py:205
  96.3 1.9 collective-permute-done.5.refs_0_
  99.6 9.0 %shard_map.117 = (f32[640,512]{1,0:T(8,128)}, f32[640,512]{1,0:T(8,128)}, f32[640,512]{1,0:T(8,128)}) custom-call(s32[4]{0:T(128)} %pad_add_fusion.place, bf16[640,896]{1,0:T(8,128)(2,1)} %collective-permute-done.9.x_last.refs_3_, bf16[640,512]{1,0:T(8,128)(2,1)} %slice.20.d0.refs_4_, bf16[640,512]{1,0:T(8,128)(2,1)} %shard_map.114.d1.refs_5_, ...), custom_call_target="tpu_custom_call" | custom-call | flops 359999995904 | bytes 10000 | tf_op jit(solution)/shard_map/pallas_call | solution.py:251
  110.3 4.9 %shard_map.118 = (f32[640,256]{1,0:T(8,128)}, f32[640,256]{1,0:T(8,128)}) custom-call(s32[4]{0:T(128)} %pad_add_fusion.place, bf16[640,512]{1,0:T(8,128)(2,1)} %collective-permute-done.7.refs_0_.refs_7_, bf16[640,2176]{1,0:T(8,128)(2,1)} %bitcast.13.came.refs_1_.refs_8_, bf16[512,7168]{1,0:T(8,128)(2,1)} %get-tuple-element.33.refs_1_.refs_2_, ...), custom_call_target="tpu_custom_call" | custom-call | flops 89999998976 | bytes 10000 | tf_op jit(solution)/shard_map/pallas_call | solution.py:283
  115.7 1.9 collective-permute-done.11.came
  120.9 4.0 %shard_map.121.refs_1_ = bf16[656,640]{1,0:T(8,128)(2,1)} custom-call(s32[4]{0:T(128)S(1)} %copy-done.4, bf16[656,512]{1,0:T(8,128)(2,1)S(1)} %get-tuple-element.43.own.refs_9_, bf16[656,512]{1,0:T(8,128)(2,1)S(1)} %collective-permute-done.13.other.refs_9_, bf16[7168,1024]{1,0:T(8,128)(2,1)} %get-tuple-element.34.refs_3_.refs_0_.ws), custom_call_target="tpu_custom_call" | custom-call | flops 120000004096 | bytes 10000 | tf_op jit(solution)/shard_map/pallas_call | solution.py:323
  124.9 1.7 collective-permute-start.14
  126.6 4.0 %shard_map.122.refs_1_._ = bf16[656,640]{1,0:T(8,128)(2,1)} custom-call(s32[4]{0:T(128)S(1)} %copy-done.4, bf16[656,512]{1,0:T(8,128)(2,1)S(1)} %get-tuple-element.43.own.refs_9_, bf16[656,512]{1,0:T(8,128)(2,1)S(1)} %collective-permute-done.13.other.refs_9_, bf16[7168,1024]{1,0:T(8,128)(2,1)} %get-tuple-element.34.refs_3_.refs_0_.ws, ...), custom_call_target="tpu_custom_call" | custom-call | flops 120000004096 | bytes 10000 | tf_op jit(solution)/shard_map/pallas_call | solution.py:323
  130.6 1.9 collective-permute-start.15
  132.5 6.1 %shard_map.126 = bf16[640,1024]{1,0:T(8,128)(2,1)} custom-call(s32[4]{0:T(128)S(1)} %copy-done.4, bf16[656,512]{1,0:T(8,128)(2,1)S(1)} %get-tuple-element.43.own.refs_9_, bf16[656,512]{1,0:T(8,128)(2,1)S(1)} %collective-permute-done.13.other.refs_9_, bf16[7168,1024]{1,0:T(8,128)(2,1)} %get-tuple-element.34.refs_3_.refs_0_.ws, ...), custom_call_target="tpu_custom_call" | custom-call | flops 120000004096 | bytes 10000 | tf_op jit(solution)/shard_map/pallas_call | solution.py:342
  138.6 6.4 %all-to-all-start.3 = ((bf16[16,40,1024]{2,1,0:T(8,128)(2,1)}), bf16[16,40,1024]{2,1,0:T(8,128)(2,1)}, u32[]{:S(2)}, u32[]{:S(2)}) async-start(bf16[16,40,1024]{2,1,0:T(8,128)(2,1)} %bitcast.30), calls=%async_computation.3 | async-start | bytes 2621440 | tf_op jit(solution)/shard_map/all_to_all | solution.py:485
  145.0 3.1 %shard_map.123 = bf16[656,640]{1,0:T(8,128)(2,1)S(1)} custom-call(s32[4]{0:T(128)S(1)} %copy-done.4, bf16[656,512]{1,0:T(8,128)(2,1)S(1)} %get-tuple-element.43.own.refs_9_, bf16[656,512]{1,0:T(8,128)(2,1)S(1)} %collective-permute-done.13.other.refs_9_, bf16[7168,1024]{1,0:T(8,128)(2,1)} %get-tuple-element.34.refs_3_.refs_0_.ws, ...), custom_call_target="tpu_custom_call" | custom-call | flops 120000004096 | bytes 10000 | tf_op jit(solution)/shard_map/pallas_call | solution.py:323
  148.1 2.2 %add_convert_fusion.refs_1_.refs_11_ = bf16[656,640]{1,0:T(8,128)(2,1)} fusion(bf16[656,640]{1,0:T(8,128)(2,1)} %collective-permute-done.14, bf16[656,640]{1,0:T(8,128)(2,1)S(1)} %shard_map.123), kind=kLoop, calls=%fused_computation | loop fusion | flops 1679360 | bytes 2519040 | tf_op jit(solution)/shard_map/convert_element_type | solution.py:493
  150.4 10.1 %shard_map.128 = (bf16[4,896,512]{2,1,0:T(8,128)(2,1)}, bf16[4,256,896]{2,1,0:T(8,128)(2,1)}) custom-call(bf16[640,896]{1,0:T(8,128)(2,1)} %shard_map.112.refs_1_.refs_0_, bf16[640,896]{1,0:T(8,128)(2,1)} %collective-permute-done.8.refs_1_, bf16[640,896]{1,0:T(8,128)(2,1)} %collective-permute-done.10.refs_2_, ...), custom_call_target="tpu_custom_call" | custom-call | flops 299999985664 | bytes 10000 | tf_op jit(solution)/shard_map/pallas_call | solution.py:400
  161.0 3.1 %shard_map.124.refs_0_ = bf16[656,640]{1,0:T(8,128)(2,1)S(1)} custom-call(s32[4]{0:T(128)S(1)} %copy-done.5, bf16[656,512]{1,0:T(8,128)(2,1)S(1)} %get-tuple-element.43.own.refs_9_, bf16[656,512]{1,0:T(8,128)(2,1)S(1)} %copy-done.8, bf16[7168,1024]{1,0:T(8,128)(2,1)} %get-tuple-element.34.refs_3_.refs_0_.ws, bf16[656,640]{1,0:T(8,128)(2,1)} %add_convert_fusion.refs_1_.refs_11_), custom_call_target="tpu_custom_call" | custom-call | flops 120000004096 | bytes 10000 | tf_op jit(solution)/shard_map/pallas_call | solution.py:323
  164.2 3.0 %shard_map.125._.refs_13_ = bf16[640,768]{1,0:T(8,128)(2,1)} custom-call(s32[1]{0:T(128)} %bitcast.expert, bf16[656,640]{1,0:T(8,128)(2,1)S(1)} %shard_map.124.refs_0_, bf16[656,640]{1,0:T(8,128)(2,1)} %collective-permute-done.15.refs_1_, bf16[656,640]{1,0:T(8,128)(2,1)} %collective-permute-done.16.refs_2_), custom_call_target="tpu_custom_call" | custom-call | flops 30000001024 | bytes 10000 | tf_op jit(solution)/shard_map/pallas_call | solution.py:471
  167.2 1.7 shard_map.127
  168.9 2.4 %collective-permute-start.17 = (f32[128,256]{1,0:T(8,128)S(1)}, f32[128,256]{1,0:T(8,128)S(1)}, u32[]{:S(2)}, u32[]{:S(2)}) collective-permute-start(f32[128,256]{1,0:T(8,128)S(1)} %get-tuple-element.45), channel_id=1, source_target_pairs={{0,6},{1,3},{2,4},{3,1},{4,2},{5,7},{6,0},{7,5},{8,14},{9,11},{10,... | collective-permute-start | bytes 393224 | tf_op jit(solution)/shard_map/ppermute | solution.py:35
  172.0 7.2 %all-to-all-start.2 = ((bf16[16,40,768]{2,1,0:T(8,128)(2,1)}), bf16[16,40,768]{2,1,0:T(8,128)(2,1)S(1)}, u32[]{:S(2)}, u32[]{:S(2)}) async-start(bf16[16,40,768]{2,1,0:T(8,128)(2,1)} %bitcast.14), calls=%async_computation.2 | async-start | bytes 1966080 | tf_op jit(solution)/shard_map/all_to_all | solution.py:485
  180.7 12.3 %shard_map.129 = (bf16[7168,256]{1,0:T(8,128)(2,1)}, bf16[7168,256]{1,0:T(8,128)(2,1)}, bf16[256,7168]{1,0:T(8,128)(2,1)}, f32[8,128]{1,0:T(8,128)}) custom-call(s32[4]{0:T(128)} %pad_add_fusion.place, s32[4]{0:T(128)} %pad_add_fusion.1.other_place, bf16[640,896]{1,0:T(8,128)(2,1)} %shard_map.112.refs_1_.refs_0_, ...), custom_call_target="tpu_custom_call" | custom-call | flops 30000001024 | bytes 10000 | tf_op jit(solution)/shard_map/pallas_call | solution.py:452
  193.0 2.5 %all-to-all-done.2 = bf16[16,40,768]{2,1,0:T(8,128)(2,1)S(1)} async-done(((bf16[16,40,768]{2,1,0:T(8,128)(2,1)}), bf16[16,40,768]{2,1,0:T(8,128)(2,1)S(1)}, u32[]{:S(2)}, u32[]{:S(2)}) %all-to-all-start.2) | async-done | bytes 983072 | tf_op jit(solution)/shard_map/all_to_all | solution.py:485
  (85 shorter events, 24.1 us)
Async XLA Ops:
  1.4 14.7 %collective-permute-start = (bf16[64,384]{1,0:T(8,128)(2,1)S(1)}, bf16[64,384]{1,0:T(8,128)(2,1)S(1)}, u32[]{:S(2)}, u32[]{:S(2)}) collective-permute-start(bf16[64,384]{1,0:T(8,128)(2,1)S(1)} %slice.15), channel_id=1, source_target_pairs={{0,2},{1,7},{2,0},{3,5},{4,6},{5,3},{6,4},{7,1},{8,10},{9,15},{10,... | collective-permute-start | bytes 147464 | tf_op jit(solution)/shard_map/ppermute | solution.py:35
  5.4 16.7 %copy-start.1 = (bf16[64,896]{1,0:T(8,128)(2,1)S(1)}, bf16[64,896]{1,0:T(8,128)(2,1)}, u32[]{:S(2)}) copy-start(bf16[64,896]{1,0:T(8,128)(2,1)} %dy.1) | copy-start | bytes 344068
  6.9 15.9 %copy-start.12 = (bf16[640,64]{1,0:T(8,128)(2,1)}, bf16[640,64]{1,0:T(8,128)(2,1)S(1)}, u32[]{:S(2)}) copy-start(bf16[640,64]{1,0:T(8,128)(2,1)S(1)} %get-tuple-element.30.onehot) | copy-start | bytes 245764
  6.9 28.6 %all-to-all-start = ((bf16[16,40,896]{2,1,0:T(8,128)(2,1)}), bf16[16,40,896]{2,1,0:T(8,128)(2,1)S(1)}, u32[]{:S(2)}, u32[]{:S(2)}) async-start(bf16[16,40,896]{2,1,0:T(8,128)(2,1)} %bitcast.7), calls=%async_computation | async-start | bytes 2293760 | tf_op jit(solution)/shard_map/all_to_all | solution.py:485
  14.8 20.7 %collective-permute-start.2 = (bf16[7168,256]{1,0:T(8,128)(2,1)}, bf16[7168,256]{1,0:T(8,128)(2,1)}, u32[]{:S(2)}, u32[]{:S(2)}) collective-permute-start(bf16[7168,256]{1,0:T(8,128)(2,1)} %bitcast.31), channel_id=1, source_target_pairs={{0,1},{1,0},{2,3},{3,2},{4,5},{5,4},{6,7},{7,6},{8,9},{9,8},{10,11... | collective-permute-start | bytes 11010056 | tf_op jit(solution)/shard_map/ppermute | solution.py:39
  15.6 20.0 %collective-permute-start.3 = (bf16[7168,256]{1,0:T(8,128)(2,1)}, bf16[7168,256]{1,0:T(8,128)(2,1)}, u32[]{:S(2)}, u32[]{:S(2)}) collective-permute-start(bf16[7168,256]{1,0:T(8,128)(2,1)} %bitcast.33), channel_id=1, source_target_pairs={{0,1},{1,0},{2,3},{3,2},{4,5},{5,4},{6,7},{7,6},{8,9},{9,8},{10,11... | collective-permute-start | bytes 11010056 | tf_op jit(solution)/shard_map/ppermute | solution.py:39
  15.7 19.9 %collective-permute-start.4 = (bf16[256,7168]{1,0:T(8,128)(2,1)}, bf16[256,7168]{1,0:T(8,128)(2,1)}, u32[]{:S(2)}, u32[]{:S(2)}) collective-permute-start(bf16[256,7168]{1,0:T(8,128)(2,1)} %bitcast.35), channel_id=1, source_target_pairs={{0,1},{1,0},{2,3},{3,2},{4,5},{5,4},{6,7},{7,6},{8,9},{9,8},{10,11... | collective-permute-start | bytes 11010056 | tf_op jit(solution)/shard_map/ppermute | solution.py:39
  16.2 5.9 %collective-permute-start.1 = (bf16[128,384]{1,0:T(8,128)(2,1)S(1)}, bf16[128,384]{1,0:T(8,128)(2,1)S(1)}, u32[]{:S(2)}, u32[]{:S(2)}) collective-permute-start(bf16[128,384]{1,0:T(8,128)(2,1)S(1)} %pad_maximum_fusion.refs_0_), channel_id=1, source_target_pairs={{0,6},{1,3},{2,4},{3,1},{4,2},{5,7},{6,0},{7,5},{8,14},{9,11},{10,... | collective-permute-start | bytes 294920 | tf_op jit(solution)/shard_map/ppermute | solution.py:35
  36.6 26.9 %collective-permute-start.8 = (bf16[640,896]{1,0:T(8,128)(2,1)}, bf16[640,896]{1,0:T(8,128)(2,1)}, u32[]{:S(2)}, u32[]{:S(2)}) collective-permute-start(bf16[640,896]{1,0:T(8,128)(2,1)} %shard_map.112.refs_1_.refs_0_), channel_id=1, source_target_pairs={{0,2},{1,7},{2,0},{3,5},{4,6},{5,3},{6,4},{7,1},{8,10},{9,15},{10,... | collective-permute-start | bytes 3440648 | tf_op jit(solution)/shard_map/ppermute | solution.py:35
  36.6 50.1 %collective-permute-start.10 = (bf16[640,896]{1,0:T(8,128)(2,1)}, bf16[640,896]{1,0:T(8,128)(2,1)}, u32[]{:S(2)}, u32[]{:S(2)}) collective-permute-start(bf16[640,896]{1,0:T(8,128)(2,1)} %shard_map.112.refs_1_.refs_0_), channel_id=1, source_target_pairs={{0,6},{1,3},{2,4},{3,1},{4,2},{5,7},{6,0},{7,5},{8,14},{9,11},{10,... | collective-permute-start | bytes 3440648 | tf_op jit(solution)/shard_map/ppermute | solution.py:35
  36.6 43.7 %all-to-all-start.1 = ((bf16[16,40,2176]{2,1,0:T(8,128)(2,1)}), bf16[16,40,2176]{2,1,0:T(8,128)(2,1)}, u32[]{:S(2)}, u32[]{:S(2)}) async-start(bf16[16,40,2176]{2,1,0:T(8,128)(2,1)} %bitcast.26), calls=%async_computation.1 | async-start | bytes 5570560 | tf_op jit(solution)/shard_map/all_to_all | solution.py:485
  63.5 36.1 %collective-permute-start.9 = (bf16[640,896]{1,0:T(8,128)(2,1)}, bf16[640,896]{1,0:T(8,128)(2,1)}, u32[]{:S(2)}, u32[]{:S(2)}) collective-permute-start(bf16[640,896]{1,0:T(8,128)(2,1)} %collective-permute-done.8.refs_1_), channel_id=1, source_target_pairs={{0,6},{1,3},{2,4},{3,1},{4,2},{5,7},{6,0},{7,5},{8,14},{9,11},{10,... | collective-permute-start | bytes 3440648 | tf_op jit(solution)/shard_map/ppermute | solution.py:35
  82.3 15.9 %collective-permute-start.5 = (bf16[640,512]{1,0:T(8,128)(2,1)}, bf16[640,512]{1,0:T(8,128)(2,1)}, u32[]{:S(2)}, u32[]{:S(2)}) collective-permute-start(bf16[640,512]{1,0:T(8,128)(2,1)} %slice.20.d0.refs_4_), channel_id=1, source_target_pairs={{0,2},{1,7},{2,0},{3,5},{4,6},{5,3},{6,4},{7,1},{8,10},{9,15},{10,... | collective-permute-start | bytes 1966088 | tf_op jit(solution)/shard_map/ppermute | solution.py:35
  83.4 14.8 %collective-permute-start.6 = (bf16[640,512]{1,0:T(8,128)(2,1)}, bf16[640,512]{1,0:T(8,128)(2,1)}, u32[]{:S(2)}, u32[]{:S(2)}) collective-permute-start(bf16[640,512]{1,0:T(8,128)(2,1)} %slice.20.d0.refs_4_), channel_id=1, source_target_pairs={{0,6},{1,3},{2,4},{3,1},{4,2},{5,7},{6,0},{7,5},{8,14},{9,11},{10,... | collective-permute-start | bytes 1966088 | tf_op jit(solution)/shard_map/ppermute | solution.py:35
  98.2 12.1 %collective-permute-start.7 = (bf16[640,512]{1,0:T(8,128)(2,1)}, bf16[640,512]{1,0:T(8,128)(2,1)}, u32[]{:S(2)}, u32[]{:S(2)}) collective-permute-start(bf16[640,512]{1,0:T(8,128)(2,1)} %shard_map.114.d1.refs_5_), channel_id=1, source_target_pairs={{0,6},{1,3},{2,4},{3,1},{4,2},{5,7},{6,0},{7,5},{8,14},{9,11},{10,... | collective-permute-start | bytes 1966088 | tf_op jit(solution)/shard_map/ppermute | solution.py:35
  108.7 6.7 %collective-permute-start.12 = (f32[640,512]{1,0:T(8,128)}, f32[640,512]{1,0:T(8,128)S(1)}, u32[]{:S(2)}, u32[]{:S(2)}) collective-permute-start(f32[640,512]{1,0:T(8,128)} %get-tuple-element.39), channel_id=1, source_target_pairs={{0,1},{1,0},{2,3},{3,2},{4,5},{5,4},{6,7},{7,6},{8,9},{9,8},{10,11... | collective-permute-start | bytes 3932168 | tf_op jit(solution)/shard_map/ppermute | solution.py:39
  115.2 2.4 %collective-permute-start.11 = (f32[640,256]{1,0:T(8,128)}, f32[640,256]{1,0:T(8,128)S(1)}, u32[]{:S(2)}, u32[]{:S(2)}) collective-permute-start(f32[640,256]{1,0:T(8,128)} %get-tuple-element.37), channel_id=1, source_target_pairs={{0,1},{1,0},{2,3},{3,2},{4,5},{5,4},{6,7},{7,6},{8,9},{9,8},{10,11... | collective-permute-start | bytes 1966088 | tf_op jit(solution)/shard_map/ppermute | solution.py:39
  118.8 42.3 %copy-start.6 = (bf16[656,512]{1,0:T(8,128)(2,1)}, bf16[656,512]{1,0:T(8,128)(2,1)S(1)}, u32[]{:S(2)}) copy-start(bf16[656,512]{1,0:T(8,128)(2,1)S(1)} %get-tuple-element.43.own.refs_9_) | copy-start | bytes 2015236
  118.8 2.1 %collective-permute-start.13 = (bf16[656,512]{1,0:T(8,128)(2,1)S(1)}, bf16[656,512]{1,0:T(8,128)(2,1)S(1)}, u32[]{:S(2)}, u32[]{:S(2)}) collective-permute-start(bf16[656,512]{1,0:T(8,128)(2,1)S(1)} %get-tuple-element.43.own.refs_9_), channel_id=1, source_target_pairs={{0,1},{1,0},{2,3},{3,2},{4,5},{5,4},{6,7},{7,6},{8,9},{9,8},{10,11... | collective-permute-start | bytes 2015240 | tf_op jit(solution)/shard_map/ppermute | solution.py:39
  118.9 31.5 %collective-permute-start.19 = (bf16[640,256]{1,0:T(8,128)(2,1)}, bf16[640,256]{1,0:T(8,128)(2,1)}, u32[]{:S(2)}, u32[]{:S(2)}) collective-permute-start(bf16[640,256]{1,0:T(8,128)(2,1)} %get-tuple-element.46.refs_10_), channel_id=1, source_target_pairs={{0,1},{1,0},{2,3},{3,2},{4,5},{5,4},{6,7},{7,6},{8,9},{9,8},{10,11... | collective-permute-start | bytes 983048 | tf_op jit(solution)/shard_map/ppermute | solution.py:39
  120.9 24.1 %copy-start.7 = (bf16[656,512]{1,0:T(8,128)(2,1)}, bf16[656,512]{1,0:T(8,128)(2,1)S(1)}, u32[]{:S(2)}) copy-start(bf16[656,512]{1,0:T(8,128)(2,1)S(1)} %collective-permute-done.13.other.refs_9_) | copy-start | bytes 2015236
  124.9 23.2 %collective-permute-start.14 = (bf16[656,640]{1,0:T(8,128)(2,1)}, bf16[656,640]{1,0:T(8,128)(2,1)}, u32[]{:S(2)}, u32[]{:S(2)}) collective-permute-start(bf16[656,640]{1,0:T(8,128)(2,1)} %shard_map.121.refs_1_), channel_id=1, source_target_pairs={{0,6},{1,3},{2,4},{3,1},{4,2},{5,7},{6,0},{7,5},{8,14},{9,11},{10,... | collective-permute-start | bytes 2519048 | tf_op jit(solution)/shard_map/ppermute | solution.py:35
  130.6 33.6 %collective-permute-start.15 = (bf16[656,640]{1,0:T(8,128)(2,1)}, bf16[656,640]{1,0:T(8,128)(2,1)}, u32[]{:S(2)}, u32[]{:S(2)}) collective-permute-start(bf16[656,640]{1,0:T(8,128)(2,1)} %shard_map.122.refs_1_._), channel_id=1, source_target_pairs={{0,6},{1,3},{2,4},{3,1},{4,2},{5,7},{6,0},{7,5},{8,14},{9,11},{10,... | collective-permute-start | bytes 2519048 | tf_op jit(solution)/shard_map/ppermute | solution.py:35
  138.6 28.6 %all-to-all-start.3 = ((bf16[16,40,1024]{2,1,0:T(8,128)(2,1)}), bf16[16,40,1024]{2,1,0:T(8,128)(2,1)}, u32[]{:S(2)}, u32[]{:S(2)}) async-start(bf16[16,40,1024]{2,1,0:T(8,128)(2,1)} %bitcast.30), calls=%async_computation.3 | async-start | bytes 2621440 | tf_op jit(solution)/shard_map/all_to_all | solution.py:485
  150.4 13.8 %collective-permute-start.16 = (bf16[656,640]{1,0:T(8,128)(2,1)}, bf16[656,640]{1,0:T(8,128)(2,1)}, u32[]{:S(2)}, u32[]{:S(2)}) collective-permute-start(bf16[656,640]{1,0:T(8,128)(2,1)} %add_convert_fusion.refs_1_.refs_11_), channel_id=1, source_target_pairs={{0,2},{1,7},{2,0},{3,5},{4,6},{5,3},{6,4},{7,1},{8,10},{9,15},{10,... | collective-permute-start | bytes 2519048 | tf_op jit(solution)/shard_map/ppermute | solution.py:35
  150.4 10.7 %copy-start.5 = (s32[4]{0:T(128)S(1)}, s32[4]{0:T(128)}, u32[]{:S(2)}) copy-start(s32[4]{0:T(128)} %pad_add_fusion.place) | copy-start | bytes 52
  150.4 10.7 %copy-start.8 = (bf16[656,512]{1,0:T(8,128)(2,1)S(1)}, bf16[656,512]{1,0:T(8,128)(2,1)}, u32[]{:S(2)}) copy-start(bf16[656,512]{1,0:T(8,128)(2,1)} %copy-done.7) | copy-start | bytes 2015236
  160.4 20.3 %collective-permute-start.20 = (bf16[4,896,512]{2,1,0:T(8,128)(2,1)}, bf16[4,896,512]{2,1,0:T(8,128)(2,1)}, u32[]{:S(2)}, u32[]{:S(2)}) collective-permute-start(bf16[4,896,512]{2,1,0:T(8,128)(2,1)} %get-tuple-element.47), channel_id=1, source_target_pairs={{0,1},{1,0},{2,3},{3,2},{4,5},{5,4},{6,7},{7,6},{8,9},{9,8},{10,11... | collective-permute-start | bytes 11010056 | tf_op jit(solution)/shard_map/ppermute | solution.py:39
  160.7 20.0 %collective-permute-start.21 = (bf16[4,256,896]{2,1,0:T(8,128)(2,1)}, bf16[4,256,896]{2,1,0:T(8,128)(2,1)}, u32[]{:S(2)}, u32[]{:S(2)}) collective-permute-start(bf16[4,256,896]{2,1,0:T(8,128)(2,1)} %get-tuple-element.48), channel_id=1, source_target_pairs={{0,1},{1,0},{2,3},{3,2},{4,5},{5,4},{6,7},{7,6},{8,9},{9,8},{10,11... | collective-permute-start | bytes 5505032 | tf_op jit(solution)/shard_map/ppermute | solution.py:39
  168.9 10.3 %collective-permute-start.17 = (f32[128,256]{1,0:T(8,128)S(1)}, f32[128,256]{1,0:T(8,128)S(1)}, u32[]{:S(2)}, u32[]{:S(2)}) collective-permute-start(f32[128,256]{1,0:T(8,128)S(1)} %get-tuple-element.45), channel_id=1, source_target_pairs={{0,6},{1,3},{2,4},{3,1},{4,2},{5,7},{6,0},{7,5},{8,14},{9,11},{10,... | collective-permute-start | bytes 393224 | tf_op jit(solution)/shard_map/ppermute | solution.py:35
  172.0 23.5 %all-to-all-start.2 = ((bf16[16,40,768]{2,1,0:T(8,128)(2,1)}), bf16[16,40,768]{2,1,0:T(8,128)(2,1)S(1)}, u32[]{:S(2)}, u32[]{:S(2)}) async-start(bf16[16,40,768]{2,1,0:T(8,128)(2,1)} %bitcast.14), calls=%async_computation.2 | async-start | bytes 1966080 | tf_op jit(solution)/shard_map/all_to_all | solution.py:485
  179.2 13.8 %collective-permute-start.18 = (f32[64,256]{1,0:T(8,128)S(1)}, f32[64,256]{1,0:T(8,128)S(1)}, u32[]{:S(2)}, u32[]{:S(2)}) collective-permute-start(f32[64,256]{1,0:T(8,128)S(1)} %get-tuple-element.60), channel_id=1, source_target_pairs={{0,2},{1,7},{2,0},{3,5},{4,6},{5,3},{6,4},{7,1},{8,10},{9,15},{10,... | collective-permute-start | bytes 196616 | tf_op jit(solution)/shard_map/ppermute | solution.py:35
  (10 other events, 22.5 us)
